TPU v7x, 32 devices: a whole 2x2x4 slice. The times are simulated.
32 devices in a mesh: row: 4 (over x, core), col: 8 (over z, y).
Axes of the slice: x: 2, y: 2, z: 4, core: 2. Of those that a mesh axis runs over, the one named last changes fastest.
Arguments:
- features: bfloat16 [4096, 256], P(('row', 'col')), may hold values from -6 to 6
- weight: bfloat16 [256, 256], replicated, may hold values from -0.375 to 0.375
- bias_vector: float32 [256], replicated, may hold values from -3 to 3
- out_grad: bfloat16 [4096, 256], P(('row', 'col')), may hold values from -6 to 6
- adj_tiles: bfloat16 [4, 8, 96, 128, 128], P('row', 'col'), as said below
- tile_pos: int32 [4, 8, 96], P('row', 'col'), may hold values from 0 to 31
- tile_count: int32 [4, 8], P('row', 'col'), may hold values from 24 to 96, as said below
Outputs:
- hidden_out: bfloat16 [4096, 256], P(('row', 'col'))
- feature_grad: bfloat16 [4096, 256], P(('row', 'col'))
- weight_grad: float32 [256, 256], replicated
- bias_grad: float32 [256], replicated
Inputs may be any that keep to these rules, and one draw needn't show every extreme that they name: `tile_pos`: several slots of one grid position may name the same tile position; their tiles add. Only the first tile_count slots of a grid position are live. In every draw some grid position has exactly 96 live slots and some other one the least number. `adj_tiles`: entries are nonnegative edge weights.
All inputs are finite; a program needn't handle non-finite values.
Results may differ from a plain program's by a relative error of at most 0.018.
Values may be sent and summed in bfloat16 or wider, within the bound.
No kernel may reach another device: no remote copies, remote signals or barrier semaphores. Data moves between devices by JAX's collectives and lax.ppermute only.
A program may use at most 64 MiB of HBM per device.

v0:
```python
import math

import jax
import jax.numpy as jnp
from jax import lax
from jax.sharding import PartitionSpec as P

TILE_BLOCK = 32


def shifted(block, axis, distance):
    devices = range(lax.axis_size(axis))
    route = [((i - distance) % len(devices), i) for i in devices]
    return lax.ppermute(block, axis, route)


def body(features, weight, bias_vector, out_grad, adj_tiles, tile_pos, tile_count):
    rows_dev = features.shape[0]
    feat_width = features.shape[1]
    tile_size = adj_tiles.shape[-1]
    row_count = lax.axis_size("row")
    col_count = lax.axis_size("col")
    row_tiles = col_count * rows_dev // tile_size
    col_tiles = row_count * rows_dev // tile_size
    tile_set = adj_tiles[0, 0]
    positions = tile_pos[0, 0]
    live_count = tile_count[0, 0]
    tile_rows = positions // col_tiles
    tile_cols = positions % col_tiles
    blocks_used = (live_count + TILE_BLOCK - 1) // TILE_BLOCK
    block_slots = jnp.arange(TILE_BLOCK, dtype=jnp.int32)
    gathered = lax.all_gather(features, "row", axis=0, tiled=True)
    col_blocks = gathered.reshape(col_tiles, tile_size, feat_width)

    def forward_block(block_index, partial_value):
        first_slot = block_index * TILE_BLOCK
        tile_group = lax.dynamic_slice_in_dim(tile_set, first_slot, TILE_BLOCK, 0)
        group_cols = lax.dynamic_slice_in_dim(tile_cols, first_slot, TILE_BLOCK, 0)
        group_rows = lax.dynamic_slice_in_dim(tile_rows, first_slot, TILE_BLOCK, 0)
        live = first_slot + block_slots < live_count
        picked = col_blocks[group_cols]
        product = jnp.einsum("tij,tjf->tif", tile_group, picked, preferred_element_type=jnp.float32)
        product = jnp.where(live[:, None, None], product, jnp.float32(0.0))
        return partial_value + jax.ops.segment_sum(product, group_rows, num_segments=row_tiles)

    partial_value = lax.fori_loop(
        0, blocks_used, forward_block, jnp.zeros((row_tiles, tile_size, feat_width), jnp.float32)
    )
    partial_value = partial_value.reshape(col_count * rows_dev, feat_width)
    summed = lax.psum_scatter(
        partial_value.astype(jnp.bfloat16), "col", scatter_dimension=0, tiled=True
    )
    pre = jnp.dot(summed, weight, preferred_element_type=jnp.float32) + bias_vector
    gate_value = jax.nn.sigmoid(pre)
    hidden_out = (pre * gate_value).astype(jnp.bfloat16)
    pre_grad = (
        out_grad.astype(jnp.float32) * (gate_value * (1.0 + pre * (1.0 - gate_value)))
    ).astype(jnp.bfloat16)
    local_weight = jnp.einsum("nf,ng->fg", summed, pre_grad, preferred_element_type=jnp.float32)
    local_bias = jnp.sum(pre_grad.astype(jnp.float32), axis=0)
    total_weight, total_bias = lax.psum((local_weight, local_bias), ("row", "col"))
    grad_scale = 1.0 / math.sqrt(row_count * col_count * rows_dev)
    weight_grad = total_weight * grad_scale
    bias_grad = total_bias * grad_scale
    agg_grad = jnp.einsum("ng,fg->nf", pre_grad, weight, preferred_element_type=jnp.float32).astype(
        jnp.bfloat16
    )
    panel = lax.all_gather(agg_grad, "col", axis=0, tiled=True)
    panel_blocks = panel.reshape(row_tiles, tile_size, feat_width)

    def backward_block(block_index, column_terms):
        first_slot = block_index * TILE_BLOCK
        tile_group = lax.dynamic_slice_in_dim(tile_set, first_slot, TILE_BLOCK, 0)
        group_cols = lax.dynamic_slice_in_dim(tile_cols, first_slot, TILE_BLOCK, 0)
        group_rows = lax.dynamic_slice_in_dim(tile_rows, first_slot, TILE_BLOCK, 0)
        live = first_slot + block_slots < live_count
        picked = panel_blocks[group_rows]
        product = jnp.einsum("tji,tjf->tif", tile_group, picked, preferred_element_type=jnp.float32)
        product = jnp.where(live[:, None, None], product, jnp.float32(0.0))
        return column_terms + jax.ops.segment_sum(product, group_cols, num_segments=col_tiles)

    column_terms = lax.fori_loop(
        0, blocks_used, backward_block, jnp.zeros((col_tiles, tile_size, feat_width), jnp.float32)
    )
    own_index = lax.axis_index("row")

    def pick_terms(section_index):
        target = (own_index - section_index - 1) % row_count
        return lax.dynamic_index_in_dim(column_terms, target, 0, keepdims=False)

    def relay_section(section_index, running):
        running = running + pick_terms(section_index)
        return shifted(running.astype(jnp.bfloat16), "row", 1).astype(running.dtype)

    running = lax.fori_loop(
        0, row_count - 1, relay_section, jnp.zeros((rows_dev, feat_width), jnp.float32)
    )
    grad_total = running + pick_terms(row_count - 1)
    feature_grad = grad_total.astype(jnp.bfloat16)
    return (hidden_out, feature_grad, weight_grad, bias_grad)


def solution(mesh):
    in_specs = (
        P(("row", "col"), None),
        P(),
        P(),
        P(("row", "col"), None),
        P("row", "col", None, None, None),
        P("row", "col", None),
        P("row", "col"),
    )
    out_specs = (P(("row", "col"), None), P(("row", "col"), None), P(), P())
    return jax.shard_map(body, mesh=mesh, in_specs=in_specs, out_specs=out_specs, check_vma=False)
```

profile of v0, /device:TPU:0, one launch (start us, length us, event | category | flops | bytes accessed | tf_op | source)
XLA Modules:
  0.0 318.0 jit_solution(7326660376137438955)
XLA Ops:
  8.6 7.4 %all_gather.6 = bf16[512,256]{1,0:T(8,128)(2,1)S(1)} all-gather(bf16[128,256]{1,0:T(8,128)(2,1)} %param.13), channel_id=1, replica_groups=mesh['row'=4,'col'=8] {'row'}, dimensions={0}, use_global_device_ids=true | all-gather | bytes 327680 | tf_op jit(solution)/shard_map/all_gather | solution.py:32
  16.1 23.7 %while.38 = (s32[]{:T(128)}, f32[8,128,256]{2,1,0:T(8,128)S(1)}, s32[]{:T(128)}, s32[96]{0:T(128)S(1)}, s32[]{:T(128)}, /*index=5*/bf16[96,128,128]{2,1,0:T(8,12...) while((s32[]{:T(128)}, f32[8,128,256]{2,1,0:T(8,128)S(1)}, ...), condition=%wide.region_2.3_spmd.clone, body=%wide.region_0.2_spmd.clone.sunk | while | flops 270533792 | bytes 24122488 | solution.py:46
  17.5 3.9 %convolution_select_fusion.4 = f32[32,128,256]{2,1,0:T(8,128)} fusion(bf16[32,128,256]{2,1,0:T(8,128)(2,1)S(1)} %gather_fusion, pred[32]{0:T(512)(128)(4,1)S(1)} %fusion.30, bf16[96,128,128]{2,1,0:T(8,128)(2,1)} %get-tuple-element.475, s32[]{:T(128)S(6)} %select_n.105), kind=kOutput, calls=%fused_computation.6.clone.1 | convolution fusion | flops 269484032 | bytes 7340068 | tf_op jit(solution)/shard_map/while/body/tij,tjf->tif/dot_general | solution.py:42
  21.5 6.4 %scatter_fusion = f32[8,128,256]{2,1,0:T(8,128)S(1)} fusion(f32[8,128,256]{2,1,0:T(8,128)S(1)} %get-tuple-element.459, s32[32]{0:T(128)S(1)} %dynamic_slice.57, f32[32,128,256]{2,1,0:T(8,128)} %convolution_select_fusion.4), kind=kCustom, calls=%fused_computation.2.clone.clone.1 | custom fusion | flops 1048576 | bytes 12583040 | tf_op jit(solution)/shard_map/while/body/scatter-add | solution.py:44
  29.4 3.9 %convolution_select_fusion.4 = f32[32,128,256]{2,1,0:T(8,128)} fusion(bf16[32,128,256]{2,1,0:T(8,128)(2,1)S(1)} %gather_fusion, pred[32]{0:T(512)(128)(4,1)S(1)} %fusion.30, bf16[96,128,128]{2,1,0:T(8,128)(2,1)} %get-tuple-element.475, s32[]{:T(128)S(6)} %select_n.105), kind=kOutput, calls=%fused_computation.6.clone.1 | convolution fusion | flops 269484032 | bytes 7340068 | tf_op jit(solution)/shard_map/while/body/tij,tjf->tif/dot_general | solution.py:42
  33.3 6.4 %scatter_fusion = f32[8,128,256]{2,1,0:T(8,128)S(1)} fusion(f32[8,128,256]{2,1,0:T(8,128)S(1)} %get-tuple-element.459, s32[32]{0:T(128)S(1)} %dynamic_slice.57, f32[32,128,256]{2,1,0:T(8,128)} %convolution_select_fusion.4), kind=kCustom, calls=%fused_computation.2.clone.clone.1 | custom fusion | flops 1048576 | bytes 12583040 | tf_op jit(solution)/shard_map/while/body/scatter-add | solution.py:44
  39.8 0.8 convert_element_type.44
  40.7 4.7 %copy.11 = bf16[1,1,96,128,128]{3,4,2,1,0:T(8,128)(2,1)} copy(bf16[1,1,96,128,128]{4,3,2,1,0:T(8,128)(2,1)} %bitcast.47) | data formatting | bytes 6291456 | tf_op args[4]
  45.4 70.9 %reduce-scatter.2.cloned.1.call-done = bf16[128,256]{1,0:T(8,128)(2,1)} async-done(((bf16[1024,256]{1,0:T(8,128)(2,1)}), bf16[128,256]{1,0:T(8,128)(2,1)}) %reduce-scatter.2.cloned.1.call-update) | async-done | bytes 65552 | tf_op jit(solution)/shard_map/reduce_scatter | solution.py:50
  116.2 1.7 convert_reduce_fusion
  118.1 31.3 %all_gather.7 = bf16[1024,256]{1,0:T(8,128)(2,1)S(1)} all-gather(bf16[128,256]{1,0:T(8,128)(2,1)S(1)} %convolution_convert_fusion), channel_id=1, replica_groups=mesh['row'=4,'col'=8] {'col'}, dimensions={0}, use_global_device_ids=true | all-gather | bytes 589824 | tf_op jit(solution)/shard_map/all_gather | solution.py:68
  149.5 23.6 %while.39 = (s32[]{:T(128)}, f32[4,128,256]{2,1,0:T(8,128)S(1)}, s32[]{:T(128)}, s32[96]{0:T(128)S(1)}, s32[]{:T(128)}, /*index=5*/bf16[96,128,128]{1,2,0:T(8,12...) while((s32[]{:T(128)}, f32[4,128,256]{2,1,0:T(8,128)S(1)}, ...), condition=%wide.region_6.7_spmd.clone, body=%wide.region_4.6_spmd.clone.sunk | while | flops 270533792 | bytes 24122488 | solution.py:82
  151.0 3.8 %convolution_select_fusion.5 = f32[32,128,256]{2,1,0:T(8,128)} fusion(bf16[32,128,256]{2,1,0:T(8,128)(2,1)S(1)} %gather_fusion.1, pred[32]{0:T(512)(128)(4,1)S(1)} %fusion.33, bf16[96,128,128]{1,2,0:T(8,128)(2,1)} %get-tuple-element.511, s32[]{:T(128)S(6)} %select_n.108), kind=kOutput, calls=%fused_computation.13.clone.1 | convolution fusion | flops 269484032 | bytes 7340068 | tf_op jit(solution)/shard_map/while/body/tji,tjf->tif/dot_general | solution.py:78
  154.9 6.4 %scatter_fusion.1 = f32[4,128,256]{2,1,0:T(8,128)S(1)} fusion(f32[4,128,256]{2,1,0:T(8,128)S(1)} %get-tuple-element.495, s32[32]{0:T(128)S(1)} %dynamic_slice.60, f32[32,128,256]{2,1,0:T(8,128)} %convolution_select_fusion.5), kind=kCustom, calls=%fused_computation.3.clone.clone.1 | custom fusion | flops 1048576 | bytes 12583040 | tf_op jit(solution)/shard_map/while/body/scatter-add | solution.py:80
  162.8 3.8 %convolution_select_fusion.5 = f32[32,128,256]{2,1,0:T(8,128)} fusion(bf16[32,128,256]{2,1,0:T(8,128)(2,1)S(1)} %gather_fusion.1, pred[32]{0:T(512)(128)(4,1)S(1)} %fusion.33, bf16[96,128,128]{1,2,0:T(8,128)(2,1)} %get-tuple-element.511, s32[]{:T(128)S(6)} %select_n.108), kind=kOutput, calls=%fused_computation.13.clone.1 | convolution fusion | flops 269484032 | bytes 7340068 | tf_op jit(solution)/shard_map/while/body/tji,tjf->tif/dot_general | solution.py:78
  166.7 6.4 %scatter_fusion.1 = f32[4,128,256]{2,1,0:T(8,128)S(1)} fusion(f32[4,128,256]{2,1,0:T(8,128)S(1)} %get-tuple-element.495, s32[32]{0:T(128)S(1)} %dynamic_slice.60, f32[32,128,256]{2,1,0:T(8,128)} %convolution_select_fusion.5), kind=kCustom, calls=%fused_computation.3.clone.clone.1 | custom fusion | flops 1048576 | bytes 12583040 | tf_op jit(solution)/shard_map/while/body/scatter-add | solution.py:80
  173.2 0.9 fusion.12
  174.1 48.4 %psum.15 = f32[256]{0:T(256)S(1)} all-reduce(f32[256]{0:T(256)S(1)} %get-tuple-element.316), channel_id=1, replica_groups=mesh['row'=4,'col'=8] {'row','col'}, use_global_device_ids=true, to_apply=%region_11.12 | all-reduce | flops 256 | bytes 2048 | tf_op jit(solution)/shard_map/psum | solution.py:61
  222.5 11.4 %while.40 = (s32[]{:T(128)}, f32[128,256]{1,0:T(8,128)S(1)}, s32[]{:T(128)}, f32[4,128,256]{2,1,0:T(8,128)S(1)}, s32[]{:T(128)}, /*index=5*/s32[]{:T(128)}, s32[]{:T(128)}, s32[]{:T(128)}, s32[]{:T(128)}) while((s32[]{:T(128)}, f32[128,256]{1,0:T(8,128)S(1)}, s32[]{:T(128)}, f32[4,128,256]{2,1,0:T(8,128)S(1)}, s32[]{:T(128)}, ...), condition=%wide.region_8.9_spmd.clone, body=%wide.region_7.8_spmd.clone.sunk | while | flops 131091 | bytes 786746 | solution.py:95
  222.5 3.7 %collective-permute-done = bf16[128,256]{1,0:T(8,128)(2,1)S(1)} collective-permute-done((bf16[128,256]{1,0:T(8,128)(2,1)S(1)}, bf16[128,256]{1,0:T(8,128)(2,1)S(1)}, u32[]{:S(2)}, u32[]{:S(2)}) %collective-permute-start) | collective-permute-done | bytes 65568 | tf_op jit(solution)/shard_map/while/body/eval_jaxpr/ppermute | solution.py:14
  226.4 3.7 %collective-permute-done = bf16[128,256]{1,0:T(8,128)(2,1)S(1)} collective-permute-done((bf16[128,256]{1,0:T(8,128)(2,1)S(1)}, bf16[128,256]{1,0:T(8,128)(2,1)S(1)}, u32[]{:S(2)}, u32[]{:S(2)}) %collective-permute-start) | collective-permute-done | bytes 65568 | tf_op jit(solution)/shard_map/while/body/eval_jaxpr/ppermute | solution.py:14
  230.2 3.7 %collective-permute-done = bf16[128,256]{1,0:T(8,128)(2,1)S(1)} collective-permute-done((bf16[128,256]{1,0:T(8,128)(2,1)S(1)}, bf16[128,256]{1,0:T(8,128)(2,1)S(1)}, u32[]{:S(2)}, u32[]{:S(2)}) %collective-permute-start) | collective-permute-done | bytes 65568 | tf_op jit(solution)/shard_map/while/body/eval_jaxpr/ppermute | solution.py:14
  235.1 74.4 %all-reduce.2.cloned.1.call-done = f32[256,256]{1,0:T(8,128)} async-done(((f32[256,256]{1,0:T(8,128)}), f32[256,256]{1,0:T(8,128)}) %all-reduce.2.cloned.1.call-update) | async-done | bytes 262160 | tf_op jit(solution)/shard_map/psum | solution.py:61
  309.5 1.7 broadcast_multiply_fusion
  (48 shorter events, 8.6 us)
Async XLA Ops:
  7.2 109.1 %copy-start = (bf16[256,256]{1,0:T(8,128)(2,1)S(1)}, bf16[256,256]{1,0:T(8,128)(2,1)}, u32[]{:S(2)}) copy-start(bf16[256,256]{1,0:T(8,128)(2,1)} %param.14) | copy-start | bytes 393220
  7.2 109.0 %reduce-scatter.2.cloned.1.call-start = ((), (), s32[]{:S(2)}) async-start(), calls=%async_computation.1 | async-start | bytes 589824 | tf_op jit(solution)/shard_map/reduce_scatter | solution.py:50
  40.6 75.6 %copy-start.2 = (bf16[128,256]{1,0:T(8,128)(2,1)S(1)}, bf16[128,256]{1,0:T(8,128)(2,1)}, u32[]{:S(2)}) copy-start(bf16[128,256]{1,0:T(8,128)(2,1)} %param.16) | copy-start | bytes 196612
  40.6 75.6 %copy-start.3 = (f32[256]{0:T(256)S(1)}, f32[256]{0:T(256)}, u32[]{:S(2)}) copy-start(f32[256]{0:T(256)} %param.15) | copy-start | bytes 3076
  40.7 268.9 %all-reduce.2.cloned.1.call-start = ((), (), s32[]{:S(2)}) async-start(), calls=%async_computation.2 | async-start | bytes 524288 | tf_op jit(solution)/shard_map/psum | solution.py:61
  149.5 23.7 %copy-start.1 = (bf16[128,256]{1,0:T(8,128)(2,1)S(1)}, bf16[128,256]{1,0:T(8,128)(2,1)}, u32[]{:S(2)}) copy-start(bf16[128,256]{1,0:T(8,128)(2,1)} %reduce-scatter.2.cloned.1.call-done) | copy-start | bytes 196612
  222.5 3.7 %collective-permute-start = (bf16[128,256]{1,0:T(8,128)(2,1)S(1)}, bf16[128,256]{1,0:T(8,128)(2,1)S(1)}, u32[]{:S(2)}, u32[]{:S(2)}) collective-permute-start(bf16[128,256]{1,0:T(8,128)(2,1)S(1)} %fusion.34), channel_id=1, source_target_pairs={{24,0},{0,8},{8,16},{16,24},{25,1},{1,9},{9,17},{17,25},{26,2},{2,... | collective-permute-start | bytes 196616 | tf_op jit(solution)/shard_map/while/body/eval_jaxpr/ppermute | solution.py:14
  226.3 3.7 %collective-permute-start = (bf16[128,256]{1,0:T(8,128)(2,1)S(1)}, bf16[128,256]{1,0:T(8,128)(2,1)S(1)}, u32[]{:S(2)}, u32[]{:S(2)}) collective-permute-start(bf16[128,256]{1,0:T(8,128)(2,1)S(1)} %fusion.34), channel_id=1, source_target_pairs={{24,0},{0,8},{8,16},{16,24},{25,1},{1,9},{9,17},{17,25},{26,2},{2,... | collective-permute-start | bytes 196616 | tf_op jit(solution)/shard_map/while/body/eval_jaxpr/ppermute | solution.py:14
  230.1 3.7 %collective-permute-start = (bf16[128,256]{1,0:T(8,128)(2,1)S(1)}, bf16[128,256]{1,0:T(8,128)(2,1)S(1)}, u32[]{:S(2)}, u32[]{:S(2)}) collective-permute-start(bf16[128,256]{1,0:T(8,128)(2,1)S(1)} %fusion.34), channel_id=1, source_target_pairs={{24,0},{0,8},{8,16},{16,24},{25,1},{1,9},{9,17},{17,25},{26,2},{2,... | collective-permute-start | bytes 196616 | tf_op jit(solution)/shard_map/while/body/eval_jaxpr/ppermute | solution.py:14
Sparse Core Ops, SparseCore 0:
  40.8 75.4 reduce-scatter.1
  174.2 135.2 all-reduce.1
where the time goes:
time: 319 us; the launch traced here: 318 us
  waiting for transfers between devices  156 us (49%)
  blocking collectives  87.1 us (27%)
  other arithmetic  33.2 us (10%)
  matrix products  18.2 us (6%)
  between operations  14.8 us (5%)
  local copies, waits for them, and re-layouts  7.82 us (2%)
    psum x1, waiting for transfers between devices, body(): lax.psum((local_weight, local_bias), ('row', 'col'))  74.4 us
    reduce_scatter x1, waiting for transfers between devices, body(): lax.psum_scatter(partial_value.astype(jnp.bfloat16), 'col', scatter_dimen...  70.9 us
    psum x1, blocking collectives, body(): lax.psum((local_weight, local_bias), ('row', 'col'))  48.4 us
    all_gather x1, blocking collectives, body(): panel = lax.all_gather(agg_grad, 'col', axis=0, tiled=True)  31.3 us
    scatter-add x2, other arithmetic, forward_block(): jax.ops.segment_sum(product, group_rows, num_segments=row_tiles)  12.9 us
    scatter-add x2, other arithmetic, backward_block(): jax.ops.segment_sum(product, group_cols, num_segments=col_tiles)  12.8 us
    ppermute x3, waiting for transfers between devices, shifted(): return lax.ppermute(block, axis, route)  11 us
    dot_general x2, matrix products, forward_block(): jnp.einsum('tij,tjf->tif', tile_group, picked, preferred_element_type=jnp...  7.7 us
  transfers between devices with their start and end apart: 5, of which 5 were waited for; matrix products, arithmetic and copies ran while one was open for 2% of the time, Pallas kernels for 0%

commit v1 on v0

v1 whole, which is shorter than its diff:
```python
import functools
import math

import jax
import jax.numpy as jnp
from jax import lax
from jax.experimental import pallas as pl
from jax.experimental.pallas import tpu as pltpu
from jax.sharding import PartitionSpec as P

BF16 = jnp.bfloat16
F32 = jnp.float32
CHUNK = 8
BIAS_ROWS = 16
VMEM = pl.BlockSpec(memory_space=pltpu.VMEM)
ANY = pl.BlockSpec(memory_space=pl.ANY)
SMEM = pl.BlockSpec(memory_space=pltpu.SMEM)


def swapped(block, axis, bit):
    n = lax.axis_size(axis)
    return lax.ppermute(block, axis, [(i, i ^ bit) for i in range(n)])


def params(mib=32):
    return pltpu.CompilerParams(vmem_limit_bytes=mib * 1024 * 1024)


def build_kernel(col_tiles, pos_ref, count_ref, tiles_ref, panel_ref, stage, acc, sems):
    slots = tiles_ref.shape[0]
    size = tiles_ref.shape[1]
    count = count_ref[0]
    chunks = slots // CHUNK

    def copy(chunk):
        part = pl.ds(chunk * CHUNK, CHUNK)
        return pltpu.make_async_copy(tiles_ref.at[part], stage.at[part], sems.at[chunk])

    for chunk in range(chunks):
        @pl.when(chunk * CHUNK < count)
        def _():
            copy(chunk).start()

    acc[...] = jnp.zeros_like(acc)
    for chunk in range(chunks):
        @pl.when(chunk * CHUNK < count)
        def _():
            copy(chunk).wait()

            def add(slot, carry):
                place = pos_ref[slot]
                acc[place] += stage[slot].astype(F32)
                return carry

            lax.fori_loop(chunk * CHUNK, jnp.minimum(count, (chunk + 1) * CHUNK), add, 0)
    for place in range(acc.shape[0]):
        r, c = place // col_tiles, place % col_tiles
        panel_ref[r * size:(r + 1) * size, c * size:(c + 1) * size] = acc[place].astype(BF16)


def build_panel(positions, count, tiles, row_tiles, col_tiles):
    slots, size = tiles.shape[0], tiles.shape[1]
    places = row_tiles * col_tiles
    return pl.pallas_call(
        functools.partial(build_kernel, col_tiles),
        out_shape=jax.ShapeDtypeStruct((row_tiles * size, col_tiles * size), BF16),
        in_specs=[SMEM, SMEM, ANY],
        out_specs=VMEM,
        scratch_shapes=[
            pltpu.VMEM((slots, size, size), BF16),
            pltpu.VMEM((places, size, size), F32),
            pltpu.SemaphoreType.DMA((slots // CHUNK,)),
        ],
        compiler_params=params(max(52, (slots * 2 + places * 6) * size * size // 2**20 + 4)),
        cost_estimate=pl.CostEstimate(
            flops=slots * size * size, bytes_accessed=2 * slots * size * size, transcendentals=0
        ),
        name="build_panel",
    )(positions, count, tiles)


def peers(count):
    return sorted(range(2, count, 2), key=lambda d: (abs(d - count // 2 - 0.5), d)) + [0]


def tree_order(count):
    return list(range(2, count, 2))


def forward_kernel(count, me_ref, panel_ref, *refs):
    blocks, outs, gathered = refs[:count], refs[count:-1], refs[-1]
    rows = blocks[0].shape[0]
    row_me, col_me = me_ref[0], me_ref[1]
    half = len(outs) // 2
    keeps, sends = outs[:half], outs[half:]
    for d in range(count):
        source = jnp.bitwise_xor(row_me, d)
        gathered[pl.ds(pl.multiple_of(source * rows, rows), rows), :] = blocks[d][...]

    def product(target):
        part = panel_ref[pl.ds(pl.multiple_of(target * rows, rows), rows), :]
        return jnp.dot(part, gathered[...], preferred_element_type=F32)

    for k, d in enumerate(peers(len(outs))):
        sends[k][...] = product(jnp.bitwise_xor(col_me, d + 1)).astype(BF16)
    for k, d in enumerate(peers(len(outs))):
        keeps[k][...] = product(jnp.bitwise_xor(col_me, d))


def forward(me, panel, blocks, col_count):
    rows, width = blocks[0].shape
    half = col_count // 2
    out = pl.pallas_call(
        functools.partial(forward_kernel, len(blocks)),
        out_shape=[jax.ShapeDtypeStruct((rows, width), F32)] * half
        + [jax.ShapeDtypeStruct((rows, width), BF16)] * half,
        in_specs=[SMEM, VMEM] + [VMEM] * len(blocks),
        out_specs=[VMEM] * col_count,
        scratch_shapes=[pltpu.VMEM((rows * len(blocks), width), BF16)],
        compiler_params=params(),
        name="forward_partial",
    )(me, panel, *blocks)
    return out[:half], out[half:]


def split_bias(value):
    high = value.astype(BF16)
    low = (value - high.astype(F32)).astype(BF16)
    return high, low


def bias_rows(value):
    high, low = split_bias(value)
    row = lax.broadcasted_iota(jnp.int32, (BIAS_ROWS, value.shape[1]), 0)
    high, low = high.astype(F32), low.astype(F32)
    return jnp.where(row == 0, high, jnp.where(row == 1, low, 0.0)).astype(BF16)


def bias_value(rows):
    return jnp.sum(rows.astype(F32), axis=0, keepdims=True)


def dense_kernel(count, me_ref, weight_ref, bias_ref, grad_ref, *refs):
    parts, outs = refs[:count], refs[count:]
    hidden_ref, agg_grad_ref, own_ref = outs[:3]
    messages, weights = outs[3:-1], outs[-1]
    rows, width = grad_ref.shape
    groups = len(messages) + 1
    chunk = width // groups
    total = parts[0][...].astype(F32)
    for part in parts[1:]:
        total = total + part[...].astype(F32)
    aggregated = total.astype(BF16)
    weight = weight_ref[...]
    pre = jnp.dot(aggregated, weight, preferred_element_type=F32) + bias_ref[...]
    gate = jax.nn.sigmoid(pre)
    hidden_ref[...] = (pre * gate).astype(BF16)
    pre_grad = (grad_ref[...].astype(F32) * (gate * (1.0 + pre * (1.0 - gate)))).astype(BF16)
    agg_grad = lax.dot_general(
        pre_grad, weight, (((1,), (1,)), ((), ())), preferred_element_type=F32
    ).astype(BF16)
    agg_grad_ref[...] = agg_grad
    weights[...] = lax.dot_general(
        aggregated, pre_grad, (((0,), (0,)), ((), ())), preferred_element_type=F32
    ).astype(BF16)
    bias_part = bias_rows(jnp.sum(pre_grad.astype(F32), axis=0, keepdims=True))

    def section(d):
        group = jnp.right_shift(jnp.bitwise_xor(me_ref[1], d), 1)
        return weights[pl.ds(pl.multiple_of(group * chunk, chunk), chunk), :]

    for d, message in zip(peers(2 * groups)[:-1], messages):
        message[:rows, :] = agg_grad
        message[rows:rows + chunk, :] = section(d)
        message[rows + chunk:, :] = bias_part
    own_ref[:chunk, :] = section(0)
    own_ref[chunk:, :] = bias_part


def dense(me, weight, bias_vector, out_grad, parts, groups):
    rows, width = out_grad.shape
    extra = width // groups + BIAS_ROWS
    return pl.pallas_call(
        functools.partial(dense_kernel, len(parts)),
        out_shape=[jax.ShapeDtypeStruct(out_grad.shape, BF16)] * 2
        + [jax.ShapeDtypeStruct((extra, width), BF16)]
        + [jax.ShapeDtypeStruct((rows + extra, width), BF16)] * (groups - 1),
        in_specs=[SMEM] + [VMEM] * (3 + len(parts)),
        out_specs=[VMEM] * (2 + groups),
        scratch_shapes=[pltpu.VMEM(weight.shape, BF16)],
        compiler_params=params(),
        name="dense_stage",
    )(me, weight, bias_vector, out_grad, *parts)


def tree_sum(values):
    while len(values) > 1:
        values = [values[k] + values[k + 1] for k in range(0, len(values), 2)]
    return values[0]


def gradient_sums(refs, start):
    weight = tree_sum([ref[start(ref):ref.shape[0] - BIAS_ROWS, :].astype(F32) for ref in refs])
    bias = tree_sum([bias_value(ref[ref.shape[0] - BIAS_ROWS:, :]) for ref in refs])
    return weight, bias


def relay_kernel(agg_grad_ref, own_ref, *refs):
    arrived, out_ref = refs[:-1], refs[-1]
    rows = agg_grad_ref.shape[0]
    extra = own_ref.shape[0]
    weight, bias = gradient_sums([own_ref, *arrived], lambda ref: ref.shape[0] - extra)
    out_ref[:rows, :] = agg_grad_ref[...]
    out_ref[rows:-BIAS_ROWS, :] = weight.astype(BF16)
    out_ref[-BIAS_ROWS:, :] = bias_rows(bias)


def relay(agg_grad, own, arrived):
    return pl.pallas_call(
        relay_kernel,
        out_shape=jax.ShapeDtypeStruct(arrived[0].shape, BF16),
        in_specs=[VMEM] * (2 + len(arrived)),
        out_specs=VMEM,
        compiler_params=params(),
        name="relay_message",
    )(agg_grad, own, *arrived)


def totals_kernel(scale, own_ref, *refs):
    arrived, (weight_ref, bias_ref) = refs[:-2], refs[-2:]
    extra = own_ref.shape[0]
    weight, bias = gradient_sums([own_ref, *arrived], lambda ref: ref.shape[0] - extra)
    weight_ref[...] = (weight * scale).astype(BF16)
    bias_ref[...] = bias * scale


def totals(own, arrived, scale):
    extra, width = own.shape
    return pl.pallas_call(
        functools.partial(totals_kernel, scale),
        out_shape=[
            jax.ShapeDtypeStruct((extra - BIAS_ROWS, width), BF16),
            jax.ShapeDtypeStruct((1, width), F32),
        ],
        in_specs=[VMEM] * (1 + len(arrived)),
        out_specs=[VMEM] * 2,
        compiler_params=params(),
        name="gradient_totals",
    )(own, *arrived)


def feature_kernel(own_ref, *refs):
    arrived, out_ref = refs[:-1], refs[-1]
    rows = out_ref.shape[0]
    total = own_ref[...]
    for ref in arrived:
        total = total + ref[:rows, :].astype(F32)
    out_ref[...] = total.astype(BF16)


def feature_sum(own, arrived):
    return pl.pallas_call(
        feature_kernel,
        out_shape=jax.ShapeDtypeStruct(own.shape, BF16),
        in_specs=[VMEM] * (1 + len(arrived)),
        out_specs=VMEM,
        compiler_params=params(),
        name="feature_sum",
    )(own, *arrived)


def assemble_kernel(me_ref, *refs):
    sections, out_ref = refs[:-1], refs[-1]
    chunk = sections[0].shape[0]
    for d, ref in zip([0] + peers(2 * len(sections))[:-1], sections):
        group = jnp.right_shift(jnp.bitwise_xor(me_ref[1], d), 1)
        out_ref[pl.ds(pl.multiple_of(group * chunk, chunk), chunk), :] = ref[...].astype(F32)


def assemble(me, sections):
    chunk, width = sections[0].shape
    return pl.pallas_call(
        assemble_kernel,
        out_shape=jax.ShapeDtypeStruct((chunk * len(sections), width), F32),
        in_specs=[SMEM] + [VMEM] * len(sections),
        out_specs=VMEM,
        compiler_params=params(),
        name="assemble_weight_grad",
    )(me, *sections)


def backward_kernel(count, me_ref, panel_ref, sent_ref, *refs):
    blocks, outs, gathered = refs[:count], refs[count:-1], refs[-1]
    rows = blocks[0].shape[0]
    own_ref, share_ref, messages = outs[0], outs[1], outs[2:]
    weight, bias = gradient_sums([sent_ref, blocks[1]], lambda ref: rows)
    weight, bias_part = weight.astype(BF16), bias_rows(bias)
    row_me, col_me = me_ref[0], me_ref[1]
    for d in range(count):
        source = jnp.bitwise_xor(col_me, d)
        gathered[pl.ds(pl.multiple_of(source * rows, rows), rows), :] = blocks[d][:rows, :]

    def product(d):
        target = jnp.bitwise_xor(row_me, d)
        part = panel_ref[:, pl.ds(pl.multiple_of(target * rows, rows), rows)]
        return lax.dot_general(part, gathered[...], (((0,), (0,)), ((), ())), preferred_element_type=F32)

    for d, message in enumerate(messages, 1):
        message[:rows, :] = product(d).astype(BF16)
        message[rows:-BIAS_ROWS, :] = weight
        message[-BIAS_ROWS:, :] = bias_part
    own_ref[...] = product(0)
    share_ref[:-BIAS_ROWS, :] = weight
    share_ref[-BIAS_ROWS:, :] = bias_part


def backward(me, panel, sent, blocks, row_count):
    rows, width = blocks[0].shape
    size = sent.shape[0]
    out = pl.pallas_call(
        functools.partial(backward_kernel, len(blocks)),
        out_shape=[
            jax.ShapeDtypeStruct((rows, width), F32),
            jax.ShapeDtypeStruct((size - rows, width), BF16),
        ]
        + [jax.ShapeDtypeStruct((size, width), BF16)] * (row_count - 1),
        in_specs=[SMEM, VMEM, VMEM] + [VMEM] * len(blocks),
        out_specs=[VMEM] * (row_count + 1),
        scratch_shapes=[pltpu.VMEM((rows * len(blocks), width), BF16)],
        compiler_params=params(),
        name="backward_terms",
    )(me, panel, sent, *blocks)
    return out[0], out[1], out[2:]


def body(features, weight, bias_vector, out_grad, adj_tiles, tile_pos, tile_count):
    rows_dev, width = features.shape
    tile_size = adj_tiles.shape[-1]
    row_count = lax.axis_size("row")
    col_count = lax.axis_size("col")
    row_tiles = col_count * rows_dev // tile_size
    col_tiles = row_count * rows_dev // tile_size
    me = jnp.stack([lax.axis_index("row"), lax.axis_index("col")]).astype(jnp.int32)

    blocks = [features] + [swapped(features, "row", d) for d in range(1, row_count)]
    panel = build_panel(tile_pos[0, 0], tile_count[0], adj_tiles[0, 0], row_tiles, col_tiles)
    keeps, sends = forward(me, panel, blocks, col_count)
    parts = []
    for d, keep, send in zip(peers(col_count), keeps, sends):
        arrived = swapped(send, "col", 1)
        if d:
            pair = (keep + arrived.astype(F32)).astype(BF16)
            parts.append(swapped(pair, "col", d))
        else:
            parts += [keep, arrived]
    groups = col_count // 2
    order = peers(col_count)[:-1]
    hidden_out, agg_grad, share, *messages = dense(
        me, weight, bias_vector.reshape(1, width), out_grad, parts, groups
    )
    grads = {0: agg_grad}
    for d, message in zip(order, messages):
        grads[d] = swapped(message, "col", d)
    sent = relay(agg_grad, share, [grads[d] for d in tree_order(col_count)])
    grads[1] = swapped(sent, "col", 1)
    for d in order:
        grads[d + 1] = swapped(grads[d][:rows_dev], "col", 1)
    blocks = [grads[d] for d in range(col_count)]
    own, share, messages = backward(me, panel, sent, blocks, row_count)
    arrived = {d: swapped(messages[d - 1], "row", d) for d in range(row_count - 1, 0, -1)}
    arrived = [arrived[d] for d in range(1, row_count)]
    scale = 1.0 / math.sqrt(row_count * col_count * rows_dev)
    section, bias_grad = totals(share, arrived, scale)
    weight_grad = assemble(me, [section] + [swapped(section, "col", d) for d in order])
    feature_grad = feature_sum(own, arrived)
    return (hidden_out, feature_grad, weight_grad, bias_grad.reshape(width))


def solution(mesh):
    in_specs = (
        P(("row", "col"), None),
        P(),
        P(),
        P(("row", "col"), None),
        P("row", "col", None, None, None),
        P("row", "col", None),
        P("row", "col"),
    )
    out_specs = (P(("row", "col"), None), P(("row", "col"), None), P(), P())
    return jax.shard_map(body, mesh=mesh, in_specs=in_specs, out_specs=out_specs, check_vma=False)
```

time: 319 us -> 62.4 us (0.20)
  waiting for transfers between devices: 156 us -> 23.4 us
  blocking collectives: 87.1 us -> 0 us
  other arithmetic: 33.2 us -> 0.13 us
  starting transfers between devices: 0.3 us -> 28.9 us
  matrix products: 18.2 us -> 0 us
  between operations: 14.8 us -> 1.41 us
  Pallas kernels: 0 us -> 8.45 us
  local copies, waits for them, and re-layouts: 7.82 us -> 0.68 us
    psum x1 -> x0, waiting for transfers between devices: 74.4 us -> none  [body(): lax.psum((local_weight, local_bias), ('row', 'col'))]
    reduce_scatter x1 -> x0, waiting for transfers between devices: 70.9 us -> none  [body(): lax.psum_scatter(partial_value.astype(jnp.bfloat16), 'col', scatter_dimen...]
    psum x1 -> x0, blocking collectives: 48.4 us -> none  [body(): lax.psum((local_weight, local_bias), ('row', 'col'))]
    all_gather x2 -> x0, blocking collectives: 38.7 us -> none  [the longest x1 31.3 us: body(): panel = lax.all_gather(agg_grad, 'col', axis=0, tiled=True)]
    ppermute x3 -> x23, starting transfers between devices: 0.22 us -> 28.9 us  [swapped(): return lax.ppermute(block, axis, [(i, i ^ bit) for i in range(n)])]
    scatter-add x4 -> x0, other arithmetic: 25.7 us -> none  [the longest x2 12.9 us: forward_block(): jax.ops.segment_sum(product, group_rows, num_segments=row_tiles)]
    dot_general x7 -> x0, matrix products: 18.2 us -> none  [the longest x2 7.7 us: forward_block(): jnp.einsum('tij,tjf->tif', tile_group, picked, preferred_element_type=jnp...]
    ppermute x3 -> x23, waiting for transfers between devices: 11 us -> 23.4 us  [swapped(): return lax.ppermute(block, axis, [(i, i ^ bit) for i in range(n)])]
  transfers between devices with their start and end apart: 5 -> 23, of which waited for: 5 -> 12; matrix products, arithmetic and copies ran while one was open for 2% -> 0% of each run, Pallas kernels for 0% -> 5%
where the time goes in v1:
time: 62.4 us; the launch traced here: 62.9 us
  starting transfers between devices  28.9 us (46%)
  waiting for transfers between devices  23.4 us (38%)
  Pallas kernels  8.45 us (14%)
  between operations  1.41 us (2%)
  local copies, waits for them, and re-layouts  0.68 us (1%)
    ppermute x23, starting transfers between devices, swapped(): return lax.ppermute(block, axis, [(i, i ^ bit) for i in range(n)])  28.9 us
    ppermute x23, waiting for transfers between devices, swapped(): return lax.ppermute(block, axis, [(i, i ^ bit) for i in range(n)])  23.4 us
    pallas_call x1, Pallas kernels, build_panel(): pl.pallas_call(functools.partial(build_kernel, col_tiles), out_shape=jax....  2.44 us
    pallas_call x1, Pallas kernels, dense(): pl.pallas_call(functools.partial(dense_kernel, len(parts)), out_shape=[ja...  1.38 us
    pallas_call x1, Pallas kernels, assemble(): pl.pallas_call(assemble_kernel, out_shape=jax.ShapeDtypeStruct((chunk * l...  1.27 us
  transfers between devices with their start and end apart: 23, of which 12 were waited for; matrix products, arithmetic and copies ran while one was open for 0% of the time, Pallas kernels for 5%

profile of v1, /device:TPU:0, one launch (start us, length us, event | category | flops | bytes accessed | tf_op | source)
XLA Modules:
  0.0 62.9 jit_solution(5831686837588178278)
XLA Ops:
  0.6 3.0 %collective-permute-start.1 = (bf16[128,256]{1,0:T(8,128)(2,1)}, bf16[128,256]{1,0:T(8,128)(2,1)S(1)}, u32[]{:S(2)}, u32[]{:S(2)}) collective-permute-start(bf16[128,256]{1,0:T(8,128)(2,1)} %refs_0_.1), channel_id=1, source_target_pairs={{0,16},{8,24},{16,0},{24,8},{1,17},{9,25},{17,1},{25,9},{2,18},{10... | collective-permute-start | bytes 196616 | tf_op jit(solution)/shard_map/ppermute | solution.py:22
  5.2 2.4 %build_panel.1.panel_ref = bf16[1024,512]{1,0:T(8,128)(2,1)S(1)} custom-call(s32[96]{0:T(128)S(1)} %bitcast.9, s32[1]{0:T(128)} %bitcast.7.count_ref, bf16[96,128,128]{2,1,0:T(8,128)(2,1)} %bitcast.10), custom_call_target="tpu_custom_call" | custom-call | flops 1572864 | bytes 3145728 | tf_op jit(solution)/shard_map/build_panel/pallas_call | solution.py:64
  8.7 2.3 %collective-permute-start.3 = (bf16[128,256]{1,0:T(8,128)(2,1)S(1)}, bf16[128,256]{1,0:T(8,128)(2,1)S(1)}, u32[]{:S(2)}, u32[]{:S(2)}) collective-permute-start(bf16[128,256]{1,0:T(8,128)(2,1)S(1)} %get-tuple-element.26), channel_id=1, source_target_pairs={{0,1},{1,0},{2,3},{3,2},{4,5},{5,4},{6,7},{7,6},{8,9},{9,8},{10,11... | collective-permute-start | bytes 196616 | tf_op jit(solution)/shard_map/ppermute | solution.py:22
  11.1 1.9 %collective-permute-start.7 = (bf16[128,256]{1,0:T(8,128)(2,1)S(1)}, bf16[128,256]{1,0:T(8,128)(2,1)S(1)}, u32[]{:S(2)}, u32[]{:S(2)}) collective-permute-start(bf16[128,256]{1,0:T(8,128)(2,1)S(1)} %get-tuple-element.30), channel_id=1, source_target_pairs={{0,1},{1,0},{2,3},{3,2},{4,5},{5,4},{6,7},{7,6},{8,9},{9,8},{10,11... | collective-permute-start | bytes 196616 | tf_op jit(solution)/shard_map/ppermute | solution.py:22
  13.7 2.8 %collective-permute-start.4 = (bf16[128,256]{1,0:T(8,128)(2,1)S(1)}, bf16[128,256]{1,0:T(8,128)(2,1)S(1)}, u32[]{:S(2)}, u32[]{:S(2)}) collective-permute-start(bf16[128,256]{1,0:T(8,128)(2,1)S(1)} %add_convert_fusion.2), channel_id=1, source_target_pairs={{0,4},{1,5},{2,6},{3,7},{4,0},{5,1},{6,2},{7,3},{8,12},{9,13},{10,... | collective-permute-start | bytes 196616 | tf_op jit(solution)/shard_map/ppermute | solution.py:22
  16.5 3.0 %collective-permute-start.6 = (bf16[128,256]{1,0:T(8,128)(2,1)S(1)}, bf16[128,256]{1,0:T(8,128)(2,1)S(1)}, u32[]{:S(2)}, u32[]{:S(2)}) collective-permute-start(bf16[128,256]{1,0:T(8,128)(2,1)S(1)} %add_convert_fusion.1), channel_id=1, source_target_pairs={{0,6},{1,7},{2,4},{3,5},{4,2},{5,3},{6,0},{7,1},{8,14},{9,15},{10,... | collective-permute-start | bytes 196616 | tf_op jit(solution)/shard_map/ppermute | solution.py:22
  19.6 3.1 %collective-permute-done.6.refs_1_ = bf16[128,256]{1,0:T(8,128)(2,1)S(1)} collective-permute-done((bf16[128,256]{1,0:T(8,128)(2,1)S(1)}, bf16[128,256]{1,0:T(8,128)(2,1)S(1)}, u32[]{:S(2)}, u32[]{:S(2)}) %collective-permute-start.6) | collective-permute-done | bytes 65568 | tf_op jit(solution)/shard_map/ppermute | solution.py:22
  22.8 1.1 %collective-permute-done.8.refs_2_ = bf16[128,256]{1,0:T(8,128)(2,1)S(1)} collective-permute-done((bf16[128,256]{1,0:T(8,128)(2,1)S(1)}, bf16[128,256]{1,0:T(8,128)(2,1)S(1)}, u32[]{:S(2)}, u32[]{:S(2)}) %collective-permute-start.8) | collective-permute-done | bytes 65568 | tf_op jit(solution)/shard_map/ppermute | solution.py:22
  23.9 1.4 %dense_stage.1 = (bf16[128,256]{1,0:T(8,128)(2,1)}, bf16[128,256]{1,0:T(8,128)(2,1)S(1)}, bf16[80,256]{1,0:T(8,128)(2,1)S(1)}, bf16[208,256]{1,0:T(8,128)(2,1)S(...) custom-call(s32[2]{0:T(128)S(1)} %pad_add_fusion.me_ref, bf16[256,256]{1,0:T(8,128)(2,1)S(1)} %copy-done, ...), custom_call_target="tpu_custom_call" | custom-call | tf_op jit(solution)/shard_map/dense_stage/pallas_call | solution.py:183
  25.9 1.9 %collective-permute-start.11 = (bf16[208,256]{1,0:T(8,128)(2,1)S(1)}, bf16[208,256]{1,0:T(8,128)(2,1)S(1)}, u32[]{:S(2)}, u32[]{:S(2)}) collective-permute-start(bf16[208,256]{1,0:T(8,128)(2,1)S(1)} %get-tuple-element.37), channel_id=1, source_target_pairs={{0,4},{1,5},{2,6},{3,7},{4,0},{5,1},{6,2},{7,3},{8,12},{9,13},{10,... | collective-permute-start | bytes 319496 | tf_op jit(solution)/shard_map/ppermute | solution.py:22
  27.8 1.8 %collective-permute-start.12 = (bf16[208,256]{1,0:T(8,128)(2,1)S(1)}, bf16[208,256]{1,0:T(8,128)(2,1)S(1)}, u32[]{:S(2)}, u32[]{:S(2)}) collective-permute-start(bf16[208,256]{1,0:T(8,128)(2,1)S(1)} %get-tuple-element.38), channel_id=1, source_target_pairs={{0,6},{1,7},{2,4},{3,5},{4,2},{5,3},{6,0},{7,1},{8,14},{9,15},{10,... | collective-permute-start | bytes 319496 | tf_op jit(solution)/shard_map/ppermute | solution.py:22
  30.2 4.4 %collective-permute-done.11.refs_1_.refs_4_ = bf16[208,256]{1,0:T(8,128)(2,1)S(1)} collective-permute-done((bf16[208,256]{1,0:T(8,128)(2,1)S(1)}, bf16[208,256]{1,0:T(8,128)(2,1)S(1)}, u32[]{:S(2)}, u32[]{:S(2)}) %collective-permute-start.11) | collective-permute-done | bytes 106528 | tf_op jit(solution)/shard_map/ppermute | solution.py:22
  34.7 1.8 %collective-permute-start.13 = (bf16[208,256]{1,0:T(8,128)(2,1)S(1)}, bf16[208,256]{1,0:T(8,128)(2,1)S(1)}, u32[]{:S(2)}, u32[]{:S(2)}) collective-permute-start(bf16[208,256]{1,0:T(8,128)(2,1)S(1)} %relay_message.1.sent_ref), channel_id=1, source_target_pairs={{0,1},{1,0},{2,3},{3,2},{4,5},{5,4},{6,7},{7,6},{8,9},{9,8},{10,11... | collective-permute-start | bytes 319496 | tf_op jit(solution)/shard_map/ppermute | solution.py:22
  36.8 1.8 %collective-permute-start.15 = (bf16[128,256]{1,0:T(8,128)(2,1)S(1)}, bf16[128,256]{1,0:T(8,128)(2,1)S(1)}, u32[]{:S(2)}, u32[]{:S(2)}) collective-permute-start(bf16[128,256]{1,0:T(8,128)(2,1)S(1)} %slice.13), channel_id=1, source_target_pairs={{0,1},{1,0},{2,3},{3,2},{4,5},{5,4},{6,7},{7,6},{8,9},{9,8},{10,11... | collective-permute-start | bytes 196616 | tf_op jit(solution)/shard_map/ppermute | solution.py:22
  38.9 2.0 %collective-permute-done.14.refs_3_ = bf16[128,256]{1,0:T(8,128)(2,1)S(1)} collective-permute-done((bf16[128,256]{1,0:T(8,128)(2,1)S(1)}, bf16[128,256]{1,0:T(8,128)(2,1)S(1)}, u32[]{:S(2)}, u32[]{:S(2)}) %collective-permute-start.14) | collective-permute-done | bytes 65568 | tf_op jit(solution)/shard_map/ppermute | solution.py:22
  41.5 1.3 %collective-permute-done.16.refs_7_ = bf16[128,256]{1,0:T(8,128)(2,1)S(1)} collective-permute-done((bf16[128,256]{1,0:T(8,128)(2,1)S(1)}, bf16[128,256]{1,0:T(8,128)(2,1)S(1)}, u32[]{:S(2)}, u32[]{:S(2)}) %collective-permute-start.16) | collective-permute-done | bytes 65568 | tf_op jit(solution)/shard_map/ppermute | solution.py:22
  44.0 1.9 %collective-permute-start.18 = (bf16[208,256]{1,0:T(8,128)(2,1)S(1)}, bf16[208,256]{1,0:T(8,128)(2,1)S(1)}, u32[]{:S(2)}, u32[]{:S(2)}) collective-permute-start(bf16[208,256]{1,0:T(8,128)(2,1)S(1)} %get-tuple-element.41), channel_id=1, source_target_pairs={{0,16},{8,24},{16,0},{24,8},{1,17},{9,25},{17,1},{25,9},{2,18},{10... | collective-permute-start | bytes 319496 | tf_op jit(solution)/shard_map/ppermute | solution.py:22
  46.0 3.9 %collective-permute-done.18.refs_1_ = bf16[208,256]{1,0:T(8,128)(2,1)S(1)} collective-permute-done((bf16[208,256]{1,0:T(8,128)(2,1)S(1)}, bf16[208,256]{1,0:T(8,128)(2,1)S(1)}, u32[]{:S(2)}, u32[]{:S(2)}) %collective-permute-start.18) | collective-permute-done | bytes 106528 | tf_op jit(solution)/shard_map/ppermute | solution.py:22
  49.9 1.5 %collective-permute-done.19.refs_2_ = bf16[208,256]{1,0:T(8,128)(2,1)S(1)} collective-permute-done((bf16[208,256]{1,0:T(8,128)(2,1)S(1)}, bf16[208,256]{1,0:T(8,128)(2,1)S(1)}, u32[]{:S(2)}, u32[]{:S(2)}) %collective-permute-start.19) | collective-permute-done | bytes 106528 | tf_op jit(solution)/shard_map/ppermute | solution.py:22
  52.0 2.2 %collective-permute-start.22 = (bf16[64,256]{1,0:T(8,128)(2,1)S(1)}, bf16[64,256]{1,0:T(8,128)(2,1)S(1)}, u32[]{:S(2)}, u32[]{:S(2)}) collective-permute-start(bf16[64,256]{1,0:T(8,128)(2,1)S(1)} %get-tuple-element.44.refs_0_), channel_id=1, source_target_pairs={{0,2},{1,3},{2,0},{3,1},{4,6},{5,7},{6,4},{7,5},{8,10},{9,11},{10,... | collective-permute-start | bytes 98312 | tf_op jit(solution)/shard_map/ppermute | solution.py:22
  54.2 2.7 %collective-permute-start.21 = (bf16[64,256]{1,0:T(8,128)(2,1)S(1)}, bf16[64,256]{1,0:T(8,128)(2,1)S(1)}, u32[]{:S(2)}, u32[]{:S(2)}) collective-permute-start(bf16[64,256]{1,0:T(8,128)(2,1)S(1)} %get-tuple-element.44.refs_0_), channel_id=1, source_target_pairs={{0,6},{1,7},{2,4},{3,5},{4,2},{5,3},{6,0},{7,1},{8,14},{9,15},{10,... | collective-permute-start | bytes 98312 | tf_op jit(solution)/shard_map/ppermute | solution.py:22
  57.5 2.4 %collective-permute-done.21.refs_2_ = bf16[64,256]{1,0:T(8,128)(2,1)S(1)} collective-permute-done((bf16[64,256]{1,0:T(8,128)(2,1)S(1)}, bf16[64,256]{1,0:T(8,128)(2,1)S(1)}, u32[]{:S(2)}, u32[]{:S(2)}) %collective-permute-start.21) | collective-permute-done | bytes 32800 | tf_op jit(solution)/shard_map/ppermute | solution.py:22
  59.9 1.8 %collective-permute-done.20.refs_1_ = bf16[64,256]{1,0:T(8,128)(2,1)S(1)} collective-permute-done((bf16[64,256]{1,0:T(8,128)(2,1)S(1)}, bf16[64,256]{1,0:T(8,128)(2,1)S(1)}, u32[]{:S(2)}, u32[]{:S(2)}) %collective-permute-start.20) | collective-permute-done | bytes 32800 | tf_op jit(solution)/shard_map/ppermute | solution.py:22
  61.6 1.3 %assemble_weight_grad.1 = f32[256,256]{1,0:T(8,128)} custom-call(s32[2]{0:T(128)S(1)} %pad_add_fusion.me_ref, bf16[64,256]{1,0:T(8,128)(2,1)S(1)} %get-tuple-element.44.refs_0_, bf16[64,256]{1,0:T(8,128)(2,1)S(1)} %collective-permute-done.20.refs_1_, bf16[64,256]{1,0:T(8,128)(2,1)S(1)} %collective-permute-done.21.refs_2_, ...), custom_call_target="tpu_custom_call" | custom-call | tf_op jit(solution)/shard_map/assemble_weight_grad/pallas_call | solution.py:282
  (47 shorter events, 7.7 us)
Async XLA Ops:
  0.6 7.1 %collective-permute-start.1 = (bf16[128,256]{1,0:T(8,128)(2,1)}, bf16[128,256]{1,0:T(8,128)(2,1)S(1)}, u32[]{:S(2)}, u32[]{:S(2)}) collective-permute-start(bf16[128,256]{1,0:T(8,128)(2,1)} %refs_0_.1), channel_id=1, source_target_pairs={{0,16},{8,24},{16,0},{24,8},{1,17},{9,25},{17,1},{25,9},{2,18},{10... | collective-permute-start | bytes 196616 | tf_op jit(solution)/shard_map/ppermute | solution.py:22
  3.6 4.1 %collective-permute-start = (bf16[128,256]{1,0:T(8,128)(2,1)}, bf16[128,256]{1,0:T(8,128)(2,1)S(1)}, u32[]{:S(2)}, u32[]{:S(2)}) collective-permute-start(bf16[128,256]{1,0:T(8,128)(2,1)} %refs_0_.1), channel_id=1, source_target_pairs={{0,8},{8,0},{16,24},{24,16},{1,9},{9,1},{17,25},{25,17},{2,10},{10... | collective-permute-start | bytes 196616 | tf_op jit(solution)/shard_map/ppermute | solution.py:22
  3.6 4.1 %collective-permute-start.2 = (bf16[128,256]{1,0:T(8,128)(2,1)}, bf16[128,256]{1,0:T(8,128)(2,1)S(1)}, u32[]{:S(2)}, u32[]{:S(2)}) collective-permute-start(bf16[128,256]{1,0:T(8,128)(2,1)} %refs_0_.1), channel_id=1, source_target_pairs={{0,24},{8,16},{16,8},{24,0},{1,25},{9,17},{17,9},{25,1},{2,26},{10... | collective-permute-start | bytes 196616 | tf_op jit(solution)/shard_map/ppermute | solution.py:22
  5.2 18.7 %copy-start.3 = (f32[256]{0:T(256)S(1)}, f32[256]{0:T(256)}, u32[]{:S(2)}) copy-start(f32[256]{0:T(256)} %param.9) | copy-start | bytes 3076
  8.7 5.0 %collective-permute-start.3 = (bf16[128,256]{1,0:T(8,128)(2,1)S(1)}, bf16[128,256]{1,0:T(8,128)(2,1)S(1)}, u32[]{:S(2)}, u32[]{:S(2)}) collective-permute-start(bf16[128,256]{1,0:T(8,128)(2,1)S(1)} %get-tuple-element.26), channel_id=1, source_target_pairs={{0,1},{1,0},{2,3},{3,2},{4,5},{5,4},{6,7},{7,6},{8,9},{9,8},{10,11... | collective-permute-start | bytes 196616 | tf_op jit(solution)/shard_map/ppermute | solution.py:22
  11.1 5.5 %collective-permute-start.5 = (bf16[128,256]{1,0:T(8,128)(2,1)S(1)}, bf16[128,256]{1,0:T(8,128)(2,1)S(1)}, u32[]{:S(2)}, u32[]{:S(2)}) collective-permute-start(bf16[128,256]{1,0:T(8,128)(2,1)S(1)} %get-tuple-element.28), channel_id=1, source_target_pairs={{0,1},{1,0},{2,3},{3,2},{4,5},{5,4},{6,7},{7,6},{8,9},{9,8},{10,11... | collective-permute-start | bytes 196616 | tf_op jit(solution)/shard_map/ppermute | solution.py:22
  11.1 8.4 %collective-permute-start.7 = (bf16[128,256]{1,0:T(8,128)(2,1)S(1)}, bf16[128,256]{1,0:T(8,128)(2,1)S(1)}, u32[]{:S(2)}, u32[]{:S(2)}) collective-permute-start(bf16[128,256]{1,0:T(8,128)(2,1)S(1)} %get-tuple-element.30), channel_id=1, source_target_pairs={{0,1},{1,0},{2,3},{3,2},{4,5},{5,4},{6,7},{7,6},{8,9},{9,8},{10,11... | collective-permute-start | bytes 196616 | tf_op jit(solution)/shard_map/ppermute | solution.py:22
  13.1 6.5 %collective-permute-start.9 = (bf16[128,256]{1,0:T(8,128)(2,1)S(1)}, bf16[128,256]{1,0:T(8,128)(2,1)S(1)}, u32[]{:S(2)}, u32[]{:S(2)}) collective-permute-start(bf16[128,256]{1,0:T(8,128)(2,1)S(1)} %get-tuple-element.32), channel_id=1, source_target_pairs={{0,1},{1,0},{2,3},{3,2},{4,5},{5,4},{6,7},{7,6},{8,9},{9,8},{10,11... | collective-permute-start | bytes 196616 | tf_op jit(solution)/shard_map/ppermute | solution.py:22
  13.7 5.9 %collective-permute-start.4 = (bf16[128,256]{1,0:T(8,128)(2,1)S(1)}, bf16[128,256]{1,0:T(8,128)(2,1)S(1)}, u32[]{:S(2)}, u32[]{:S(2)}) collective-permute-start(bf16[128,256]{1,0:T(8,128)(2,1)S(1)} %add_convert_fusion.2), channel_id=1, source_target_pairs={{0,4},{1,5},{2,6},{3,7},{4,0},{5,1},{6,2},{7,3},{8,12},{9,13},{10,... | collective-permute-start | bytes 196616 | tf_op jit(solution)/shard_map/ppermute | solution.py:22
  16.5 6.2 %collective-permute-start.6 = (bf16[128,256]{1,0:T(8,128)(2,1)S(1)}, bf16[128,256]{1,0:T(8,128)(2,1)S(1)}, u32[]{:S(2)}, u32[]{:S(2)}) collective-permute-start(bf16[128,256]{1,0:T(8,128)(2,1)S(1)} %add_convert_fusion.1), channel_id=1, source_target_pairs={{0,6},{1,7},{2,4},{3,5},{4,2},{5,3},{6,0},{7,1},{8,14},{9,15},{10,... | collective-permute-start | bytes 196616 | tf_op jit(solution)/shard_map/ppermute | solution.py:22
  19.5 4.3 %collective-permute-start.8 = (bf16[128,256]{1,0:T(8,128)(2,1)S(1)}, bf16[128,256]{1,0:T(8,128)(2,1)S(1)}, u32[]{:S(2)}, u32[]{:S(2)}) collective-permute-start(bf16[128,256]{1,0:T(8,128)(2,1)S(1)} %add_convert_fusion), channel_id=1, source_target_pairs={{0,2},{1,3},{2,0},{3,1},{4,6},{5,7},{6,4},{7,5},{8,10},{9,11},{10,... | collective-permute-start | bytes 196616 | tf_op jit(solution)/shard_map/ppermute | solution.py:22
  25.3 5.0 %collective-permute-start.10 = (bf16[208,256]{1,0:T(8,128)(2,1)S(1)}, bf16[208,256]{1,0:T(8,128)(2,1)S(1)}, u32[]{:S(2)}, u32[]{:S(2)}) collective-permute-start(bf16[208,256]{1,0:T(8,128)(2,1)S(1)} %get-tuple-element.36), channel_id=1, source_target_pairs={{0,2},{1,3},{2,0},{3,1},{4,6},{5,7},{6,4},{7,5},{8,10},{9,11},{10,... | collective-permute-start | bytes 319496 | tf_op jit(solution)/shard_map/ppermute | solution.py:22
  25.9 8.8 %collective-permute-start.11 = (bf16[208,256]{1,0:T(8,128)(2,1)S(1)}, bf16[208,256]{1,0:T(8,128)(2,1)S(1)}, u32[]{:S(2)}, u32[]{:S(2)}) collective-permute-start(bf16[208,256]{1,0:T(8,128)(2,1)S(1)} %get-tuple-element.37), channel_id=1, source_target_pairs={{0,4},{1,5},{2,6},{3,7},{4,0},{5,1},{6,2},{7,3},{8,12},{9,13},{10,... | collective-permute-start | bytes 319496 | tf_op jit(solution)/shard_map/ppermute | solution.py:22
  27.8 6.9 %collective-permute-start.12 = (bf16[208,256]{1,0:T(8,128)(2,1)S(1)}, bf16[208,256]{1,0:T(8,128)(2,1)S(1)}, u32[]{:S(2)}, u32[]{:S(2)}) collective-permute-start(bf16[208,256]{1,0:T(8,128)(2,1)S(1)} %get-tuple-element.38), channel_id=1, source_target_pairs={{0,6},{1,7},{2,4},{3,5},{4,2},{5,3},{6,0},{7,1},{8,14},{9,15},{10,... | collective-permute-start | bytes 319496 | tf_op jit(solution)/shard_map/ppermute | solution.py:22
  34.7 8.1 %collective-permute-start.13 = (bf16[208,256]{1,0:T(8,128)(2,1)S(1)}, bf16[208,256]{1,0:T(8,128)(2,1)S(1)}, u32[]{:S(2)}, u32[]{:S(2)}) collective-permute-start(bf16[208,256]{1,0:T(8,128)(2,1)S(1)} %relay_message.1.sent_ref), channel_id=1, source_target_pairs={{0,1},{1,0},{2,3},{3,2},{4,5},{5,4},{6,7},{7,6},{8,9},{9,8},{10,11... | collective-permute-start | bytes 319496 | tf_op jit(solution)/shard_map/ppermute | solution.py:22
  36.6 4.3 %collective-permute-start.14 = (bf16[128,256]{1,0:T(8,128)(2,1)S(1)}, bf16[128,256]{1,0:T(8,128)(2,1)S(1)}, u32[]{:S(2)}, u32[]{:S(2)}) collective-permute-start(bf16[128,256]{1,0:T(8,128)(2,1)S(1)} %slice.12), channel_id=1, source_target_pairs={{0,1},{1,0},{2,3},{3,2},{4,5},{5,4},{6,7},{7,6},{8,9},{9,8},{10,11... | collective-permute-start | bytes 196616 | tf_op jit(solution)/shard_map/ppermute | solution.py:22
  36.8 4.7 %collective-permute-start.15 = (bf16[128,256]{1,0:T(8,128)(2,1)S(1)}, bf16[128,256]{1,0:T(8,128)(2,1)S(1)}, u32[]{:S(2)}, u32[]{:S(2)}) collective-permute-start(bf16[128,256]{1,0:T(8,128)(2,1)S(1)} %slice.13), channel_id=1, source_target_pairs={{0,1},{1,0},{2,3},{3,2},{4,5},{5,4},{6,7},{7,6},{8,9},{9,8},{10,11... | collective-permute-start | bytes 196616 | tf_op jit(solution)/shard_map/ppermute | solution.py:22
  38.6 4.3 %collective-permute-start.16 = (bf16[128,256]{1,0:T(8,128)(2,1)S(1)}, bf16[128,256]{1,0:T(8,128)(2,1)S(1)}, u32[]{:S(2)}, u32[]{:S(2)}) collective-permute-start(bf16[128,256]{1,0:T(8,128)(2,1)S(1)} %slice.14), channel_id=1, source_target_pairs={{0,1},{1,0},{2,3},{3,2},{4,5},{5,4},{6,7},{7,6},{8,9},{9,8},{10,11... | collective-permute-start | bytes 196616 | tf_op jit(solution)/shard_map/ppermute | solution.py:22
  43.9 2.0 %collective-permute-start.17 = (bf16[208,256]{1,0:T(8,128)(2,1)S(1)}, bf16[208,256]{1,0:T(8,128)(2,1)S(1)}, u32[]{:S(2)}, u32[]{:S(2)}) collective-permute-start(bf16[208,256]{1,0:T(8,128)(2,1)S(1)} %get-tuple-element.40), channel_id=1, source_target_pairs={{0,8},{8,0},{16,24},{24,16},{1,9},{9,1},{17,25},{25,17},{2,10},{10... | collective-permute-start | bytes 319496 | tf_op jit(solution)/shard_map/ppermute | solution.py:22
  44.0 5.8 %collective-permute-start.18 = (bf16[208,256]{1,0:T(8,128)(2,1)S(1)}, bf16[208,256]{1,0:T(8,128)(2,1)S(1)}, u32[]{:S(2)}, u32[]{:S(2)}) collective-permute-start(bf16[208,256]{1,0:T(8,128)(2,1)S(1)} %get-tuple-element.41), channel_id=1, source_target_pairs={{0,16},{8,24},{16,0},{24,8},{1,17},{9,25},{17,1},{25,9},{2,18},{10... | collective-permute-start | bytes 319496 | tf_op jit(solution)/shard_map/ppermute | solution.py:22
  45.9 5.5 %collective-permute-start.19 = (bf16[208,256]{1,0:T(8,128)(2,1)S(1)}, bf16[208,256]{1,0:T(8,128)(2,1)S(1)}, u32[]{:S(2)}, u32[]{:S(2)}) collective-permute-start(bf16[208,256]{1,0:T(8,128)(2,1)S(1)} %get-tuple-element.42), channel_id=1, source_target_pairs={{0,24},{8,16},{16,8},{24,0},{1,25},{9,17},{17,9},{25,1},{2,26},{10... | collective-permute-start | bytes 319496 | tf_op jit(solution)/shard_map/ppermute | solution.py:22
  52.0 5.5 %collective-permute-start.22 = (bf16[64,256]{1,0:T(8,128)(2,1)S(1)}, bf16[64,256]{1,0:T(8,128)(2,1)S(1)}, u32[]{:S(2)}, u32[]{:S(2)}) collective-permute-start(bf16[64,256]{1,0:T(8,128)(2,1)S(1)} %get-tuple-element.44.refs_0_), channel_id=1, source_target_pairs={{0,2},{1,3},{2,0},{3,1},{4,6},{5,7},{6,4},{7,5},{8,10},{9,11},{10,... | collective-permute-start | bytes 98312 | tf_op jit(solution)/shard_map/ppermute | solution.py:22
  54.2 5.7 %collective-permute-start.21 = (bf16[64,256]{1,0:T(8,128)(2,1)S(1)}, bf16[64,256]{1,0:T(8,128)(2,1)S(1)}, u32[]{:S(2)}, u32[]{:S(2)}) collective-permute-start(bf16[64,256]{1,0:T(8,128)(2,1)S(1)} %get-tuple-element.44.refs_0_), channel_id=1, source_target_pairs={{0,6},{1,7},{2,4},{3,5},{4,2},{5,3},{6,0},{7,1},{8,14},{9,15},{10,... | collective-permute-start | bytes 98312 | tf_op jit(solution)/shard_map/ppermute | solution.py:22
  56.8 4.8 %collective-permute-start.20 = (bf16[64,256]{1,0:T(8,128)(2,1)S(1)}, bf16[64,256]{1,0:T(8,128)(2,1)S(1)}, u32[]{:S(2)}, u32[]{:S(2)}) collective-permute-start(bf16[64,256]{1,0:T(8,128)(2,1)S(1)} %get-tuple-element.44.refs_0_), channel_id=1, source_target_pairs={{0,4},{1,5},{2,6},{3,7},{4,0},{5,1},{6,2},{7,3},{8,12},{9,13},{10,... | collective-permute-start | bytes 98312 | tf_op jit(solution)/shard_map/ppermute | solution.py:22
  (4 other events, 45.2 us)

commit v2 on v1

v2 whole, which is shorter than its diff:
```python
import functools
import math

import jax
import jax.numpy as jnp
from jax import lax
from jax.experimental import pallas as pl
from jax.experimental.pallas import tpu as pltpu
from jax.sharding import PartitionSpec as P

BF16 = jnp.bfloat16
F32 = jnp.float32
CHUNK = 8
BIAS_ROWS = 16
VMEM = pl.BlockSpec(memory_space=pltpu.VMEM)
ANY = pl.BlockSpec(memory_space=pl.ANY)
SMEM = pl.BlockSpec(memory_space=pltpu.SMEM)


def swapped(block, axis, bit):
    n = lax.axis_size(axis)
    return lax.ppermute(block, axis, [(i, i ^ bit) for i in range(n)])


def params(mib=32):
    return pltpu.CompilerParams(vmem_limit_bytes=mib * 1024 * 1024)


def build_kernel(col_tiles, pos_ref, count_ref, tiles_ref, panel_ref, stage, acc, places, live, sems):
    slots = tiles_ref.shape[0]
    size = tiles_ref.shape[1]
    chunks = slots // CHUNK
    copies = [
        pltpu.make_async_copy(pos_ref, places, sems.at[chunks]),
        pltpu.make_async_copy(count_ref, live, sems.at[chunks + 1]),
    ]
    for chunk in range(chunks):
        part = pl.ds(chunk * CHUNK, CHUNK)
        copies.append(pltpu.make_async_copy(tiles_ref.at[part], stage.at[part], sems.at[chunk]))
    for copy in copies:
        copy.start()
    acc[...] = jnp.zeros_like(acc)
    copies[0].wait()
    copies[1].wait()
    count = live[0, 0]

    def add(slot, carry):
        acc[places[0, slot]] += stage[slot].astype(F32)
        return carry

    for chunk in range(chunks):
        copies[chunk + 2].wait()
        lax.fori_loop(chunk * CHUNK, jnp.minimum(count, (chunk + 1) * CHUNK), add, 0)
    for place in range(acc.shape[0]):
        r, c = place // col_tiles, place % col_tiles
        panel_ref[r * size:(r + 1) * size, c * size:(c + 1) * size] = acc[place].astype(BF16)


def build_panel(positions, count, tiles, row_tiles, col_tiles):
    slots, size = tiles.shape[0], tiles.shape[1]
    places = row_tiles * col_tiles
    return pl.pallas_call(
        functools.partial(build_kernel, col_tiles),
        out_shape=jax.ShapeDtypeStruct((row_tiles * size, col_tiles * size), BF16),
        in_specs=[pl.BlockSpec(memory_space=pltpu.HBM)] * 3,
        out_specs=VMEM,
        scratch_shapes=[
            pltpu.VMEM((slots, size, size), BF16),
            pltpu.VMEM((places, size, size), F32),
            pltpu.SMEM((1, slots), jnp.int32),
            pltpu.SMEM((1, 1), jnp.int32),
            pltpu.SemaphoreType.DMA((slots // CHUNK + 2,)),
        ],
        compiler_params=params(max(52, (slots * 2 + places * 6) * size * size // 2**20 + 4)),
        cost_estimate=pl.CostEstimate(
            flops=slots * size * size, bytes_accessed=2 * slots * size * size, transcendentals=0
        ),
        name="build_panel",
    )(positions, count, tiles)


def peers(count):
    return sorted(range(2, count, 2), key=lambda d: (abs(d - count // 2 - 0.5), d)) + [0]


def forward_kernel(count, flip, panel_ref, *refs):
    blocks, outs, gathered = refs[:count], refs[count:-1], refs[-1]
    rows = blocks[0].shape[0]
    row_me, col_me = lax.axis_index("row"), lax.axis_index("col")
    for d in range(count):
        source = jnp.bitwise_xor(row_me, d)
        gathered[pl.ds(pl.multiple_of(source * rows, rows), rows), :] = blocks[d][...]
    for d, out in zip(peers(2 * len(outs)), outs):
        target = jnp.bitwise_xor(col_me, d + flip)
        part = panel_ref[pl.ds(pl.multiple_of(target * rows, rows), rows), :]
        out[...] = jnp.dot(part, gathered[...], preferred_element_type=F32).astype(out.dtype)


def forward(panel, blocks, half, flip, dtype):
    rows, width = blocks[0].shape
    return pl.pallas_call(
        functools.partial(forward_kernel, len(blocks), flip),
        out_shape=[jax.ShapeDtypeStruct((rows, width), dtype)] * half,
        in_specs=[VMEM] * (1 + len(blocks)),
        out_specs=[VMEM] * half,
        scratch_shapes=[pltpu.VMEM((rows * len(blocks), width), BF16)],
        compiler_params=params(),
        name="forward_partial",
    )(panel, *blocks)


def split_bias(value):
    high = value.astype(BF16)
    low = (value - high.astype(F32)).astype(BF16)
    return high, low


def bias_rows(value):
    high, low = split_bias(value)
    row = lax.broadcasted_iota(jnp.int32, (BIAS_ROWS, value.shape[1]), 0)
    high, low = high.astype(F32), low.astype(F32)
    return jnp.where(row == 0, high, jnp.where(row == 1, low, 0.0)).astype(BF16)


def bias_value(rows):
    return jnp.sum(rows.astype(F32), axis=0, keepdims=True)


def split_rows(bit, whole, bias_part, keep_ref, send_ref):
    half = whole.shape[0] // 2
    mine = jnp.where(jnp.bitwise_and(lax.axis_index("row"), bit) != 0, half, 0)
    keep_ref[:half, :] = whole[pl.ds(pl.multiple_of(mine, half), half), :]
    send_ref[:half, :] = whole[pl.ds(pl.multiple_of(half - mine, half), half), :]
    keep_ref[half:, :] = bias_part
    send_ref[half:, :] = bias_part


def dense_kernel(count, weight_ref, bias_ref, grad_ref, *refs):
    parts, outs = refs[:count], refs[count:]
    hidden_ref, agg_grad_ref, keep_ref, send_ref, weights = outs
    total = parts[0][...].astype(F32)
    for part in parts[1:]:
        total = total + part[...].astype(F32)
    aggregated = total.astype(BF16)
    weight = weight_ref[...]
    pre = jnp.dot(aggregated, weight, preferred_element_type=F32) + bias_ref[...]
    gate = jax.nn.sigmoid(pre)
    hidden_ref[...] = (pre * gate).astype(BF16)
    pre_grad = (grad_ref[...].astype(F32) * (gate * (1.0 + pre * (1.0 - gate)))).astype(BF16)
    agg_grad = lax.dot_general(
        pre_grad, weight, (((1,), (1,)), ((), ())), preferred_element_type=F32
    ).astype(BF16)
    agg_grad_ref[...] = agg_grad
    weights[...] = lax.dot_general(
        aggregated, pre_grad, (((0,), (0,)), ((), ())), preferred_element_type=F32
    ).astype(BF16)
    bias_part = bias_rows(jnp.sum(pre_grad.astype(F32), axis=0, keepdims=True))

    split_rows(1, weights, bias_part, keep_ref, send_ref)


def dense(weight, bias_vector, out_grad, parts):
    width = out_grad.shape[1]
    extra = width // 2 + BIAS_ROWS
    return pl.pallas_call(
        functools.partial(dense_kernel, len(parts)),
        out_shape=[jax.ShapeDtypeStruct(out_grad.shape, BF16)] * 2
        + [jax.ShapeDtypeStruct((extra, width), BF16)] * 2,
        in_specs=[VMEM] * (3 + len(parts)),
        out_specs=[VMEM] * 4,
        scratch_shapes=[pltpu.VMEM(weight.shape, BF16)],
        compiler_params=params(),
        name="dense_stage",
    )(weight, bias_vector, out_grad, *parts)


def tree_sum(values):
    while len(values) > 1:
        values = [values[k] + values[k + 1] for k in range(0, len(values), 2)]
    return values[0]


def gradient_sums(refs, start):
    weight = tree_sum([ref[start(ref):ref.shape[0] - BIAS_ROWS, :].astype(F32) for ref in refs])
    bias = tree_sum([bias_value(ref[ref.shape[0] - BIAS_ROWS:, :]) for ref in refs])
    return weight, bias


def relay_kernel(agg_grad_ref, left_ref, right_ref, *refs):
    shares, out_ref = [left_ref, right_ref], refs[-1]
    rows = agg_grad_ref.shape[0]
    weight, bias = gradient_sums(shares, lambda ref: 0)
    out_ref[:rows, :] = agg_grad_ref[...]
    out_ref[rows:-BIAS_ROWS, :] = weight.astype(BF16)
    out_ref[-BIAS_ROWS:, :] = bias_rows(bias)


def relay(agg_grad, shares, after):
    size = agg_grad.shape[0] + shares[0].shape[0]
    return pl.pallas_call(
        relay_kernel,
        out_shape=jax.ShapeDtypeStruct((size, agg_grad.shape[1]), BF16),
        in_specs=[VMEM] * 3 + [ANY] * len(after),
        out_specs=VMEM,
        compiler_params=params(),
        name="relay_message",
    )(agg_grad, *shares, *after)


def split_kernel(bit, left_ref, right_ref, keep_ref, send_ref, whole):
    weight, bias = gradient_sums([left_ref, right_ref], lambda ref: 0)
    whole[...] = weight.astype(BF16)
    split_rows(bit, whole, bias_rows(bias), keep_ref, send_ref)


def split_sum(bit, left, right):
    rows, width = left.shape[0] - BIAS_ROWS, left.shape[1]
    return pl.pallas_call(
        functools.partial(split_kernel, bit),
        out_shape=[jax.ShapeDtypeStruct((rows // 2 + BIAS_ROWS, width), BF16)] * 2,
        in_specs=[VMEM, VMEM],
        out_specs=[VMEM, VMEM],
        scratch_shapes=[pltpu.VMEM((rows, width), BF16)],
        compiler_params=params(),
        name="split_sum",
    )(left, right)


def pair_kernel(extra, left_ref, right_ref, out_ref):
    weight, bias = gradient_sums([left_ref, right_ref], lambda ref: ref.shape[0] - extra)
    out_ref[:-BIAS_ROWS, :] = weight.astype(BF16)
    out_ref[-BIAS_ROWS:, :] = bias_rows(bias)


def pair_sum(extra, left, right):
    return pl.pallas_call(
        functools.partial(pair_kernel, extra),
        out_shape=jax.ShapeDtypeStruct((extra, left.shape[1]), BF16),
        in_specs=[VMEM, VMEM],
        out_specs=VMEM,
        compiler_params=params(),
        name="pair_sum",
    )(left, right)


def totals_kernel(scale, *refs):
    shares, (weight_ref, bias_ref) = refs[:-2], refs[-2:]
    weight, bias = gradient_sums(shares, lambda ref: 0)
    weight_ref[...] = (weight * scale).astype(BF16)
    bias_ref[...] = bias * scale


def totals(shares, scale):
    extra, width = shares[0].shape
    return pl.pallas_call(
        functools.partial(totals_kernel, scale),
        out_shape=[
            jax.ShapeDtypeStruct((extra - BIAS_ROWS, width), BF16),
            jax.ShapeDtypeStruct((1, width), F32),
        ],
        in_specs=[VMEM] * len(shares),
        out_specs=[VMEM] * 2,
        compiler_params=params(),
        name="gradient_totals",
    )(*shares)


def halve_kernel(keep_ref, arrived_ref, rest_ref, send_ref):
    half = rest_ref.shape[0]
    rest_ref[...] = keep_ref[:half, :] + arrived_ref[:half, :].astype(F32)
    send_ref[...] = (keep_ref[half:, :] + arrived_ref[half:, :].astype(F32)).astype(BF16)


def halve(keep, arrived):
    shape = (keep.shape[0] // 2, keep.shape[1])
    return pl.pallas_call(
        halve_kernel,
        out_shape=[jax.ShapeDtypeStruct(shape, F32), jax.ShapeDtypeStruct(shape, BF16)],
        in_specs=[VMEM, VMEM],
        out_specs=[VMEM, VMEM],
        compiler_params=params(),
        name="halve_terms",
    )(keep, arrived)


def feature_kernel(own_ref, arrived_ref, out_ref, token_ref):
    token_ref[...] = jnp.zeros_like(token_ref)
    out_ref[...] = (own_ref[...] + arrived_ref[...].astype(F32)).astype(BF16)


def feature_sum(own, arrived):
    return pl.pallas_call(
        feature_kernel,
        out_shape=[jax.ShapeDtypeStruct(own.shape, BF16), jax.ShapeDtypeStruct((8, 128), F32)],
        in_specs=[VMEM, VMEM],
        out_specs=[VMEM, VMEM],
        compiler_params=params(),
        name="feature_sum",
    )(own, arrived)


def assemble_kernel(after_ref, *refs):
    sections, out_ref = refs[:-1], refs[-1]
    chunk, count = sections[0].shape[0], len(sections)
    for d, ref in enumerate(sections):
        device, start, bit = jnp.bitwise_xor(lax.axis_index("row"), d), 0, 1
        while bit < count:
            start += jnp.where(jnp.bitwise_and(device, bit) != 0, chunk * count // (2 * bit), 0)
            bit *= 2
        out_ref[pl.ds(pl.multiple_of(start, chunk), chunk), :] = ref[...].astype(F32)


def assemble(after, sections):
    chunk, width = sections[0].shape
    return pl.pallas_call(
        assemble_kernel,
        out_shape=jax.ShapeDtypeStruct((chunk * len(sections), width), F32),
        in_specs=[ANY] + [VMEM] * len(sections),
        out_specs=VMEM,
        compiler_params=params(),
        name="assemble_weight_grad",
    )(after, *sections)


def backward_kernel(count, flip, panel_ref, *refs):
    blocks, (out_ref, gathered) = refs[:count], (refs[-2], refs[-1])
    rows = gathered.shape[0] // count
    row_me, col_me = lax.axis_index("row"), lax.axis_index("col")
    for d in range(count):
        source = jnp.bitwise_xor(col_me, d)
        gathered[pl.ds(pl.multiple_of(source * rows, rows), rows), :] = blocks[d][:rows, :]
    for k in range(out_ref.shape[0] // rows):
        target = jnp.bitwise_xor(row_me, 2 * k + flip)
        part = panel_ref[:, pl.ds(pl.multiple_of(target * rows, rows), rows)]
        value = lax.dot_general(part, gathered[...], (((0,), (0,)), ((), ())), preferred_element_type=F32)
        out_ref[k * rows:(k + 1) * rows, :] = value.astype(out_ref.dtype)


def backward(panel, blocks, after, half, flip, dtype):
    rows, width = blocks[0].shape
    return pl.pallas_call(
        functools.partial(backward_kernel, len(blocks), flip),
        out_shape=jax.ShapeDtypeStruct((rows * half, width), dtype),
        in_specs=[VMEM] * (1 + len(blocks)) + [ANY] * len(after),
        out_specs=VMEM,
        scratch_shapes=[pltpu.VMEM((rows * len(blocks), width), BF16)],
        compiler_params=params(),
        name="backward_terms",
    )(panel, *blocks, *after)


def body(features, weight, bias_vector, out_grad, adj_tiles, tile_pos, tile_count):
    rows_dev, width = features.shape
    tile_size = adj_tiles.shape[-1]
    row_count = lax.axis_size("row")
    col_count = lax.axis_size("col")
    row_tiles = col_count * rows_dev // tile_size
    col_tiles = row_count * rows_dev // tile_size

    blocks = [features] + [swapped(features, "row", d) for d in range(1, row_count)]
    panel = build_panel(tile_pos[0], tile_count, adj_tiles[0, 0], row_tiles, col_tiles)
    sends = forward(panel, blocks, col_count // 2, 1, BF16)
    keeps = forward(panel, blocks, col_count // 2, 0, F32)
    parts = []
    for d, keep, send in zip(peers(col_count), keeps, sends):
        arrived = swapped(send, "col", 1)
        if d:
            pair = (keep + arrived.astype(F32)).astype(BF16)
            parts.append(swapped(pair, "col", d))
        else:
            parts += [keep, arrived]
    order = peers(col_count)[:-1]
    hidden_out, agg_grad, share, send = dense(
        weight, bias_vector.reshape(1, width), out_grad, parts
    )
    arrived = swapped(send, "row", 1)
    grads = {0: agg_grad}
    for d in order:
        grads[d] = swapped(agg_grad, "col", d)
    bit = 2
    while bit < row_count:
        share, send = split_sum(bit, share, arrived)
        arrived = swapped(send, "row", bit)
        bit *= 2
    extra = share.shape[0]
    sent = relay(agg_grad, [share, arrived], [grads[d] for d in order[:-1]])
    grads[1] = swapped(sent, "col", 1)
    for d in order:
        grads[d + 1] = swapped(grads[d], "col", 1)
    blocks = [grads[d] for d in range(col_count)]
    share = pair_sum(extra, sent, grads[1])
    shares = {d: swapped(share, "col", d) for d in order}
    shares = [share] + [shares[d] for d in range(2, col_count, 2)]

    send = backward(panel, blocks, shares[1:], row_count // 2, 1, BF16)
    keep = backward(panel, blocks, [], row_count // 2, 0, F32)
    terms = swapped(send, "row", 1)
    bit = row_count // 2
    while bit > 1:
        keep, send = halve(keep, terms)
        terms = swapped(send, "row", bit)
        bit //= 2
    feature_grad, token = feature_sum(keep, terms)
    scale = 1.0 / math.sqrt(row_count * col_count * rows_dev)
    section, bias_grad = totals(shares, scale)
    sections = [section] + [swapped(section, "row", d) for d in range(1, row_count)]
    weight_grad = assemble(token, sections)
    return (hidden_out, feature_grad, weight_grad, bias_grad.reshape(width))


def solution(mesh):
    in_specs = (
        P(("row", "col"), None),
        P(),
        P(),
        P(("row", "col"), None),
        P("row", "col", None, None, None),
        P("row", "col", None),
        P("row", "col"),
    )
    out_specs = (P(("row", "col"), None), P(("row", "col"), None), P(), P())
    return jax.shard_map(body, mesh=mesh, in_specs=in_specs, out_specs=out_specs, check_vma=False)
```

time: 62.4 us -> 55.3 us (0.89)
  waiting for transfers between devices: 23.4 us -> 15 us
  starting transfers between devices: 28.9 us -> 31.5 us
  Pallas kernels: 8.45 us -> 6.54 us
    ppermute x23 -> x27, waiting for transfers between devices: 23.4 us -> 15 us  [swapped(): return lax.ppermute(block, axis, [(i, i ^ bit) for i in range(n)])]
    ppermute x23 -> x27, starting transfers between devices: 28.9 us -> 31.5 us  [swapped(): return lax.ppermute(block, axis, [(i, i ^ bit) for i in range(n)])]
    pallas_call x4 -> x9, Pallas kernels: 2.78 us -> 2.18 us  [the longest x2 0.77 us: backward(): pl.pallas_call(functools.partial(backward_kernel, len(blocks), flip), out...]
  transfers between devices with their start and end apart: 23 -> 27, of which waited for: 12 -> 14; matrix products, arithmetic and copies ran while one was open for 0% -> 0% of each run, Pallas kernels for 5% -> 8%
where the time goes in v2:
time: 55.3 us; the launch traced here: 55.2 us
  starting transfers between devices  31.5 us (57%)
  waiting for transfers between devices  15 us (27%)
  Pallas kernels  6.54 us (12%)
  between operations  1.41 us (3%)
  local copies, waits for them, and re-layouts  0.66 us (1%)
    ppermute x27, starting transfers between devices, swapped(): return lax.ppermute(block, axis, [(i, i ^ bit) for i in range(n)])  31.5 us
    ppermute x27, waiting for transfers between devices, swapped(): return lax.ppermute(block, axis, [(i, i ^ bit) for i in range(n)])  15 us
    pallas_call x1, Pallas kernels, build_panel(): pl.pallas_call(functools.partial(build_kernel, col_tiles), out_shape=jax....  2.21 us
  transfers between devices with their start and end apart: 27, of which 14 were waited for; matrix products, arithmetic and copies ran while one was open for 0% of the time, Pallas kernels for 8%

profile of v2, /device:TPU:0, one launch (start us, length us, event | category | flops | bytes accessed | tf_op | source)
XLA Modules:
  0.0 55.2 jit_solution(16656011029221938053)
XLA Ops:
  0.6 2.4 %collective-permute-start.2 = (bf16[128,256]{1,0:T(8,128)(2,1)}, bf16[128,256]{1,0:T(8,128)(2,1)S(1)}, u32[]{:S(2)}, u32[]{:S(2)}) collective-permute-start(bf16[128,256]{1,0:T(8,128)(2,1)} %refs_0_.3), channel_id=1, source_target_pairs={{0,24},{8,16},{16,8},{24,0},{1,25},{9,17},{17,9},{25,1},{2,26},{10... | collective-permute-start | bytes 196616 | tf_op jit(solution)/shard_map/ppermute | solution.py:22
  5.1 2.2 %build_panel.1.panel_ref = bf16[1024,512]{1,0:T(8,128)(2,1)S(1)} custom-call(s32[1,96]{1,0:T(1,128)S(1)} %bitcast.5, s32[1,1]{1,0:T(1,128)S(6)} %copy.11.count_ref, bf16[96,128,128]{2,1,0:T(8,128)(2,1)} %bitcast.6), custom_call_target="tpu_custom_call" | custom-call | flops 1572864 | bytes 3145728 | tf_op jit(solution)/shard_map/build_panel/pallas_call | solution.py:62
  8.3 1.8 %collective-permute-start.5 = (bf16[128,256]{1,0:T(8,128)(2,1)S(1)}, bf16[128,256]{1,0:T(8,128)(2,1)S(1)}, u32[]{:S(2)}, u32[]{:S(2)}) collective-permute-start(bf16[128,256]{1,0:T(8,128)(2,1)S(1)} %get-tuple-element.27), channel_id=1, source_target_pairs={{0,1},{1,0},{2,3},{3,2},{4,5},{5,4},{6,7},{7,6},{8,9},{9,8},{10,11... | collective-permute-start | bytes 196616 | tf_op jit(solution)/shard_map/ppermute | solution.py:22
  10.4 1.7 %collective-permute-start.7 = (bf16[128,256]{1,0:T(8,128)(2,1)S(1)}, bf16[128,256]{1,0:T(8,128)(2,1)S(1)}, u32[]{:S(2)}, u32[]{:S(2)}) collective-permute-start(bf16[128,256]{1,0:T(8,128)(2,1)S(1)} %get-tuple-element.29), channel_id=1, source_target_pairs={{0,1},{1,0},{2,3},{3,2},{4,5},{5,4},{6,7},{7,6},{8,9},{9,8},{10,11... | collective-permute-start | bytes 196616 | tf_op jit(solution)/shard_map/ppermute | solution.py:22
  13.0 4.0 %collective-permute-start.6 = (bf16[128,256]{1,0:T(8,128)(2,1)S(1)}, bf16[128,256]{1,0:T(8,128)(2,1)S(1)}, u32[]{:S(2)}, u32[]{:S(2)}) collective-permute-start(bf16[128,256]{1,0:T(8,128)(2,1)S(1)} %add_convert_fusion.1), channel_id=1, source_target_pairs={{0,6},{1,7},{2,4},{3,5},{4,2},{5,3},{6,0},{7,1},{8,14},{9,15},{10,... | collective-permute-start | bytes 196616 | tf_op jit(solution)/shard_map/ppermute | solution.py:22
  17.8 1.6 %collective-permute-start.8 = (bf16[128,256]{1,0:T(8,128)(2,1)S(1)}, bf16[128,256]{1,0:T(8,128)(2,1)S(1)}, u32[]{:S(2)}, u32[]{:S(2)}) collective-permute-start(bf16[128,256]{1,0:T(8,128)(2,1)S(1)} %add_convert_fusion), channel_id=1, source_target_pairs={{0,2},{1,3},{2,0},{3,1},{4,6},{5,7},{6,4},{7,5},{8,10},{9,11},{10,... | collective-permute-start | bytes 196616 | tf_op jit(solution)/shard_map/ppermute | solution.py:22
  19.6 2.7 %collective-permute-done.4.refs_0_ = bf16[128,256]{1,0:T(8,128)(2,1)S(1)} collective-permute-done((bf16[128,256]{1,0:T(8,128)(2,1)S(1)}, bf16[128,256]{1,0:T(8,128)(2,1)S(1)}, u32[]{:S(2)}, u32[]{:S(2)}) %collective-permute-start.4) | collective-permute-done | bytes 65568 | tf_op jit(solution)/shard_map/ppermute | solution.py:22
  22.9 0.8 %dense_stage.1 = (bf16[128,256]{1,0:T(8,128)(2,1)}, bf16[128,256]{1,0:T(8,128)(2,1)S(1)}, bf16[144,256]{1,0:T(8,128)(2,1)S(1)}, bf16[144,256]{1,0:T(8,128)(2,1)S(1)}) custom-call(bf16[256,256]{1,0:T(8,128)(2,1)S(1)} %copy-done.1, f32[1,256]{1,0:T(1,128)S(1)} %bitcast.4, bf16[128,256]{1,0:T(8,128)(2,1)S(1)} %copy-done.2, ...), custom_call_target="tpu_custom_call" | custom-call | tf_op jit(solution)/shard_map/dense_stage/pallas_call | solution.py:165
  23.7 2.2 %collective-permute-start.13 = (bf16[128,256]{1,0:T(8,128)(2,1)S(1)}, bf16[128,256]{1,0:T(8,128)(2,1)S(1)}, u32[]{:S(2)}, u32[]{:S(2)}) collective-permute-start(bf16[128,256]{1,0:T(8,128)(2,1)S(1)} %get-tuple-element.33.agg_grad_ref.refs_0_), channel_id=1, source_target_pairs={{0,6},{1,7},{2,4},{3,5},{4,2},{5,3},{6,0},{7,1},{8,14},{9,15},{10,... | collective-permute-start | bytes 196616 | tf_op jit(solution)/shard_map/ppermute | solution.py:22
  26.1 1.6 %collective-permute-start.11 = (bf16[80,256]{1,0:T(8,128)(2,1)S(1)}, bf16[80,256]{1,0:T(8,128)(2,1)S(1)}, u32[]{:S(2)}, u32[]{:S(2)}) collective-permute-start(bf16[80,256]{1,0:T(8,128)(2,1)S(1)} %get-tuple-element.37), channel_id=1, source_target_pairs={{0,16},{8,24},{16,0},{24,8},{1,17},{9,25},{17,1},{25,9},{2,18},{10... | collective-permute-start | bytes 122888 | tf_op jit(solution)/shard_map/ppermute | solution.py:22
  27.6 2.0 %collective-permute-start.15 = (bf16[128,256]{1,0:T(8,128)(2,1)S(1)}, bf16[128,256]{1,0:T(8,128)(2,1)S(1)}, u32[]{:S(2)}, u32[]{:S(2)}) collective-permute-start(bf16[128,256]{1,0:T(8,128)(2,1)S(1)} %get-tuple-element.33.agg_grad_ref.refs_0_), channel_id=1, source_target_pairs={{0,2},{1,3},{2,0},{3,1},{4,6},{5,7},{6,4},{7,5},{8,10},{9,11},{10,... | collective-permute-start | bytes 196616 | tf_op jit(solution)/shard_map/ppermute | solution.py:22
  29.6 0.8 %collective-permute-done.13.refs_1_.refs_6_ = bf16[128,256]{1,0:T(8,128)(2,1)S(1)} collective-permute-done((bf16[128,256]{1,0:T(8,128)(2,1)S(1)}, bf16[128,256]{1,0:T(8,128)(2,1)S(1)}, u32[]{:S(2)}, u32[]{:S(2)}) %collective-permute-start.13) | collective-permute-done | bytes 65568 | tf_op jit(solution)/shard_map/ppermute | solution.py:22
  30.5 2.4 %collective-permute-done.12.refs_0_.refs_4_ = bf16[128,256]{1,0:T(8,128)(2,1)S(1)} collective-permute-done((bf16[128,256]{1,0:T(8,128)(2,1)S(1)}, bf16[128,256]{1,0:T(8,128)(2,1)S(1)}, u32[]{:S(2)}, u32[]{:S(2)}) %collective-permute-start.12) | collective-permute-done | bytes 65568 | tf_op jit(solution)/shard_map/ppermute | solution.py:22
  33.0 1.4 %collective-permute-start.14 = (bf16[208,256]{1,0:T(8,128)(2,1)S(1)}, bf16[208,256]{1,0:T(8,128)(2,1)S(1)}, u32[]{:S(2)}, u32[]{:S(2)}) collective-permute-start(bf16[208,256]{1,0:T(8,128)(2,1)S(1)} %relay_message.1.left_ref), channel_id=1, source_target_pairs={{0,1},{1,0},{2,3},{3,2},{4,5},{5,4},{6,7},{7,6},{8,9},{9,8},{10,11... | collective-permute-start | bytes 319496 | tf_op jit(solution)/shard_map/ppermute | solution.py:22
  35.1 1.3 %collective-permute-start.18 = (bf16[128,256]{1,0:T(8,128)(2,1)S(1)}, bf16[128,256]{1,0:T(8,128)(2,1)S(1)}, u32[]{:S(2)}, u32[]{:S(2)}) collective-permute-start(bf16[128,256]{1,0:T(8,128)(2,1)S(1)} %collective-permute-done.13.refs_1_.refs_6_), channel_id=1, source_target_pairs={{0,1},{1,0},{2,3},{3,2},{4,5},{5,4},{6,7},{7,6},{8,9},{9,8},{10,11... | collective-permute-start | bytes 196616 | tf_op jit(solution)/shard_map/ppermute | solution.py:22
  37.1 1.8 %collective-permute-done.14.refs_1_.right_ref = bf16[208,256]{1,0:T(8,128)(2,1)S(1)} collective-permute-done((bf16[208,256]{1,0:T(8,128)(2,1)S(1)}, bf16[208,256]{1,0:T(8,128)(2,1)S(1)}, u32[]{:S(2)}, u32[]{:S(2)}) %collective-permute-start.14) | collective-permute-done | bytes 106528 | tf_op jit(solution)/shard_map/ppermute | solution.py:22
  38.9 2.3 %collective-permute-start.21 = (bf16[80,256]{1,0:T(8,128)(2,1)S(1)}, bf16[80,256]{1,0:T(8,128)(2,1)S(1)}, u32[]{:S(2)}, u32[]{:S(2)}) collective-permute-start(bf16[80,256]{1,0:T(8,128)(2,1)S(1)} %pair_sum.1.refs_0_), channel_id=1, source_target_pairs={{0,6},{1,7},{2,4},{3,5},{4,2},{5,3},{6,0},{7,1},{8,14},{9,15},{10,... | collective-permute-start | bytes 122888 | tf_op jit(solution)/shard_map/ppermute | solution.py:22
  41.2 2.2 %collective-permute-start.19 = (bf16[80,256]{1,0:T(8,128)(2,1)S(1)}, bf16[80,256]{1,0:T(8,128)(2,1)S(1)}, u32[]{:S(2)}, u32[]{:S(2)}) collective-permute-start(bf16[80,256]{1,0:T(8,128)(2,1)S(1)} %pair_sum.1.refs_0_), channel_id=1, source_target_pairs={{0,2},{1,3},{2,0},{3,1},{4,6},{5,7},{6,4},{7,5},{8,10},{9,11},{10,... | collective-permute-start | bytes 122888 | tf_op jit(solution)/shard_map/ppermute | solution.py:22
  43.4 1.4 %collective-permute-done.21.refs_10_.refs_3_ = bf16[80,256]{1,0:T(8,128)(2,1)S(1)} collective-permute-done((bf16[80,256]{1,0:T(8,128)(2,1)S(1)}, bf16[80,256]{1,0:T(8,128)(2,1)S(1)}, u32[]{:S(2)}, u32[]{:S(2)}) %collective-permute-start.21) | collective-permute-done | bytes 40992 | tf_op jit(solution)/shard_map/ppermute | solution.py:22
  44.8 1.3 %collective-permute-done.20.refs_9_.refs_2_ = bf16[80,256]{1,0:T(8,128)(2,1)S(1)} collective-permute-done((bf16[80,256]{1,0:T(8,128)(2,1)S(1)}, bf16[80,256]{1,0:T(8,128)(2,1)S(1)}, u32[]{:S(2)}, u32[]{:S(2)}) %collective-permute-start.20) | collective-permute-done | bytes 40992 | tf_op jit(solution)/shard_map/ppermute | solution.py:22
  46.9 0.9 %collective-permute-done.22.arrived_ref = bf16[256,256]{1,0:T(8,128)(2,1)S(1)} collective-permute-done((bf16[256,256]{1,0:T(8,128)(2,1)S(1)}, bf16[256,256]{1,0:T(8,128)(2,1)S(1)}, u32[]{:S(2)}, u32[]{:S(2)}) %collective-permute-start.22) | collective-permute-done | bytes 131104 | tf_op jit(solution)/shard_map/ppermute | solution.py:22
  47.9 1.6 %collective-permute-start.23 = (bf16[128,256]{1,0:T(8,128)(2,1)S(1)}, bf16[128,256]{1,0:T(8,128)(2,1)S(1)}, u32[]{:S(2)}, u32[]{:S(2)}) collective-permute-start(bf16[128,256]{1,0:T(8,128)(2,1)S(1)} %get-tuple-element.39), channel_id=1, source_target_pairs={{0,16},{8,24},{16,0},{24,8},{1,17},{9,25},{17,1},{25,9},{2,18},{10... | collective-permute-start | bytes 196616 | tf_op jit(solution)/shard_map/ppermute | solution.py:22
  50.0 1.5 %collective-permute-start.25 = (bf16[64,256]{1,0:T(8,128)(2,1)S(1)}, bf16[64,256]{1,0:T(8,128)(2,1)S(1)}, u32[]{:S(2)}, u32[]{:S(2)}) collective-permute-start(bf16[64,256]{1,0:T(8,128)(2,1)S(1)} %get-tuple-element.42.refs_0_), channel_id=1, source_target_pairs={{0,16},{8,24},{16,0},{24,8},{1,17},{9,25},{17,1},{25,9},{2,18},{10... | collective-permute-start | bytes 98312 | tf_op jit(solution)/shard_map/ppermute | solution.py:22
  52.9 0.8 %collective-permute-done.26.refs_3_ = bf16[64,256]{1,0:T(8,128)(2,1)S(1)} collective-permute-done((bf16[64,256]{1,0:T(8,128)(2,1)S(1)}, bf16[64,256]{1,0:T(8,128)(2,1)S(1)}, u32[]{:S(2)}, u32[]{:S(2)}) %collective-permute-start.26) | collective-permute-done | bytes 32800 | tf_op jit(solution)/shard_map/ppermute | solution.py:22
  (56 shorter events, 10.9 us)
Async XLA Ops:
  0.6 6.7 %collective-permute-start.2 = (bf16[128,256]{1,0:T(8,128)(2,1)}, bf16[128,256]{1,0:T(8,128)(2,1)S(1)}, u32[]{:S(2)}, u32[]{:S(2)}) collective-permute-start(bf16[128,256]{1,0:T(8,128)(2,1)} %refs_0_.3), channel_id=1, source_target_pairs={{0,24},{8,16},{16,8},{24,0},{1,25},{9,17},{17,9},{25,1},{2,26},{10... | collective-permute-start | bytes 196616 | tf_op jit(solution)/shard_map/ppermute | solution.py:22
  3.1 4.9 %collective-permute-start.1 = (bf16[128,256]{1,0:T(8,128)(2,1)}, bf16[128,256]{1,0:T(8,128)(2,1)S(1)}, u32[]{:S(2)}, u32[]{:S(2)}) collective-permute-start(bf16[128,256]{1,0:T(8,128)(2,1)} %refs_0_.3), channel_id=1, source_target_pairs={{0,16},{8,24},{16,0},{24,8},{1,17},{9,25},{17,1},{25,9},{2,18},{10... | collective-permute-start | bytes 196616 | tf_op jit(solution)/shard_map/ppermute | solution.py:22
  3.7 4.2 %collective-permute-start = (bf16[128,256]{1,0:T(8,128)(2,1)}, bf16[128,256]{1,0:T(8,128)(2,1)S(1)}, u32[]{:S(2)}, u32[]{:S(2)}) collective-permute-start(bf16[128,256]{1,0:T(8,128)(2,1)} %refs_0_.3), channel_id=1, source_target_pairs={{0,8},{8,0},{16,24},{24,16},{1,9},{9,1},{17,25},{25,17},{2,10},{10... | collective-permute-start | bytes 196616 | tf_op jit(solution)/shard_map/ppermute | solution.py:22
  8.3 4.7 %collective-permute-start.5 = (bf16[128,256]{1,0:T(8,128)(2,1)S(1)}, bf16[128,256]{1,0:T(8,128)(2,1)S(1)}, u32[]{:S(2)}, u32[]{:S(2)}) collective-permute-start(bf16[128,256]{1,0:T(8,128)(2,1)S(1)} %get-tuple-element.27), channel_id=1, source_target_pairs={{0,1},{1,0},{2,3},{3,2},{4,5},{5,4},{6,7},{7,6},{8,9},{9,8},{10,11... | collective-permute-start | bytes 196616 | tf_op jit(solution)/shard_map/ppermute | solution.py:22
  10.1 6.9 %collective-permute-start.3 = (bf16[128,256]{1,0:T(8,128)(2,1)S(1)}, bf16[128,256]{1,0:T(8,128)(2,1)S(1)}, u32[]{:S(2)}, u32[]{:S(2)}) collective-permute-start(bf16[128,256]{1,0:T(8,128)(2,1)S(1)} %get-tuple-element.25), channel_id=1, source_target_pairs={{0,1},{1,0},{2,3},{3,2},{4,5},{5,4},{6,7},{7,6},{8,9},{9,8},{10,11... | collective-permute-start | bytes 196616 | tf_op jit(solution)/shard_map/ppermute | solution.py:22
  10.4 7.4 %collective-permute-start.7 = (bf16[128,256]{1,0:T(8,128)(2,1)S(1)}, bf16[128,256]{1,0:T(8,128)(2,1)S(1)}, u32[]{:S(2)}, u32[]{:S(2)}) collective-permute-start(bf16[128,256]{1,0:T(8,128)(2,1)S(1)} %get-tuple-element.29), channel_id=1, source_target_pairs={{0,1},{1,0},{2,3},{3,2},{4,5},{5,4},{6,7},{7,6},{8,9},{9,8},{10,11... | collective-permute-start | bytes 196616 | tf_op jit(solution)/shard_map/ppermute | solution.py:22
  12.1 7.3 %collective-permute-start.9 = (bf16[128,256]{1,0:T(8,128)(2,1)S(1)}, bf16[128,256]{1,0:T(8,128)(2,1)S(1)}, u32[]{:S(2)}, u32[]{:S(2)}) collective-permute-start(bf16[128,256]{1,0:T(8,128)(2,1)S(1)} %get-tuple-element.31), channel_id=1, source_target_pairs={{0,1},{1,0},{2,3},{3,2},{4,5},{5,4},{6,7},{7,6},{8,9},{9,8},{10,11... | collective-permute-start | bytes 196616 | tf_op jit(solution)/shard_map/ppermute | solution.py:22
  13.0 6.5 %collective-permute-start.6 = (bf16[128,256]{1,0:T(8,128)(2,1)S(1)}, bf16[128,256]{1,0:T(8,128)(2,1)S(1)}, u32[]{:S(2)}, u32[]{:S(2)}) collective-permute-start(bf16[128,256]{1,0:T(8,128)(2,1)S(1)} %add_convert_fusion.1), channel_id=1, source_target_pairs={{0,6},{1,7},{2,4},{3,5},{4,2},{5,3},{6,0},{7,1},{8,14},{9,15},{10,... | collective-permute-start | bytes 196616 | tf_op jit(solution)/shard_map/ppermute | solution.py:22
  17.0 5.3 %collective-permute-start.4 = (bf16[128,256]{1,0:T(8,128)(2,1)S(1)}, bf16[128,256]{1,0:T(8,128)(2,1)S(1)}, u32[]{:S(2)}, u32[]{:S(2)}) collective-permute-start(bf16[128,256]{1,0:T(8,128)(2,1)S(1)} %add_convert_fusion.2), channel_id=1, source_target_pairs={{0,4},{1,5},{2,6},{3,7},{4,0},{5,1},{6,2},{7,3},{8,12},{9,13},{10,... | collective-permute-start | bytes 196616 | tf_op jit(solution)/shard_map/ppermute | solution.py:22
  17.8 5.1 %collective-permute-start.8 = (bf16[128,256]{1,0:T(8,128)(2,1)S(1)}, bf16[128,256]{1,0:T(8,128)(2,1)S(1)}, u32[]{:S(2)}, u32[]{:S(2)}) collective-permute-start(bf16[128,256]{1,0:T(8,128)(2,1)S(1)} %add_convert_fusion), channel_id=1, source_target_pairs={{0,2},{1,3},{2,0},{3,1},{4,6},{5,7},{6,4},{7,5},{8,10},{9,11},{10,... | collective-permute-start | bytes 196616 | tf_op jit(solution)/shard_map/ppermute | solution.py:22
  23.7 6.8 %collective-permute-start.13 = (bf16[128,256]{1,0:T(8,128)(2,1)S(1)}, bf16[128,256]{1,0:T(8,128)(2,1)S(1)}, u32[]{:S(2)}, u32[]{:S(2)}) collective-permute-start(bf16[128,256]{1,0:T(8,128)(2,1)S(1)} %get-tuple-element.33.agg_grad_ref.refs_0_), channel_id=1, source_target_pairs={{0,6},{1,7},{2,4},{3,5},{4,2},{5,3},{6,0},{7,1},{8,14},{9,15},{10,... | collective-permute-start | bytes 196616 | tf_op jit(solution)/shard_map/ppermute | solution.py:22
  25.9 7.0 %collective-permute-start.12 = (bf16[128,256]{1,0:T(8,128)(2,1)S(1)}, bf16[128,256]{1,0:T(8,128)(2,1)S(1)}, u32[]{:S(2)}, u32[]{:S(2)}) collective-permute-start(bf16[128,256]{1,0:T(8,128)(2,1)S(1)} %get-tuple-element.33.agg_grad_ref.refs_0_), channel_id=1, source_target_pairs={{0,4},{1,5},{2,6},{3,7},{4,0},{5,1},{6,2},{7,3},{8,12},{9,13},{10,... | collective-permute-start | bytes 196616 | tf_op jit(solution)/shard_map/ppermute | solution.py:22
  26.1 6.9 %collective-permute-start.11 = (bf16[80,256]{1,0:T(8,128)(2,1)S(1)}, bf16[80,256]{1,0:T(8,128)(2,1)S(1)}, u32[]{:S(2)}, u32[]{:S(2)}) collective-permute-start(bf16[80,256]{1,0:T(8,128)(2,1)S(1)} %get-tuple-element.37), channel_id=1, source_target_pairs={{0,16},{8,24},{16,0},{24,8},{1,17},{9,25},{17,1},{25,9},{2,18},{10... | collective-permute-start | bytes 122888 | tf_op jit(solution)/shard_map/ppermute | solution.py:22
  27.6 6.7 %collective-permute-start.15 = (bf16[128,256]{1,0:T(8,128)(2,1)S(1)}, bf16[128,256]{1,0:T(8,128)(2,1)S(1)}, u32[]{:S(2)}, u32[]{:S(2)}) collective-permute-start(bf16[128,256]{1,0:T(8,128)(2,1)S(1)} %get-tuple-element.33.agg_grad_ref.refs_0_), channel_id=1, source_target_pairs={{0,2},{1,3},{2,0},{3,1},{4,6},{5,7},{6,4},{7,5},{8,10},{9,11},{10,... | collective-permute-start | bytes 196616 | tf_op jit(solution)/shard_map/ppermute | solution.py:22
  33.0 5.9 %collective-permute-start.14 = (bf16[208,256]{1,0:T(8,128)(2,1)S(1)}, bf16[208,256]{1,0:T(8,128)(2,1)S(1)}, u32[]{:S(2)}, u32[]{:S(2)}) collective-permute-start(bf16[208,256]{1,0:T(8,128)(2,1)S(1)} %relay_message.1.left_ref), channel_id=1, source_target_pairs={{0,1},{1,0},{2,3},{3,2},{4,5},{5,4},{6,7},{7,6},{8,9},{9,8},{10,11... | collective-permute-start | bytes 319496 | tf_op jit(solution)/shard_map/ppermute | solution.py:22
  34.4 6.8 %collective-permute-start.16 = (bf16[128,256]{1,0:T(8,128)(2,1)S(1)}, bf16[128,256]{1,0:T(8,128)(2,1)S(1)}, u32[]{:S(2)}, u32[]{:S(2)}) collective-permute-start(bf16[128,256]{1,0:T(8,128)(2,1)S(1)} %collective-permute-done.15.refs_2_), channel_id=1, source_target_pairs={{0,1},{1,0},{2,3},{3,2},{4,5},{5,4},{6,7},{7,6},{8,9},{9,8},{10,11... | collective-permute-start | bytes 196616 | tf_op jit(solution)/shard_map/ppermute | solution.py:22
  35.1 8.3 %collective-permute-start.18 = (bf16[128,256]{1,0:T(8,128)(2,1)S(1)}, bf16[128,256]{1,0:T(8,128)(2,1)S(1)}, u32[]{:S(2)}, u32[]{:S(2)}) collective-permute-start(bf16[128,256]{1,0:T(8,128)(2,1)S(1)} %collective-permute-done.13.refs_1_.refs_6_), channel_id=1, source_target_pairs={{0,1},{1,0},{2,3},{3,2},{4,5},{5,4},{6,7},{7,6},{8,9},{9,8},{10,11... | collective-permute-start | bytes 196616 | tf_op jit(solution)/shard_map/ppermute | solution.py:22
  36.4 7.0 %collective-permute-start.17 = (bf16[128,256]{1,0:T(8,128)(2,1)S(1)}, bf16[128,256]{1,0:T(8,128)(2,1)S(1)}, u32[]{:S(2)}, u32[]{:S(2)}) collective-permute-start(bf16[128,256]{1,0:T(8,128)(2,1)S(1)} %collective-permute-done.12.refs_0_.refs_4_), channel_id=1, source_target_pairs={{0,1},{1,0},{2,3},{3,2},{4,5},{5,4},{6,7},{7,6},{8,9},{9,8},{10,11... | collective-permute-start | bytes 196616 | tf_op jit(solution)/shard_map/ppermute | solution.py:22
  38.9 5.9 %collective-permute-start.21 = (bf16[80,256]{1,0:T(8,128)(2,1)S(1)}, bf16[80,256]{1,0:T(8,128)(2,1)S(1)}, u32[]{:S(2)}, u32[]{:S(2)}) collective-permute-start(bf16[80,256]{1,0:T(8,128)(2,1)S(1)} %pair_sum.1.refs_0_), channel_id=1, source_target_pairs={{0,6},{1,7},{2,4},{3,5},{4,2},{5,3},{6,0},{7,1},{8,14},{9,15},{10,... | collective-permute-start | bytes 122888 | tf_op jit(solution)/shard_map/ppermute | solution.py:22
  41.2 4.9 %collective-permute-start.20 = (bf16[80,256]{1,0:T(8,128)(2,1)S(1)}, bf16[80,256]{1,0:T(8,128)(2,1)S(1)}, u32[]{:S(2)}, u32[]{:S(2)}) collective-permute-start(bf16[80,256]{1,0:T(8,128)(2,1)S(1)} %pair_sum.1.refs_0_), channel_id=1, source_target_pairs={{0,4},{1,5},{2,6},{3,7},{4,0},{5,1},{6,2},{7,3},{8,12},{9,13},{10,... | collective-permute-start | bytes 122888 | tf_op jit(solution)/shard_map/ppermute | solution.py:22
  41.2 4.9 %collective-permute-start.19 = (bf16[80,256]{1,0:T(8,128)(2,1)S(1)}, bf16[80,256]{1,0:T(8,128)(2,1)S(1)}, u32[]{:S(2)}, u32[]{:S(2)}) collective-permute-start(bf16[80,256]{1,0:T(8,128)(2,1)S(1)} %pair_sum.1.refs_0_), channel_id=1, source_target_pairs={{0,2},{1,3},{2,0},{3,1},{4,6},{5,7},{6,4},{7,5},{8,10},{9,11},{10,... | collective-permute-start | bytes 122888 | tf_op jit(solution)/shard_map/ppermute | solution.py:22
  47.9 4.3 %collective-permute-start.23 = (bf16[128,256]{1,0:T(8,128)(2,1)S(1)}, bf16[128,256]{1,0:T(8,128)(2,1)S(1)}, u32[]{:S(2)}, u32[]{:S(2)}) collective-permute-start(bf16[128,256]{1,0:T(8,128)(2,1)S(1)} %get-tuple-element.39), channel_id=1, source_target_pairs={{0,16},{8,24},{16,0},{24,8},{1,17},{9,25},{17,1},{25,9},{2,18},{10... | collective-permute-start | bytes 196616 | tf_op jit(solution)/shard_map/ppermute | solution.py:22
  50.0 3.6 %collective-permute-start.26 = (bf16[64,256]{1,0:T(8,128)(2,1)S(1)}, bf16[64,256]{1,0:T(8,128)(2,1)S(1)}, u32[]{:S(2)}, u32[]{:S(2)}) collective-permute-start(bf16[64,256]{1,0:T(8,128)(2,1)S(1)} %get-tuple-element.42.refs_0_), channel_id=1, source_target_pairs={{0,24},{8,16},{16,8},{24,0},{1,25},{9,17},{17,9},{25,1},{2,26},{10... | collective-permute-start | bytes 98312 | tf_op jit(solution)/shard_map/ppermute | solution.py:22
  50.0 4.4 %collective-permute-start.25 = (bf16[64,256]{1,0:T(8,128)(2,1)S(1)}, bf16[64,256]{1,0:T(8,128)(2,1)S(1)}, u32[]{:S(2)}, u32[]{:S(2)}) collective-permute-start(bf16[64,256]{1,0:T(8,128)(2,1)S(1)} %get-tuple-element.42.refs_0_), channel_id=1, source_target_pairs={{0,16},{8,24},{16,0},{24,8},{1,17},{9,25},{17,1},{25,9},{2,18},{10... | collective-permute-start | bytes 98312 | tf_op jit(solution)/shard_map/ppermute | solution.py:22
  (8 other events, 68.0 us)

commit v3 on v2

--- a/solution.py
+++ b/solution.py
@@ -186,27 +186,6 @@
     return weight, bias
 
 
-def relay_kernel(agg_grad_ref, left_ref, right_ref, *refs):
-    shares, out_ref = [left_ref, right_ref], refs[-1]
-    rows = agg_grad_ref.shape[0]
-    weight, bias = gradient_sums(shares, lambda ref: 0)
-    out_ref[:rows, :] = agg_grad_ref[...]
-    out_ref[rows:-BIAS_ROWS, :] = weight.astype(BF16)
-    out_ref[-BIAS_ROWS:, :] = bias_rows(bias)
-
-
-def relay(agg_grad, shares, after):
-    size = agg_grad.shape[0] + shares[0].shape[0]
-    return pl.pallas_call(
-        relay_kernel,
-        out_shape=jax.ShapeDtypeStruct((size, agg_grad.shape[1]), BF16),
-        in_specs=[VMEM] * 3 + [ANY] * len(after),
-        out_specs=VMEM,
-        compiler_params=params(),
-        name="relay_message",
-    )(agg_grad, *shares, *after)
-
-
 def split_kernel(bit, left_ref, right_ref, keep_ref, send_ref, whole):
     weight, bias = gradient_sums([left_ref, right_ref], lambda ref: 0)
     whole[...] = weight.astype(BF16)
@@ -226,127 +205,139 @@
     )(left, right)
 
 
-def pair_kernel(extra, left_ref, right_ref, out_ref):
-    weight, bias = gradient_sums([left_ref, right_ref], lambda ref: ref.shape[0] - extra)
+def sum_kernel(count, *refs):
+    weight, bias = gradient_sums(refs[:count], lambda ref: 0)
+    out_ref = refs[-1]
     out_ref[:-BIAS_ROWS, :] = weight.astype(BF16)
     out_ref[-BIAS_ROWS:, :] = bias_rows(bias)
 
 
-def pair_sum(extra, left, right):
-    return pl.pallas_call(
-        functools.partial(pair_kernel, extra),
-        out_shape=jax.ShapeDtypeStruct((extra, left.shape[1]), BF16),
-        in_specs=[VMEM, VMEM],
+def sum_shares(shares, after):
+    return pl.pallas_call(
+        functools.partial(sum_kernel, len(shares)),
+        out_shape=jax.ShapeDtypeStruct(shares[0].shape, BF16),
+        in_specs=[VMEM] * len(shares) + [ANY] * len(after),
         out_specs=VMEM,
         compiler_params=params(),
-        name="pair_sum",
-    )(left, right)
-
-
-def totals_kernel(scale, *refs):
-    shares, (weight_ref, bias_ref) = refs[:-2], refs[-2:]
-    weight, bias = gradient_sums(shares, lambda ref: 0)
-    weight_ref[...] = (weight * scale).astype(BF16)
-    bias_ref[...] = bias * scale
-
-
-def totals(shares, scale):
-    extra, width = shares[0].shape
-    return pl.pallas_call(
-        functools.partial(totals_kernel, scale),
+        name="sum_shares",
+    )(*shares, *after)
+
+
+def halve_kernel(keep_ref, sent_ref, arrived_ref, rest_ref, send_ref):
+    rows, half = keep_ref.shape[0], rest_ref.shape[0]
+    held = sent_ref.shape[0] - rows
+    rest_ref[...] = keep_ref[:half, :] + arrived_ref[:half, :].astype(F32)
+    send_ref[:half, :] = (keep_ref[half:, :] + arrived_ref[half:rows, :].astype(F32)).astype(BF16)
+    send_ref[half:half + held, :] = sent_ref[rows:, :]
+    send_ref[half + held:, :] = arrived_ref[rows:, :]
+
+
+def halve(keep, sent, arrived):
+    rows, width = keep.shape
+    size = rows // 2 + 2 * (sent.shape[0] - rows)
+    return pl.pallas_call(
+        halve_kernel,
         out_shape=[
-            jax.ShapeDtypeStruct((extra - BIAS_ROWS, width), BF16),
-            jax.ShapeDtypeStruct((1, width), F32),
+            jax.ShapeDtypeStruct((rows // 2, width), F32),
+            jax.ShapeDtypeStruct((size, width), BF16),
         ],
-        in_specs=[VMEM] * len(shares),
-        out_specs=[VMEM] * 2,
-        compiler_params=params(),
-        name="gradient_totals",
-    )(*shares)
-
-
-def halve_kernel(keep_ref, arrived_ref, rest_ref, send_ref):
-    half = rest_ref.shape[0]
-    rest_ref[...] = keep_ref[:half, :] + arrived_ref[:half, :].astype(F32)
-    send_ref[...] = (keep_ref[half:, :] + arrived_ref[half:, :].astype(F32)).astype(BF16)
-
-
-def halve(keep, arrived):
-    shape = (keep.shape[0] // 2, keep.shape[1])
-    return pl.pallas_call(
-        halve_kernel,
-        out_shape=[jax.ShapeDtypeStruct(shape, F32), jax.ShapeDtypeStruct(shape, BF16)],
-        in_specs=[VMEM, VMEM],
+        in_specs=[VMEM] * 3,
         out_specs=[VMEM, VMEM],
         compiler_params=params(),
         name="halve_terms",
-    )(keep, arrived)
-
-
-def feature_kernel(own_ref, arrived_ref, out_ref, token_ref):
-    token_ref[...] = jnp.zeros_like(token_ref)
-    out_ref[...] = (own_ref[...] + arrived_ref[...].astype(F32)).astype(BF16)
-
-
-def feature_sum(own, arrived):
-    return pl.pallas_call(
-        feature_kernel,
-        out_shape=[jax.ShapeDtypeStruct(own.shape, BF16), jax.ShapeDtypeStruct((8, 128), F32)],
-        in_specs=[VMEM, VMEM],
-        out_specs=[VMEM, VMEM],
-        compiler_params=params(),
-        name="feature_sum",
-    )(own, arrived)
-
-
-def assemble_kernel(after_ref, *refs):
-    sections, out_ref = refs[:-1], refs[-1]
-    chunk, count = sections[0].shape[0], len(sections)
-    for d, ref in enumerate(sections):
+    )(keep, sent, arrived)
+
+
+def final_kernel(owners, keep_ref, sent_ref, arrived_ref, feature_ref, weight_ref):
+    rows = keep_ref.shape[0]
+    feature_ref[...] = (keep_ref[...] + arrived_ref[:rows, :].astype(F32)).astype(BF16)
+    count = len(owners)
+    chunk = weight_ref.shape[0] // count
+    for k, d in enumerate(owners):
         device, start, bit = jnp.bitwise_xor(lax.axis_index("row"), d), 0, 1
         while bit < count:
             start += jnp.where(jnp.bitwise_and(device, bit) != 0, chunk * count // (2 * bit), 0)
             bit *= 2
-        out_ref[pl.ds(pl.multiple_of(start, chunk), chunk), :] = ref[...].astype(F32)
-
-
-def assemble(after, sections):
-    chunk, width = sections[0].shape
-    return pl.pallas_call(
-        assemble_kernel,
-        out_shape=jax.ShapeDtypeStruct((chunk * len(sections), width), F32),
-        in_specs=[ANY] + [VMEM] * len(sections),
-        out_specs=VMEM,
-        compiler_params=params(),
-        name="assemble_weight_grad",
-    )(after, *sections)
-
-
-def backward_kernel(count, flip, panel_ref, *refs):
-    blocks, (out_ref, gathered) = refs[:count], (refs[-2], refs[-1])
-    rows = gathered.shape[0] // count
-    row_me, col_me = lax.axis_index("row"), lax.axis_index("col")
-    for d in range(count):
-        source = jnp.bitwise_xor(col_me, d)
-        gathered[pl.ds(pl.multiple_of(source * rows, rows), rows), :] = blocks[d][:rows, :]
-    for k in range(out_ref.shape[0] // rows):
-        target = jnp.bitwise_xor(row_me, 2 * k + flip)
-        part = panel_ref[:, pl.ds(pl.multiple_of(target * rows, rows), rows)]
-        value = lax.dot_general(part, gathered[...], (((0,), (0,)), ((), ())), preferred_element_type=F32)
-        out_ref[k * rows:(k + 1) * rows, :] = value.astype(out_ref.dtype)
-
-
-def backward(panel, blocks, after, half, flip, dtype):
+        source, place = (sent_ref, k) if k < count // 2 else (arrived_ref, k - count // 2)
+        value = source[rows + place * chunk:rows + (place + 1) * chunk, :].astype(F32)
+        weight_ref[pl.ds(pl.multiple_of(start, chunk), chunk), :] = value
+
+
+def final(owners, keep, sent, arrived):
+    rows, width = keep.shape
+    return pl.pallas_call(
+        functools.partial(final_kernel, owners),
+        out_shape=[
+            jax.ShapeDtypeStruct((rows, width), BF16),
+            jax.ShapeDtypeStruct((2 * (sent.shape[0] - rows), width), F32),
+        ],
+        in_specs=[VMEM] * 3,
+        out_specs=[VMEM, VMEM],
+        compiler_params=params(),
+        name="final_sums",
+    )(keep, sent, arrived)
+
+
+def gather_terms(blocks, gathered):
+    rows = blocks[0].shape[0]
+    for d, block in enumerate(blocks):
+        source = jnp.bitwise_xor(lax.axis_index("col"), d)
+        gathered[pl.ds(pl.multiple_of(source * rows, rows), rows), :] = block[...]
+
+
+def term(panel_ref, gathered, rows, d):
+    target = jnp.bitwise_xor(lax.axis_index("row"), d)
+    part = panel_ref[:, pl.ds(pl.multiple_of(target * rows, rows), rows)]
+    return lax.dot_general(part, gathered[...], (((0,), (0,)), ((), ())), preferred_element_type=F32)
+
+
+def send_kernel(count, scale, panel_ref, left_ref, right_ref, *refs):
+    blocks, (send_ref, gathered) = refs[:count], refs[count:]
+    rows = blocks[0].shape[0]
+    gather_terms(blocks, gathered)
+    weight, _ = gradient_sums([left_ref, right_ref], lambda ref: 0)
+    half = send_ref.shape[0] - weight.shape[0]
+    send_ref[half:, :] = (weight * scale).astype(BF16)
+    for k in range(half // rows):
+        send_ref[k * rows:(k + 1) * rows, :] = term(panel_ref, gathered, rows, 2 * k + 1).astype(BF16)
+
+
+def backward_send(panel, blocks, left, right, half, scale):
     rows, width = blocks[0].shape
     return pl.pallas_call(
-        functools.partial(backward_kernel, len(blocks), flip),
-        out_shape=jax.ShapeDtypeStruct((rows * half, width), dtype),
-        in_specs=[VMEM] * (1 + len(blocks)) + [ANY] * len(after),
+        functools.partial(send_kernel, len(blocks), scale),
+        out_shape=jax.ShapeDtypeStruct((rows * half + left.shape[0] - BIAS_ROWS, width), BF16),
+        in_specs=[VMEM] * (3 + len(blocks)),
         out_specs=VMEM,
         scratch_shapes=[pltpu.VMEM((rows * len(blocks), width), BF16)],
         compiler_params=params(),
-        name="backward_terms",
-    )(panel, *blocks, *after)
+        name="backward_send",
+    )(panel, left, right, *blocks)
+
+
+def keep_kernel(count, scale, panel_ref, left_ref, right_ref, *refs):
+    blocks, (keep_ref, bias_ref, gathered) = refs[:count], refs[count:]
+    rows = blocks[0].shape[0]
+    gather_terms(blocks, gathered)
+    bias_ref[...] = gradient_sums([left_ref, right_ref], lambda ref: 0)[1] * scale
+    for k in range(keep_ref.shape[0] // rows):
+        keep_ref[k * rows:(k + 1) * rows, :] = term(panel_ref, gathered, rows, 2 * k)
+
+
+def backward_keep(panel, blocks, left, right, half, scale):
+    rows, width = blocks[0].shape
+    return pl.pallas_call(
+        functools.partial(keep_kernel, len(blocks), scale),
+        out_shape=[
+            jax.ShapeDtypeStruct((rows * half, width), F32),
+            jax.ShapeDtypeStruct((1, width), F32),
+        ],
+        in_specs=[VMEM] * (3 + len(blocks)),
+        out_specs=[VMEM, VMEM],
+        scratch_shapes=[pltpu.VMEM((rows * len(blocks), width), BF16)],
+        compiler_params=params(),
+        name="backward_keep",
+    )(panel, left, right, *blocks)
 
 
 def body(features, weight, bias_vector, out_grad, adj_tiles, tile_pos, tile_count):
@@ -358,7 +349,7 @@
     col_tiles = row_count * rows_dev // tile_size
 
     blocks = [features] + [swapped(features, "row", d) for d in range(1, row_count)]
-    panel = build_panel(tile_pos[0], tile_count, adj_tiles[0, 0], row_tiles, col_tiles)
+    panel = build_panel(pltpu.with_memory_space_constraint(tile_pos[0], pltpu.HBM), tile_count, adj_tiles[0, 0], row_tiles, col_tiles)
     sends = forward(panel, blocks, col_count // 2, 1, BF16)
     keeps = forward(panel, blocks, col_count // 2, 0, F32)
     parts = []
@@ -382,29 +373,28 @@
         share, send = split_sum(bit, share, arrived)
         arrived = swapped(send, "row", bit)
         bit *= 2
-    extra = share.shape[0]
-    sent = relay(agg_grad, [share, arrived], [grads[d] for d in order[:-1]])
-    grads[1] = swapped(sent, "col", 1)
+    grads[1] = swapped(agg_grad, "col", 1)
     for d in order:
         grads[d + 1] = swapped(grads[d], "col", 1)
     blocks = [grads[d] for d in range(col_count)]
-    share = pair_sum(extra, sent, grads[1])
+    share = sum_shares([share, arrived], [grads[d] for d in order[:-1]])
     shares = {d: swapped(share, "col", d) for d in order}
     shares = [share] + [shares[d] for d in range(2, col_count, 2)]
-
-    send = backward(panel, blocks, shares[1:], row_count // 2, 1, BF16)
-    keep = backward(panel, blocks, [], row_count // 2, 0, F32)
-    terms = swapped(send, "row", 1)
-    bit = row_count // 2
+    share = sum_shares(shares, [grads[d + 1] for d in order[:1]])
+    arrived = swapped(share, "col", 1)
+
+    scale = 1.0 / math.sqrt(row_count * col_count * rows_dev)
+    pair = (share, arrived, row_count // 2, scale)
+    sent = backward_send(panel, blocks, *pair)
+    keep, bias_grad = backward_keep(panel, blocks, *pair)
+    terms = swapped(sent, "row", 1)
+    owners, bit = [0, 1], row_count // 2
     while bit > 1:
-        keep, send = halve(keep, terms)
-        terms = swapped(send, "row", bit)
+        keep, sent = halve(keep, sent, terms)
+        terms = swapped(sent, "row", bit)
+        owners = owners + [d ^ bit for d in owners]
         bit //= 2
-    feature_grad, token = feature_sum(keep, terms)
-    scale = 1.0 / math.sqrt(row_count * col_count * rows_dev)
-    section, bias_grad = totals(shares, scale)
-    sections = [section] + [swapped(section, "row", d) for d in range(1, row_count)]
-    weight_grad = assemble(token, sections)
+    feature_grad, weight_grad = final(owners, keep, sent, terms)
     return (hidden_out, feature_grad, weight_grad, bias_grad.reshape(width))
 
 

time: 55.3 us -> 53.3 us (0.964)
  starting transfers between devices: 31.5 us -> 30.3 us
  Pallas kernels: 6.54 us -> 5.78 us
  local copies, waits for them, and re-layouts: 0.66 us -> 0.02 us
  waiting for transfers between devices: 15 us -> 15.6 us
    ppermute x27 -> x25, starting transfers between devices: 31.5 us -> 30.3 us  [swapped(): return lax.ppermute(block, axis, [(i, i ^ bit) for i in range(n)])]
    pallas_call x8 -> x6, Pallas kernels: 2.8 us -> 2.04 us  [the longest x1 0.82 us: backward_keep(): pl.pallas_call(functools.partial(keep_kernel, len(blocks), scale), out_sh...]
    ppermute x27 -> x25, waiting for transfers between devices: 15 us -> 15.6 us  [swapped(): return lax.ppermute(block, axis, [(i, i ^ bit) for i in range(n)])]
    unnamed x10 -> x8, local copies, waits for them, and re-layouts: 0.66 us -> 0.02 us
  transfers between devices with their start and end apart: 27 -> 25, of which waited for: 14 -> 12; matrix products, arithmetic and copies ran while one was open for 0% -> 0% of each run, Pallas kernels for 8% -> 6%
where the time goes in v3:
time: 53.3 us; the launch traced here: 53.2 us
  starting transfers between devices  30.3 us (57%)
  waiting for transfers between devices  15.6 us (29%)
  Pallas kernels  5.78 us (11%)
  between operations  1.42 us (3%)
    ppermute x25, starting transfers between devices, swapped(): return lax.ppermute(block, axis, [(i, i ^ bit) for i in range(n)])  30.3 us
    ppermute x25, waiting for transfers between devices, swapped(): return lax.ppermute(block, axis, [(i, i ^ bit) for i in range(n)])  15.6 us
    pallas_call x1, Pallas kernels, build_panel(): pl.pallas_call(functools.partial(build_kernel, col_tiles), out_shape=jax....  2.21 us
  transfers between devices with their start and end apart: 25, of which 12 were waited for; matrix products, arithmetic and copies ran while one was open for 0% of the time, Pallas kernels for 6%

profile of v3, /device:TPU:0, one launch (start us, length us, event | category | flops | bytes accessed | tf_op | source)
XLA Modules:
  0.0 53.2 jit_solution(15435551688284775741)
XLA Ops:
  0.6 2.4 %collective-permute-start.2 = (bf16[128,256]{1,0:T(8,128)(2,1)}, bf16[128,256]{1,0:T(8,128)(2,1)S(1)}, u32[]{:S(2)}, u32[]{:S(2)}) collective-permute-start(bf16[128,256]{1,0:T(8,128)(2,1)} %refs_0_.3), channel_id=1, source_target_pairs={{0,24},{8,16},{16,8},{24,0},{1,25},{9,17},{17,9},{25,1},{2,26},{10... | collective-permute-start | bytes 196616 | tf_op jit(solution)/shard_map/ppermute | solution.py:22
  4.4 2.2 %build_panel.1.panel_ref = bf16[1024,512]{1,0:T(8,128)(2,1)S(1)} custom-call(s32[1,96]{1,0:T(1,128)} %bitcast.6, s32[1,1]{1,0:T(1,128)S(6)} %copy.11.count_ref, bf16[96,128,128]{2,1,0:T(8,128)(2,1)} %bitcast.5), custom_call_target="tpu_custom_call" | custom-call | flops 1572864 | bytes 3145728 | tf_op jit(solution)/shard_map/build_panel/pallas_call | solution.py:62
  6.7 1.3 %collective-permute-done.1.refs_2_ = bf16[128,256]{1,0:T(8,128)(2,1)S(1)} collective-permute-done((bf16[128,256]{1,0:T(8,128)(2,1)}, bf16[128,256]{1,0:T(8,128)(2,1)S(1)}, u32[]{:S(2)}, u32[]{:S(2)}) %collective-permute-start.1) | collective-permute-done | bytes 65568 | tf_op jit(solution)/shard_map/ppermute | solution.py:22
  8.3 1.8 %collective-permute-start.5 = (bf16[128,256]{1,0:T(8,128)(2,1)S(1)}, bf16[128,256]{1,0:T(8,128)(2,1)S(1)}, u32[]{:S(2)}, u32[]{:S(2)}) collective-permute-start(bf16[128,256]{1,0:T(8,128)(2,1)S(1)} %get-tuple-element.27), channel_id=1, source_target_pairs={{0,1},{1,0},{2,3},{3,2},{4,5},{5,4},{6,7},{7,6},{8,9},{9,8},{10,11... | collective-permute-start | bytes 196616 | tf_op jit(solution)/shard_map/ppermute | solution.py:22
  10.4 1.7 %collective-permute-start.7 = (bf16[128,256]{1,0:T(8,128)(2,1)S(1)}, bf16[128,256]{1,0:T(8,128)(2,1)S(1)}, u32[]{:S(2)}, u32[]{:S(2)}) collective-permute-start(bf16[128,256]{1,0:T(8,128)(2,1)S(1)} %get-tuple-element.29), channel_id=1, source_target_pairs={{0,1},{1,0},{2,3},{3,2},{4,5},{5,4},{6,7},{7,6},{8,9},{9,8},{10,11... | collective-permute-start | bytes 196616 | tf_op jit(solution)/shard_map/ppermute | solution.py:22
  13.0 4.0 %collective-permute-start.6 = (bf16[128,256]{1,0:T(8,128)(2,1)S(1)}, bf16[128,256]{1,0:T(8,128)(2,1)S(1)}, u32[]{:S(2)}, u32[]{:S(2)}) collective-permute-start(bf16[128,256]{1,0:T(8,128)(2,1)S(1)} %add_convert_fusion.1), channel_id=1, source_target_pairs={{0,6},{1,7},{2,4},{3,5},{4,2},{5,3},{6,0},{7,1},{8,14},{9,15},{10,... | collective-permute-start | bytes 196616 | tf_op jit(solution)/shard_map/ppermute | solution.py:22
  17.0 0.7 %collective-permute-start.4 = (bf16[128,256]{1,0:T(8,128)(2,1)S(1)}, bf16[128,256]{1,0:T(8,128)(2,1)S(1)}, u32[]{:S(2)}, u32[]{:S(2)}) collective-permute-start(bf16[128,256]{1,0:T(8,128)(2,1)S(1)} %add_convert_fusion.2), channel_id=1, source_target_pairs={{0,4},{1,5},{2,6},{3,7},{4,0},{5,1},{6,2},{7,3},{8,12},{9,13},{10,... | collective-permute-start | bytes 196616 | tf_op jit(solution)/shard_map/ppermute | solution.py:22
  17.8 1.6 %collective-permute-start.8 = (bf16[128,256]{1,0:T(8,128)(2,1)S(1)}, bf16[128,256]{1,0:T(8,128)(2,1)S(1)}, u32[]{:S(2)}, u32[]{:S(2)}) collective-permute-start(bf16[128,256]{1,0:T(8,128)(2,1)S(1)} %add_convert_fusion), channel_id=1, source_target_pairs={{0,2},{1,3},{2,0},{3,1},{4,6},{5,7},{6,4},{7,5},{8,10},{9,11},{10,... | collective-permute-start | bytes 196616 | tf_op jit(solution)/shard_map/ppermute | solution.py:22
  19.6 2.7 %collective-permute-done.4.refs_0_ = bf16[128,256]{1,0:T(8,128)(2,1)S(1)} collective-permute-done((bf16[128,256]{1,0:T(8,128)(2,1)S(1)}, bf16[128,256]{1,0:T(8,128)(2,1)S(1)}, u32[]{:S(2)}, u32[]{:S(2)}) %collective-permute-start.4) | collective-permute-done | bytes 65568 | tf_op jit(solution)/shard_map/ppermute | solution.py:22
  22.9 0.8 %dense_stage.1 = (bf16[128,256]{1,0:T(8,128)(2,1)}, bf16[128,256]{1,0:T(8,128)(2,1)S(1)}, bf16[144,256]{1,0:T(8,128)(2,1)S(1)}, bf16[144,256]{1,0:T(8,128)(2,1)S(1)}) custom-call(bf16[256,256]{1,0:T(8,128)(2,1)S(1)} %copy-done.1, f32[1,256]{1,0:T(1,128)S(1)} %bitcast.4, bf16[128,256]{1,0:T(8,128)(2,1)S(1)} %copy-done.2, ...), custom_call_target="tpu_custom_call" | custom-call | tf_op jit(solution)/shard_map/dense_stage/pallas_call | solution.py:165
  23.7 1.5 %collective-permute-start.12 = (bf16[128,256]{1,0:T(8,128)(2,1)S(1)}, bf16[128,256]{1,0:T(8,128)(2,1)S(1)}, u32[]{:S(2)}, u32[]{:S(2)}) collective-permute-start(bf16[128,256]{1,0:T(8,128)(2,1)S(1)} %get-tuple-element.37.refs_0_), channel_id=1, source_target_pairs={{0,4},{1,5},{2,6},{3,7},{4,0},{5,1},{6,2},{7,3},{8,12},{9,13},{10,... | collective-permute-start | bytes 196616 | tf_op jit(solution)/shard_map/ppermute | solution.py:22
  25.2 1.7 %collective-permute-start.13 = (bf16[128,256]{1,0:T(8,128)(2,1)S(1)}, bf16[128,256]{1,0:T(8,128)(2,1)S(1)}, u32[]{:S(2)}, u32[]{:S(2)}) collective-permute-start(bf16[128,256]{1,0:T(8,128)(2,1)S(1)} %get-tuple-element.37.refs_0_), channel_id=1, source_target_pairs={{0,6},{1,7},{2,4},{3,5},{4,2},{5,3},{6,0},{7,1},{8,14},{9,15},{10,... | collective-permute-start | bytes 196616 | tf_op jit(solution)/shard_map/ppermute | solution.py:22
  27.0 1.5 %collective-permute-start.11 = (bf16[80,256]{1,0:T(8,128)(2,1)S(1)}, bf16[80,256]{1,0:T(8,128)(2,1)S(1)}, u32[]{:S(2)}, u32[]{:S(2)}) collective-permute-start(bf16[80,256]{1,0:T(8,128)(2,1)S(1)} %get-tuple-element.36), channel_id=1, source_target_pairs={{0,16},{8,24},{16,0},{24,8},{1,17},{9,25},{17,1},{25,9},{2,18},{10... | collective-permute-start | bytes 122888 | tf_op jit(solution)/shard_map/ppermute | solution.py:22
  28.7 3.5 %collective-permute-done.12.refs_2_.refs_4_ = bf16[128,256]{1,0:T(8,128)(2,1)S(1)} collective-permute-done((bf16[128,256]{1,0:T(8,128)(2,1)S(1)}, bf16[128,256]{1,0:T(8,128)(2,1)S(1)}, u32[]{:S(2)}, u32[]{:S(2)}) %collective-permute-start.12) | collective-permute-done | bytes 65568 | tf_op jit(solution)/shard_map/ppermute | solution.py:22
  32.2 1.4 %collective-permute-start.17 = (bf16[128,256]{1,0:T(8,128)(2,1)S(1)}, bf16[128,256]{1,0:T(8,128)(2,1)S(1)}, u32[]{:S(2)}, u32[]{:S(2)}) collective-permute-start(bf16[128,256]{1,0:T(8,128)(2,1)S(1)} %collective-permute-done.12.refs_2_.refs_4_), channel_id=1, source_target_pairs={{0,1},{1,0},{2,3},{3,2},{4,5},{5,4},{6,7},{7,6},{8,9},{9,8},{10,11... | collective-permute-start | bytes 196616 | tf_op jit(solution)/shard_map/ppermute | solution.py:22
  33.6 2.2 %collective-permute-start.16 = (bf16[80,256]{1,0:T(8,128)(2,1)S(1)}, bf16[80,256]{1,0:T(8,128)(2,1)S(1)}, u32[]{:S(2)}, u32[]{:S(2)}) collective-permute-start(bf16[80,256]{1,0:T(8,128)(2,1)S(1)} %sum_shares.2.refs_0_), channel_id=1, source_target_pairs={{0,6},{1,7},{2,4},{3,5},{4,2},{5,3},{6,0},{7,1},{8,14},{9,15},{10,... | collective-permute-start | bytes 122888 | tf_op jit(solution)/shard_map/ppermute | solution.py:22
  35.9 2.2 %collective-permute-start.14 = (bf16[80,256]{1,0:T(8,128)(2,1)S(1)}, bf16[80,256]{1,0:T(8,128)(2,1)S(1)}, u32[]{:S(2)}, u32[]{:S(2)}) collective-permute-start(bf16[80,256]{1,0:T(8,128)(2,1)S(1)} %sum_shares.2.refs_0_), channel_id=1, source_target_pairs={{0,2},{1,3},{2,0},{3,1},{4,6},{5,7},{6,4},{7,5},{8,10},{9,11},{10,... | collective-permute-start | bytes 122888 | tf_op jit(solution)/shard_map/ppermute | solution.py:22
  38.8 1.4 %collective-permute-start.21 = (bf16[128,256]{1,0:T(8,128)(2,1)S(1)}, bf16[128,256]{1,0:T(8,128)(2,1)S(1)}, u32[]{:S(2)}, u32[]{:S(2)}) collective-permute-start(bf16[128,256]{1,0:T(8,128)(2,1)S(1)} %collective-permute-done.20.refs_2_), channel_id=1, source_target_pairs={{0,1},{1,0},{2,3},{3,2},{4,5},{5,4},{6,7},{7,6},{8,9},{9,8},{10,11... | collective-permute-start | bytes 196616 | tf_op jit(solution)/shard_map/ppermute | solution.py:22
  40.9 1.4 %collective-permute-start.18 = (bf16[80,256]{1,0:T(8,128)(2,1)S(1)}, bf16[80,256]{1,0:T(8,128)(2,1)S(1)}, u32[]{:S(2)}, u32[]{:S(2)}) collective-permute-start(bf16[80,256]{1,0:T(8,128)(2,1)S(1)} %sum_shares.3.left_ref), channel_id=1, source_target_pairs={{0,1},{1,0},{2,3},{3,2},{4,5},{5,4},{6,7},{7,6},{8,9},{9,8},{10,11... | collective-permute-start | bytes 122888 | tf_op jit(solution)/shard_map/ppermute | solution.py:22
  43.1 1.3 %collective-permute-done.22.refs_7_ = bf16[128,256]{1,0:T(8,128)(2,1)S(1)} collective-permute-done((bf16[128,256]{1,0:T(8,128)(2,1)S(1)}, bf16[128,256]{1,0:T(8,128)(2,1)S(1)}, u32[]{:S(2)}, u32[]{:S(2)}) %collective-permute-start.22) | collective-permute-done | bytes 65568 | tf_op jit(solution)/shard_map/ppermute | solution.py:22
  45.4 0.8 %backward_keep.1 = (f32[256,256]{1,0:T(8,128)S(1)}, f32[1,256]{1,0:T(1,128)}) custom-call(bf16[1024,512]{1,0:T(8,128)(2,1)S(1)} %build_panel.1.panel_ref, bf16[80,256]{1,0:T(8,128)(2,1)S(1)} %sum_shares.3.left_ref, bf16[80,256]{1,0:T(8,128)(2,1)S(1)} %collective-permute-done.18.right_ref, bf16[128,256]{1,0:T(8,128)(2,1)S(1)} %get-tuple-element.37.refs_0_, ...), custom_call_target="tpu_custom_call" | custom-call | tf_op jit(solution)/shard_map/backward_keep/pallas_call | solution.py:329
  46.8 1.7 %collective-permute-start.24 = (bf16[256,256]{1,0:T(8,128)(2,1)S(1)}, bf16[256,256]{1,0:T(8,128)(2,1)S(1)}, u32[]{:S(2)}, u32[]{:S(2)}) collective-permute-start(bf16[256,256]{1,0:T(8,128)(2,1)S(1)} %get-tuple-element.40.sent_ref), channel_id=1, source_target_pairs={{0,16},{8,24},{16,0},{24,8},{1,17},{9,25},{17,1},{25,9},{2,18},{10... | collective-permute-start | bytes 393224 | tf_op jit(solution)/shard_map/ppermute | solution.py:22
  48.5 3.9 %collective-permute-done.24.arrived_ref = bf16[256,256]{1,0:T(8,128)(2,1)S(1)} collective-permute-done((bf16[256,256]{1,0:T(8,128)(2,1)S(1)}, bf16[256,256]{1,0:T(8,128)(2,1)S(1)}, u32[]{:S(2)}, u32[]{:S(2)}) %collective-permute-start.24) | collective-permute-done | bytes 131104 | tf_op jit(solution)/shard_map/ppermute | solution.py:22
  52.4 0.8 %final_sums.1 = (bf16[128,256]{1,0:T(8,128)(2,1)}, f32[256,256]{1,0:T(8,128)}) custom-call(f32[128,256]{1,0:T(8,128)S(1)} %get-tuple-element.39.keep_ref, bf16[256,256]{1,0:T(8,128)(2,1)S(1)} %get-tuple-element.40.sent_ref, bf16[256,256]{1,0:T(8,128)(2,1)S(1)} %collective-permute-done.24.arrived_ref), custom_call_target="tpu_custom_call" | custom-call | tf_op jit(solution)/shard_map/final_sums/pallas_call | solution.py:268
  (48 shorter events, 7.1 us)
Async XLA Ops:
  0.6 6.0 %collective-permute-start.2 = (bf16[128,256]{1,0:T(8,128)(2,1)}, bf16[128,256]{1,0:T(8,128)(2,1)S(1)}, u32[]{:S(2)}, u32[]{:S(2)}) collective-permute-start(bf16[128,256]{1,0:T(8,128)(2,1)} %refs_0_.3), channel_id=1, source_target_pairs={{0,24},{8,16},{16,8},{24,0},{1,25},{9,17},{17,9},{25,1},{2,26},{10... | collective-permute-start | bytes 196616 | tf_op jit(solution)/shard_map/ppermute | solution.py:22
  3.1 4.9 %collective-permute-start.1 = (bf16[128,256]{1,0:T(8,128)(2,1)}, bf16[128,256]{1,0:T(8,128)(2,1)S(1)}, u32[]{:S(2)}, u32[]{:S(2)}) collective-permute-start(bf16[128,256]{1,0:T(8,128)(2,1)} %refs_0_.3), channel_id=1, source_target_pairs={{0,16},{8,24},{16,0},{24,8},{1,17},{9,25},{17,1},{25,9},{2,18},{10... | collective-permute-start | bytes 196616 | tf_op jit(solution)/shard_map/ppermute | solution.py:22
  3.7 4.2 %collective-permute-start = (bf16[128,256]{1,0:T(8,128)(2,1)}, bf16[128,256]{1,0:T(8,128)(2,1)S(1)}, u32[]{:S(2)}, u32[]{:S(2)}) collective-permute-start(bf16[128,256]{1,0:T(8,128)(2,1)} %refs_0_.3), channel_id=1, source_target_pairs={{0,8},{8,0},{16,24},{24,16},{1,9},{9,1},{17,25},{25,17},{2,10},{10... | collective-permute-start | bytes 196616 | tf_op jit(solution)/shard_map/ppermute | solution.py:22
  8.3 4.7 %collective-permute-start.5 = (bf16[128,256]{1,0:T(8,128)(2,1)S(1)}, bf16[128,256]{1,0:T(8,128)(2,1)S(1)}, u32[]{:S(2)}, u32[]{:S(2)}) collective-permute-start(bf16[128,256]{1,0:T(8,128)(2,1)S(1)} %get-tuple-element.27), channel_id=1, source_target_pairs={{0,1},{1,0},{2,3},{3,2},{4,5},{5,4},{6,7},{7,6},{8,9},{9,8},{10,11... | collective-permute-start | bytes 196616 | tf_op jit(solution)/shard_map/ppermute | solution.py:22
  10.1 6.9 %collective-permute-start.3 = (bf16[128,256]{1,0:T(8,128)(2,1)S(1)}, bf16[128,256]{1,0:T(8,128)(2,1)S(1)}, u32[]{:S(2)}, u32[]{:S(2)}) collective-permute-start(bf16[128,256]{1,0:T(8,128)(2,1)S(1)} %get-tuple-element.25), channel_id=1, source_target_pairs={{0,1},{1,0},{2,3},{3,2},{4,5},{5,4},{6,7},{7,6},{8,9},{9,8},{10,11... | collective-permute-start | bytes 196616 | tf_op jit(solution)/shard_map/ppermute | solution.py:22
  10.4 7.4 %collective-permute-start.7 = (bf16[128,256]{1,0:T(8,128)(2,1)S(1)}, bf16[128,256]{1,0:T(8,128)(2,1)S(1)}, u32[]{:S(2)}, u32[]{:S(2)}) collective-permute-start(bf16[128,256]{1,0:T(8,128)(2,1)S(1)} %get-tuple-element.29), channel_id=1, source_target_pairs={{0,1},{1,0},{2,3},{3,2},{4,5},{5,4},{6,7},{7,6},{8,9},{9,8},{10,11... | collective-permute-start | bytes 196616 | tf_op jit(solution)/shard_map/ppermute | solution.py:22
  12.1 7.3 %collective-permute-start.9 = (bf16[128,256]{1,0:T(8,128)(2,1)S(1)}, bf16[128,256]{1,0:T(8,128)(2,1)S(1)}, u32[]{:S(2)}, u32[]{:S(2)}) collective-permute-start(bf16[128,256]{1,0:T(8,128)(2,1)S(1)} %get-tuple-element.31), channel_id=1, source_target_pairs={{0,1},{1,0},{2,3},{3,2},{4,5},{5,4},{6,7},{7,6},{8,9},{9,8},{10,11... | collective-permute-start | bytes 196616 | tf_op jit(solution)/shard_map/ppermute | solution.py:22
  13.0 6.5 %collective-permute-start.6 = (bf16[128,256]{1,0:T(8,128)(2,1)S(1)}, bf16[128,256]{1,0:T(8,128)(2,1)S(1)}, u32[]{:S(2)}, u32[]{:S(2)}) collective-permute-start(bf16[128,256]{1,0:T(8,128)(2,1)S(1)} %add_convert_fusion.1), channel_id=1, source_target_pairs={{0,6},{1,7},{2,4},{3,5},{4,2},{5,3},{6,0},{7,1},{8,14},{9,15},{10,... | collective-permute-start | bytes 196616 | tf_op jit(solution)/shard_map/ppermute | solution.py:22
  17.0 5.3 %collective-permute-start.4 = (bf16[128,256]{1,0:T(8,128)(2,1)S(1)}, bf16[128,256]{1,0:T(8,128)(2,1)S(1)}, u32[]{:S(2)}, u32[]{:S(2)}) collective-permute-start(bf16[128,256]{1,0:T(8,128)(2,1)S(1)} %add_convert_fusion.2), channel_id=1, source_target_pairs={{0,4},{1,5},{2,6},{3,7},{4,0},{5,1},{6,2},{7,3},{8,12},{9,13},{10,... | collective-permute-start | bytes 196616 | tf_op jit(solution)/shard_map/ppermute | solution.py:22
  17.8 5.1 %collective-permute-start.8 = (bf16[128,256]{1,0:T(8,128)(2,1)S(1)}, bf16[128,256]{1,0:T(8,128)(2,1)S(1)}, u32[]{:S(2)}, u32[]{:S(2)}) collective-permute-start(bf16[128,256]{1,0:T(8,128)(2,1)S(1)} %add_convert_fusion), channel_id=1, source_target_pairs={{0,2},{1,3},{2,0},{3,1},{4,6},{5,7},{6,4},{7,5},{8,10},{9,11},{10,... | collective-permute-start | bytes 196616 | tf_op jit(solution)/shard_map/ppermute | solution.py:22
  23.7 3.2 %collective-permute-start.10 = (bf16[144,256]{1,0:T(8,128)(2,1)S(1)}, bf16[144,256]{1,0:T(8,128)(2,1)S(1)}, u32[]{:S(2)}, u32[]{:S(2)}) collective-permute-start(bf16[144,256]{1,0:T(8,128)(2,1)S(1)} %get-tuple-element.34), channel_id=1, source_target_pairs={{0,8},{8,0},{16,24},{24,16},{1,9},{9,1},{17,25},{25,17},{2,10},{10... | collective-permute-start | bytes 221192 | tf_op jit(solution)/shard_map/ppermute | solution.py:22
  23.7 8.5 %collective-permute-start.12 = (bf16[128,256]{1,0:T(8,128)(2,1)S(1)}, bf16[128,256]{1,0:T(8,128)(2,1)S(1)}, u32[]{:S(2)}, u32[]{:S(2)}) collective-permute-start(bf16[128,256]{1,0:T(8,128)(2,1)S(1)} %get-tuple-element.37.refs_0_), channel_id=1, source_target_pairs={{0,4},{1,5},{2,6},{3,7},{4,0},{5,1},{6,2},{7,3},{8,12},{9,13},{10,... | collective-permute-start | bytes 196616 | tf_op jit(solution)/shard_map/ppermute | solution.py:22
  25.2 8.4 %collective-permute-start.13 = (bf16[128,256]{1,0:T(8,128)(2,1)S(1)}, bf16[128,256]{1,0:T(8,128)(2,1)S(1)}, u32[]{:S(2)}, u32[]{:S(2)}) collective-permute-start(bf16[128,256]{1,0:T(8,128)(2,1)S(1)} %get-tuple-element.37.refs_0_), channel_id=1, source_target_pairs={{0,6},{1,7},{2,4},{3,5},{4,2},{5,3},{6,0},{7,1},{8,14},{9,15},{10,... | collective-permute-start | bytes 196616 | tf_op jit(solution)/shard_map/ppermute | solution.py:22
  27.0 6.6 %collective-permute-start.11 = (bf16[80,256]{1,0:T(8,128)(2,1)S(1)}, bf16[80,256]{1,0:T(8,128)(2,1)S(1)}, u32[]{:S(2)}, u32[]{:S(2)}) collective-permute-start(bf16[80,256]{1,0:T(8,128)(2,1)S(1)} %get-tuple-element.36), channel_id=1, source_target_pairs={{0,16},{8,24},{16,0},{24,8},{1,17},{9,25},{17,1},{25,9},{2,18},{10... | collective-permute-start | bytes 122888 | tf_op jit(solution)/shard_map/ppermute | solution.py:22
  28.5 9.6 %collective-permute-start.20 = (bf16[128,256]{1,0:T(8,128)(2,1)S(1)}, bf16[128,256]{1,0:T(8,128)(2,1)S(1)}, u32[]{:S(2)}, u32[]{:S(2)}) collective-permute-start(bf16[128,256]{1,0:T(8,128)(2,1)S(1)} %get-tuple-element.37.refs_0_), channel_id=1, source_target_pairs={{0,2},{1,3},{2,0},{3,1},{4,6},{5,7},{6,4},{7,5},{8,10},{9,11},{10,... | collective-permute-start | bytes 196616 | tf_op jit(solution)/shard_map/ppermute | solution.py:22
  32.2 6.5 %collective-permute-start.17 = (bf16[128,256]{1,0:T(8,128)(2,1)S(1)}, bf16[128,256]{1,0:T(8,128)(2,1)S(1)}, u32[]{:S(2)}, u32[]{:S(2)}) collective-permute-start(bf16[128,256]{1,0:T(8,128)(2,1)S(1)} %collective-permute-done.12.refs_2_.refs_4_), channel_id=1, source_target_pairs={{0,1},{1,0},{2,3},{3,2},{4,5},{5,4},{6,7},{7,6},{8,9},{9,8},{10,11... | collective-permute-start | bytes 196616 | tf_op jit(solution)/shard_map/ppermute | solution.py:22
  33.6 6.5 %collective-permute-start.16 = (bf16[80,256]{1,0:T(8,128)(2,1)S(1)}, bf16[80,256]{1,0:T(8,128)(2,1)S(1)}, u32[]{:S(2)}, u32[]{:S(2)}) collective-permute-start(bf16[80,256]{1,0:T(8,128)(2,1)S(1)} %sum_shares.2.refs_0_), channel_id=1, source_target_pairs={{0,6},{1,7},{2,4},{3,5},{4,2},{5,3},{6,0},{7,1},{8,14},{9,15},{10,... | collective-permute-start | bytes 122888 | tf_op jit(solution)/shard_map/ppermute | solution.py:22
  35.9 4.9 %collective-permute-start.15 = (bf16[80,256]{1,0:T(8,128)(2,1)S(1)}, bf16[80,256]{1,0:T(8,128)(2,1)S(1)}, u32[]{:S(2)}, u32[]{:S(2)}) collective-permute-start(bf16[80,256]{1,0:T(8,128)(2,1)S(1)} %sum_shares.2.refs_0_), channel_id=1, source_target_pairs={{0,4},{1,5},{2,6},{3,7},{4,0},{5,1},{6,2},{7,3},{8,12},{9,13},{10,... | collective-permute-start | bytes 122888 | tf_op jit(solution)/shard_map/ppermute | solution.py:22
  35.9 4.9 %collective-permute-start.14 = (bf16[80,256]{1,0:T(8,128)(2,1)S(1)}, bf16[80,256]{1,0:T(8,128)(2,1)S(1)}, u32[]{:S(2)}, u32[]{:S(2)}) collective-permute-start(bf16[80,256]{1,0:T(8,128)(2,1)S(1)} %sum_shares.2.refs_0_), channel_id=1, source_target_pairs={{0,2},{1,3},{2,0},{3,1},{4,6},{5,7},{6,4},{7,5},{8,10},{9,11},{10,... | collective-permute-start | bytes 122888 | tf_op jit(solution)/shard_map/ppermute | solution.py:22
  38.1 4.3 %collective-permute-start.19 = (bf16[128,256]{1,0:T(8,128)(2,1)S(1)}, bf16[128,256]{1,0:T(8,128)(2,1)S(1)}, u32[]{:S(2)}, u32[]{:S(2)}) collective-permute-start(bf16[128,256]{1,0:T(8,128)(2,1)S(1)} %get-tuple-element.37.refs_0_), channel_id=1, source_target_pairs={{0,1},{1,0},{2,3},{3,2},{4,5},{5,4},{6,7},{7,6},{8,9},{9,8},{10,11... | collective-permute-start | bytes 196616 | tf_op jit(solution)/shard_map/ppermute | solution.py:22
  38.8 4.3 %collective-permute-start.21 = (bf16[128,256]{1,0:T(8,128)(2,1)S(1)}, bf16[128,256]{1,0:T(8,128)(2,1)S(1)}, u32[]{:S(2)}, u32[]{:S(2)}) collective-permute-start(bf16[128,256]{1,0:T(8,128)(2,1)S(1)} %collective-permute-done.20.refs_2_), channel_id=1, source_target_pairs={{0,1},{1,0},{2,3},{3,2},{4,5},{5,4},{6,7},{7,6},{8,9},{9,8},{10,11... | collective-permute-start | bytes 196616 | tf_op jit(solution)/shard_map/ppermute | solution.py:22
  40.1 4.3 %collective-permute-start.22 = (bf16[128,256]{1,0:T(8,128)(2,1)S(1)}, bf16[128,256]{1,0:T(8,128)(2,1)S(1)}, u32[]{:S(2)}, u32[]{:S(2)}) collective-permute-start(bf16[128,256]{1,0:T(8,128)(2,1)S(1)} %collective-permute-done.13.refs_3_.refs_6_), channel_id=1, source_target_pairs={{0,1},{1,0},{2,3},{3,2},{4,5},{5,4},{6,7},{7,6},{8,9},{9,8},{10,11... | collective-permute-start | bytes 196616 | tf_op jit(solution)/shard_map/ppermute | solution.py:22
  40.9 4.1 %collective-permute-start.18 = (bf16[80,256]{1,0:T(8,128)(2,1)S(1)}, bf16[80,256]{1,0:T(8,128)(2,1)S(1)}, u32[]{:S(2)}, u32[]{:S(2)}) collective-permute-start(bf16[80,256]{1,0:T(8,128)(2,1)S(1)} %sum_shares.3.left_ref), channel_id=1, source_target_pairs={{0,1},{1,0},{2,3},{3,2},{4,5},{5,4},{6,7},{7,6},{8,9},{9,8},{10,11... | collective-permute-start | bytes 122888 | tf_op jit(solution)/shard_map/ppermute | solution.py:22
  46.8 5.6 %collective-permute-start.24 = (bf16[256,256]{1,0:T(8,128)(2,1)S(1)}, bf16[256,256]{1,0:T(8,128)(2,1)S(1)}, u32[]{:S(2)}, u32[]{:S(2)}) collective-permute-start(bf16[256,256]{1,0:T(8,128)(2,1)S(1)} %get-tuple-element.40.sent_ref), channel_id=1, source_target_pairs={{0,16},{8,24},{16,0},{24,8},{1,17},{9,25},{17,1},{25,9},{2,18},{10... | collective-permute-start | bytes 393224 | tf_op jit(solution)/shard_map/ppermute | solution.py:22
  (5 other events, 64.1 us)

commit v4 on v3

--- a/solution.py
+++ b/solution.py
@@ -81,6 +81,21 @@
 
 def peers(count):
     return sorted(range(2, count, 2), key=lambda d: (abs(d - count // 2 - 0.5), d)) + [0]
+
+
+def copy_kernel(block_ref, after_ref, out_ref):
+    out_ref[...] = block_ref[...]
+
+
+def copied(block, after):
+    return pl.pallas_call(
+        copy_kernel,
+        out_shape=jax.ShapeDtypeStruct(block.shape, block.dtype),
+        in_specs=[VMEM, ANY],
+        out_specs=VMEM,
+        compiler_params=params(),
+        name="copy_block",
+    )(block, after)
 
 
 def forward_kernel(count, flip, panel_ref, *refs):
@@ -348,8 +363,14 @@
     row_tiles = col_count * rows_dev // tile_size
     col_tiles = row_count * rows_dev // tile_size
 
-    blocks = [features] + [swapped(features, "row", d) for d in range(1, row_count)]
-    panel = build_panel(pltpu.with_memory_space_constraint(tile_pos[0], pltpu.HBM), tile_count, adj_tiles[0, 0], row_tiles, col_tiles)
+    blocks = [features] * row_count
+    for d in range(2, row_count, 2):
+        blocks[d] = swapped(features, "row", d)
+    blocks[1] = swapped(features, "row", 1)
+    pinned = pltpu.with_memory_space_constraint(tile_pos[0], pltpu.HBM)
+    panel = build_panel(pinned, tile_count, adj_tiles[0, 0], row_tiles, col_tiles)
+    for d in range(2, row_count, 2):
+        blocks[d + 1] = swapped(copied(blocks[d], panel), "row", 1)
     sends = forward(panel, blocks, col_count // 2, 1, BF16)
     keeps = forward(panel, blocks, col_count // 2, 0, F32)
     parts = []
@@ -377,10 +398,10 @@
     for d in order:
         grads[d + 1] = swapped(grads[d], "col", 1)
     blocks = [grads[d] for d in range(col_count)]
-    share = sum_shares([share, arrived], [grads[d] for d in order[:-1]])
+    share = sum_shares([share, arrived], [grads[order[0]]])
     shares = {d: swapped(share, "col", d) for d in order}
     shares = [share] + [shares[d] for d in range(2, col_count, 2)]
-    share = sum_shares(shares, [grads[d + 1] for d in order[:1]])
+    share = sum_shares(shares, [grads[1]])
     arrived = swapped(share, "col", 1)
 
     scale = 1.0 / math.sqrt(row_count * col_count * rows_dev)

time: 53.3 us -> 51.5 us (0.966)
  waiting for transfers between devices: 15.6 us -> 11.7 us
  starting transfers between devices: 30.3 us -> 32.4 us
    ppermute x25, waiting for transfers between devices: 15.6 us -> 11.7 us  [swapped(): return lax.ppermute(block, axis, [(i, i ^ bit) for i in range(n)])]
    ppermute x25, starting transfers between devices: 30.3 us -> 32.4 us  [swapped(): return lax.ppermute(block, axis, [(i, i ^ bit) for i in range(n)])]
  transfers between devices with their start and end apart: 25 -> 25, of which waited for: 12 -> 11; matrix products, arithmetic and copies ran while one was open for 0% -> 0% of each run, Pallas kernels for 6% -> 7%
where the time goes in v4:
time: 51.5 us; the launch traced here: 51.4 us
  starting transfers between devices  32.4 us (63%)
  waiting for transfers between devices  11.7 us (23%)
  Pallas kernels  5.79 us (11%)
  between operations  1.42 us (3%)
    ppermute x25, starting transfers between devices, swapped(): return lax.ppermute(block, axis, [(i, i ^ bit) for i in range(n)])  32.4 us
    ppermute x25, waiting for transfers between devices, swapped(): return lax.ppermute(block, axis, [(i, i ^ bit) for i in range(n)])  11.7 us
    pallas_call x1, Pallas kernels, build_panel(): pl.pallas_call(functools.partial(build_kernel, col_tiles), out_shape=jax....  2.21 us
  transfers between devices with their start and end apart: 25, of which 11 were waited for; matrix products, arithmetic and copies ran while one was open for 0% of the time, Pallas kernels for 7%

profile of v4, /device:TPU:0, one launch (start us, length us, event | category | flops | bytes accessed | tf_op | source)
XLA Modules:
  0.0 51.4 jit_solution(4589312772945255269)
XLA Ops:
  0.6 3.0 %collective-permute-start.1 = (bf16[128,256]{1,0:T(8,128)(2,1)}, bf16[128,256]{1,0:T(8,128)(2,1)S(1)}, u32[]{:S(2)}, u32[]{:S(2)}) collective-permute-start(bf16[128,256]{1,0:T(8,128)(2,1)} %refs_0_.3), channel_id=1, source_target_pairs={{0,16},{8,24},{16,0},{24,8},{1,17},{9,25},{17,1},{25,9},{2,18},{10... | collective-permute-start | bytes 196616 | tf_op jit(solution)/shard_map/ppermute | solution.py:22
  4.3 2.2 %build_panel.1.after_ref.panel_ref = bf16[1024,512]{1,0:T(8,128)(2,1)S(1)} custom-call(s32[1,96]{1,0:T(1,128)} %bitcast.6, s32[1,1]{1,0:T(1,128)S(6)} %copy.11.count_ref, bf16[96,128,128]{2,1,0:T(8,128)(2,1)} %bitcast.5), custom_call_target="tpu_custom_call" | custom-call | flops 1572864 | bytes 3145728 | tf_op jit(solution)/shard_map/build_panel/pallas_call | solution.py:62
  7.2 0.9 %collective-permute-done.2.refs_3_ = bf16[128,256]{1,0:T(8,128)(2,1)S(1)} collective-permute-done((bf16[128,256]{1,0:T(8,128)(2,1)S(1)}, bf16[128,256]{1,0:T(8,128)(2,1)S(1)}, u32[]{:S(2)}, u32[]{:S(2)}) %collective-permute-start.2) | collective-permute-done | bytes 65568 | tf_op jit(solution)/shard_map/ppermute | solution.py:22
  8.4 1.6 %collective-permute-start.5 = (bf16[128,256]{1,0:T(8,128)(2,1)S(1)}, bf16[128,256]{1,0:T(8,128)(2,1)S(1)}, u32[]{:S(2)}, u32[]{:S(2)}) collective-permute-start(bf16[128,256]{1,0:T(8,128)(2,1)S(1)} %get-tuple-element.27), channel_id=1, source_target_pairs={{0,1},{1,0},{2,3},{3,2},{4,5},{5,4},{6,7},{7,6},{8,9},{9,8},{10,11... | collective-permute-start | bytes 196616 | tf_op jit(solution)/shard_map/ppermute | solution.py:22
  10.5 1.5 %collective-permute-start.7 = (bf16[128,256]{1,0:T(8,128)(2,1)S(1)}, bf16[128,256]{1,0:T(8,128)(2,1)S(1)}, u32[]{:S(2)}, u32[]{:S(2)}) collective-permute-start(bf16[128,256]{1,0:T(8,128)(2,1)S(1)} %get-tuple-element.29), channel_id=1, source_target_pairs={{0,1},{1,0},{2,3},{3,2},{4,5},{5,4},{6,7},{7,6},{8,9},{9,8},{10,11... | collective-permute-start | bytes 196616 | tf_op jit(solution)/shard_map/ppermute | solution.py:22
  13.0 3.7 %collective-permute-start.6 = (bf16[128,256]{1,0:T(8,128)(2,1)S(1)}, bf16[128,256]{1,0:T(8,128)(2,1)S(1)}, u32[]{:S(2)}, u32[]{:S(2)}) collective-permute-start(bf16[128,256]{1,0:T(8,128)(2,1)S(1)} %add_convert_fusion.1), channel_id=1, source_target_pairs={{0,6},{1,7},{2,4},{3,5},{4,2},{5,3},{6,0},{7,1},{8,14},{9,15},{10,... | collective-permute-start | bytes 196616 | tf_op jit(solution)/shard_map/ppermute | solution.py:22
  16.7 0.9 %collective-permute-start.4 = (bf16[128,256]{1,0:T(8,128)(2,1)S(1)}, bf16[128,256]{1,0:T(8,128)(2,1)S(1)}, u32[]{:S(2)}, u32[]{:S(2)}) collective-permute-start(bf16[128,256]{1,0:T(8,128)(2,1)S(1)} %add_convert_fusion.2), channel_id=1, source_target_pairs={{0,4},{1,5},{2,6},{3,7},{4,0},{5,1},{6,2},{7,3},{8,12},{9,13},{10,... | collective-permute-start | bytes 196616 | tf_op jit(solution)/shard_map/ppermute | solution.py:22
  17.6 1.6 %collective-permute-start.8 = (bf16[128,256]{1,0:T(8,128)(2,1)S(1)}, bf16[128,256]{1,0:T(8,128)(2,1)S(1)}, u32[]{:S(2)}, u32[]{:S(2)}) collective-permute-start(bf16[128,256]{1,0:T(8,128)(2,1)S(1)} %add_convert_fusion), channel_id=1, source_target_pairs={{0,2},{1,3},{2,0},{3,1},{4,6},{5,7},{6,4},{7,5},{8,10},{9,11},{10,... | collective-permute-start | bytes 196616 | tf_op jit(solution)/shard_map/ppermute | solution.py:22
  19.9 2.4 %collective-permute-done.4.refs_0_ = bf16[128,256]{1,0:T(8,128)(2,1)S(1)} collective-permute-done((bf16[128,256]{1,0:T(8,128)(2,1)S(1)}, bf16[128,256]{1,0:T(8,128)(2,1)S(1)}, u32[]{:S(2)}, u32[]{:S(2)}) %collective-permute-start.4) | collective-permute-done | bytes 65568 | tf_op jit(solution)/shard_map/ppermute | solution.py:22
  22.7 0.8 %dense_stage.1 = (bf16[128,256]{1,0:T(8,128)(2,1)}, bf16[128,256]{1,0:T(8,128)(2,1)S(1)}, bf16[144,256]{1,0:T(8,128)(2,1)S(1)}, bf16[144,256]{1,0:T(8,128)(2,1)S(1)}) custom-call(bf16[256,256]{1,0:T(8,128)(2,1)S(1)} %copy-done.1, f32[1,256]{1,0:T(1,128)S(1)} %bitcast.4, bf16[128,256]{1,0:T(8,128)(2,1)S(1)} %copy-done.2, ...), custom_call_target="tpu_custom_call" | custom-call | tf_op jit(solution)/shard_map/dense_stage/pallas_call | solution.py:180
  23.5 1.4 %collective-permute-start.12 = (bf16[128,256]{1,0:T(8,128)(2,1)S(1)}, bf16[128,256]{1,0:T(8,128)(2,1)S(1)}, u32[]{:S(2)}, u32[]{:S(2)}) collective-permute-start(bf16[128,256]{1,0:T(8,128)(2,1)S(1)} %get-tuple-element.37.refs_0_), channel_id=1, source_target_pairs={{0,4},{1,5},{2,6},{3,7},{4,0},{5,1},{6,2},{7,3},{8,12},{9,13},{10,... | collective-permute-start | bytes 196616 | tf_op jit(solution)/shard_map/ppermute | solution.py:22
  25.0 1.4 %collective-permute-start.11 = (bf16[80,256]{1,0:T(8,128)(2,1)S(1)}, bf16[80,256]{1,0:T(8,128)(2,1)S(1)}, u32[]{:S(2)}, u32[]{:S(2)}) collective-permute-start(bf16[80,256]{1,0:T(8,128)(2,1)S(1)} %get-tuple-element.36), channel_id=1, source_target_pairs={{0,16},{8,24},{16,0},{24,8},{1,17},{9,25},{17,1},{25,9},{2,18},{10... | collective-permute-start | bytes 122888 | tf_op jit(solution)/shard_map/ppermute | solution.py:22
  26.4 2.2 %collective-permute-start.21 = (bf16[128,256]{1,0:T(8,128)(2,1)S(1)}, bf16[128,256]{1,0:T(8,128)(2,1)S(1)}, u32[]{:S(2)}, u32[]{:S(2)}) collective-permute-start(bf16[128,256]{1,0:T(8,128)(2,1)S(1)} %get-tuple-element.37.refs_0_), channel_id=1, source_target_pairs={{0,6},{1,7},{2,4},{3,5},{4,2},{5,3},{6,0},{7,1},{8,14},{9,15},{10,... | collective-permute-start | bytes 196616 | tf_op jit(solution)/shard_map/ppermute | solution.py:22
  28.6 1.5 %collective-permute-start.16 = (bf16[128,256]{1,0:T(8,128)(2,1)S(1)}, bf16[128,256]{1,0:T(8,128)(2,1)S(1)}, u32[]{:S(2)}, u32[]{:S(2)}) collective-permute-start(bf16[128,256]{1,0:T(8,128)(2,1)S(1)} %get-tuple-element.37.refs_0_), channel_id=1, source_target_pairs={{0,1},{1,0},{2,3},{3,2},{4,5},{5,4},{6,7},{7,6},{8,9},{9,8},{10,11... | collective-permute-start | bytes 196616 | tf_op jit(solution)/shard_map/ppermute | solution.py:22
  30.7 2.1 %collective-permute-start.15 = (bf16[80,256]{1,0:T(8,128)(2,1)S(1)}, bf16[80,256]{1,0:T(8,128)(2,1)S(1)}, u32[]{:S(2)}, u32[]{:S(2)}) collective-permute-start(bf16[80,256]{1,0:T(8,128)(2,1)S(1)} %sum_shares.2.refs_0_), channel_id=1, source_target_pairs={{0,6},{1,7},{2,4},{3,5},{4,2},{5,3},{6,0},{7,1},{8,14},{9,15},{10,... | collective-permute-start | bytes 122888 | tf_op jit(solution)/shard_map/ppermute | solution.py:22
  32.8 0.8 %collective-permute-start.14 = (bf16[80,256]{1,0:T(8,128)(2,1)S(1)}, bf16[80,256]{1,0:T(8,128)(2,1)S(1)}, u32[]{:S(2)}, u32[]{:S(2)}) collective-permute-start(bf16[80,256]{1,0:T(8,128)(2,1)S(1)} %sum_shares.2.refs_0_), channel_id=1, source_target_pairs={{0,4},{1,5},{2,6},{3,7},{4,0},{5,1},{6,2},{7,3},{8,12},{9,13},{10,... | collective-permute-start | bytes 122888 | tf_op jit(solution)/shard_map/ppermute | solution.py:22
  33.6 1.6 %collective-permute-start.13 = (bf16[80,256]{1,0:T(8,128)(2,1)S(1)}, bf16[80,256]{1,0:T(8,128)(2,1)S(1)}, u32[]{:S(2)}, u32[]{:S(2)}) collective-permute-start(bf16[80,256]{1,0:T(8,128)(2,1)S(1)} %sum_shares.2.refs_0_), channel_id=1, source_target_pairs={{0,2},{1,3},{2,0},{3,1},{4,6},{5,7},{6,4},{7,5},{8,10},{9,11},{10,... | collective-permute-start | bytes 122888 | tf_op jit(solution)/shard_map/ppermute | solution.py:22
  35.2 1.4 %collective-permute-start.22 = (bf16[128,256]{1,0:T(8,128)(2,1)S(1)}, bf16[128,256]{1,0:T(8,128)(2,1)S(1)}, u32[]{:S(2)}, u32[]{:S(2)}) collective-permute-start(bf16[128,256]{1,0:T(8,128)(2,1)S(1)} %collective-permute-done.21.refs_6_), channel_id=1, source_target_pairs={{0,1},{1,0},{2,3},{3,2},{4,5},{5,4},{6,7},{7,6},{8,9},{9,8},{10,11... | collective-permute-start | bytes 196616 | tf_op jit(solution)/shard_map/ppermute | solution.py:22
  37.2 1.4 %collective-permute-start.20 = (bf16[128,256]{1,0:T(8,128)(2,1)S(1)}, bf16[128,256]{1,0:T(8,128)(2,1)S(1)}, u32[]{:S(2)}, u32[]{:S(2)}) collective-permute-start(bf16[128,256]{1,0:T(8,128)(2,1)S(1)} %collective-permute-done.12.refs_2_.refs_4_), channel_id=1, source_target_pairs={{0,1},{1,0},{2,3},{3,2},{4,5},{5,4},{6,7},{7,6},{8,9},{9,8},{10,11... | collective-permute-start | bytes 196616 | tf_op jit(solution)/shard_map/ppermute | solution.py:22
  38.6 1.8 %collective-permute-start.17 = (bf16[80,256]{1,0:T(8,128)(2,1)S(1)}, bf16[80,256]{1,0:T(8,128)(2,1)S(1)}, u32[]{:S(2)}, u32[]{:S(2)}) collective-permute-start(bf16[80,256]{1,0:T(8,128)(2,1)S(1)} %sum_shares.3.left_ref), channel_id=1, source_target_pairs={{0,1},{1,0},{2,3},{3,2},{4,5},{5,4},{6,7},{7,6},{8,9},{9,8},{10,11... | collective-permute-start | bytes 122888 | tf_op jit(solution)/shard_map/ppermute | solution.py:22
  41.8 0.9 %collective-permute-done.17.right_ref = bf16[80,256]{1,0:T(8,128)(2,1)S(1)} collective-permute-done((bf16[80,256]{1,0:T(8,128)(2,1)S(1)}, bf16[80,256]{1,0:T(8,128)(2,1)S(1)}, u32[]{:S(2)}, u32[]{:S(2)}) %collective-permute-start.17) | collective-permute-done | bytes 40992 | tf_op jit(solution)/shard_map/ppermute | solution.py:22
  43.2 0.8 %backward_keep.1 = (f32[256,256]{1,0:T(8,128)S(1)}, f32[1,256]{1,0:T(1,128)}) custom-call(bf16[1024,512]{1,0:T(8,128)(2,1)S(1)} %build_panel.1.after_ref.panel_ref, bf16[80,256]{1,0:T(8,128)(2,1)S(1)} %sum_shares.3.left_ref, bf16[80,256]{1,0:T(8,128)(2,1)S(1)} %collective-permute-done.17.right_ref, bf16[128,256]{1,0:T(8,128)(2,1)S(1)} %get-tuple-element.37.refs_0_, ...), custom_call_target="tpu_custom_call" | custom-call | tf_op jit(solution)/shard_map/backward_keep/pallas_call | solution.py:344
  44.6 2.2 %collective-permute-start.24 = (bf16[256,256]{1,0:T(8,128)(2,1)S(1)}, bf16[256,256]{1,0:T(8,128)(2,1)S(1)}, u32[]{:S(2)}, u32[]{:S(2)}) collective-permute-start(bf16[256,256]{1,0:T(8,128)(2,1)S(1)} %get-tuple-element.40.sent_ref), channel_id=1, source_target_pairs={{0,16},{8,24},{16,0},{24,8},{1,17},{9,25},{17,1},{25,9},{2,18},{10... | collective-permute-start | bytes 393224 | tf_op jit(solution)/shard_map/ppermute | solution.py:22
  46.8 3.8 %collective-permute-done.24.arrived_ref = bf16[256,256]{1,0:T(8,128)(2,1)S(1)} collective-permute-done((bf16[256,256]{1,0:T(8,128)(2,1)S(1)}, bf16[256,256]{1,0:T(8,128)(2,1)S(1)}, u32[]{:S(2)}, u32[]{:S(2)}) %collective-permute-start.24) | collective-permute-done | bytes 131104 | tf_op jit(solution)/shard_map/ppermute | solution.py:22
  (49 shorter events, 7.9 us)
Async XLA Ops:
  0.6 5.9 %collective-permute-start.1 = (bf16[128,256]{1,0:T(8,128)(2,1)}, bf16[128,256]{1,0:T(8,128)(2,1)S(1)}, u32[]{:S(2)}, u32[]{:S(2)}) collective-permute-start(bf16[128,256]{1,0:T(8,128)(2,1)} %refs_0_.3), channel_id=1, source_target_pairs={{0,16},{8,24},{16,0},{24,8},{1,17},{9,25},{17,1},{25,9},{2,18},{10... | collective-permute-start | bytes 196616 | tf_op jit(solution)/shard_map/ppermute | solution.py:22
  3.6 3.5 %collective-permute-start = (bf16[128,256]{1,0:T(8,128)(2,1)}, bf16[128,256]{1,0:T(8,128)(2,1)S(1)}, u32[]{:S(2)}, u32[]{:S(2)}) collective-permute-start(bf16[128,256]{1,0:T(8,128)(2,1)} %refs_0_.3), channel_id=1, source_target_pairs={{0,8},{8,0},{16,24},{24,16},{1,9},{9,1},{17,25},{25,17},{2,10},{10... | collective-permute-start | bytes 196616 | tf_op jit(solution)/shard_map/ppermute | solution.py:22
  6.6 1.5 %collective-permute-start.2 = (bf16[128,256]{1,0:T(8,128)(2,1)S(1)}, bf16[128,256]{1,0:T(8,128)(2,1)S(1)}, u32[]{:S(2)}, u32[]{:S(2)}) collective-permute-start(bf16[128,256]{1,0:T(8,128)(2,1)S(1)} %copy_block.1), channel_id=1, source_target_pairs={{0,8},{8,0},{16,24},{24,16},{1,9},{9,1},{17,25},{25,17},{2,10},{10... | collective-permute-start | bytes 196616 | tf_op jit(solution)/shard_map/ppermute | solution.py:22
  8.4 4.6 %collective-permute-start.5 = (bf16[128,256]{1,0:T(8,128)(2,1)S(1)}, bf16[128,256]{1,0:T(8,128)(2,1)S(1)}, u32[]{:S(2)}, u32[]{:S(2)}) collective-permute-start(bf16[128,256]{1,0:T(8,128)(2,1)S(1)} %get-tuple-element.27), channel_id=1, source_target_pairs={{0,1},{1,0},{2,3},{3,2},{4,5},{5,4},{6,7},{7,6},{8,9},{9,8},{10,11... | collective-permute-start | bytes 196616 | tf_op jit(solution)/shard_map/ppermute | solution.py:22
  10.0 6.7 %collective-permute-start.3 = (bf16[128,256]{1,0:T(8,128)(2,1)S(1)}, bf16[128,256]{1,0:T(8,128)(2,1)S(1)}, u32[]{:S(2)}, u32[]{:S(2)}) collective-permute-start(bf16[128,256]{1,0:T(8,128)(2,1)S(1)} %get-tuple-element.25), channel_id=1, source_target_pairs={{0,1},{1,0},{2,3},{3,2},{4,5},{5,4},{6,7},{7,6},{8,9},{9,8},{10,11... | collective-permute-start | bytes 196616 | tf_op jit(solution)/shard_map/ppermute | solution.py:22
  10.5 7.1 %collective-permute-start.7 = (bf16[128,256]{1,0:T(8,128)(2,1)S(1)}, bf16[128,256]{1,0:T(8,128)(2,1)S(1)}, u32[]{:S(2)}, u32[]{:S(2)}) collective-permute-start(bf16[128,256]{1,0:T(8,128)(2,1)S(1)} %get-tuple-element.29), channel_id=1, source_target_pairs={{0,1},{1,0},{2,3},{3,2},{4,5},{5,4},{6,7},{7,6},{8,9},{9,8},{10,11... | collective-permute-start | bytes 196616 | tf_op jit(solution)/shard_map/ppermute | solution.py:22
  12.0 7.3 %collective-permute-start.9 = (bf16[128,256]{1,0:T(8,128)(2,1)S(1)}, bf16[128,256]{1,0:T(8,128)(2,1)S(1)}, u32[]{:S(2)}, u32[]{:S(2)}) collective-permute-start(bf16[128,256]{1,0:T(8,128)(2,1)S(1)} %get-tuple-element.31), channel_id=1, source_target_pairs={{0,1},{1,0},{2,3},{3,2},{4,5},{5,4},{6,7},{7,6},{8,9},{9,8},{10,11... | collective-permute-start | bytes 196616 | tf_op jit(solution)/shard_map/ppermute | solution.py:22
  13.0 6.9 %collective-permute-start.6 = (bf16[128,256]{1,0:T(8,128)(2,1)S(1)}, bf16[128,256]{1,0:T(8,128)(2,1)S(1)}, u32[]{:S(2)}, u32[]{:S(2)}) collective-permute-start(bf16[128,256]{1,0:T(8,128)(2,1)S(1)} %add_convert_fusion.1), channel_id=1, source_target_pairs={{0,6},{1,7},{2,4},{3,5},{4,2},{5,3},{6,0},{7,1},{8,14},{9,15},{10,... | collective-permute-start | bytes 196616 | tf_op jit(solution)/shard_map/ppermute | solution.py:22
  16.7 5.6 %collective-permute-start.4 = (bf16[128,256]{1,0:T(8,128)(2,1)S(1)}, bf16[128,256]{1,0:T(8,128)(2,1)S(1)}, u32[]{:S(2)}, u32[]{:S(2)}) collective-permute-start(bf16[128,256]{1,0:T(8,128)(2,1)S(1)} %add_convert_fusion.2), channel_id=1, source_target_pairs={{0,4},{1,5},{2,6},{3,7},{4,0},{5,1},{6,2},{7,3},{8,12},{9,13},{10,... | collective-permute-start | bytes 196616 | tf_op jit(solution)/shard_map/ppermute | solution.py:22
  17.6 5.0 %collective-permute-start.8 = (bf16[128,256]{1,0:T(8,128)(2,1)S(1)}, bf16[128,256]{1,0:T(8,128)(2,1)S(1)}, u32[]{:S(2)}, u32[]{:S(2)}) collective-permute-start(bf16[128,256]{1,0:T(8,128)(2,1)S(1)} %add_convert_fusion), channel_id=1, source_target_pairs={{0,2},{1,3},{2,0},{3,1},{4,6},{5,7},{6,4},{7,5},{8,10},{9,11},{10,... | collective-permute-start | bytes 196616 | tf_op jit(solution)/shard_map/ppermute | solution.py:22
  23.5 7.1 %collective-permute-start.12 = (bf16[128,256]{1,0:T(8,128)(2,1)S(1)}, bf16[128,256]{1,0:T(8,128)(2,1)S(1)}, u32[]{:S(2)}, u32[]{:S(2)}) collective-permute-start(bf16[128,256]{1,0:T(8,128)(2,1)S(1)} %get-tuple-element.37.refs_0_), channel_id=1, source_target_pairs={{0,4},{1,5},{2,6},{3,7},{4,0},{5,1},{6,2},{7,3},{8,12},{9,13},{10,... | collective-permute-start | bytes 196616 | tf_op jit(solution)/shard_map/ppermute | solution.py:22
  25.0 5.7 %collective-permute-start.11 = (bf16[80,256]{1,0:T(8,128)(2,1)S(1)}, bf16[80,256]{1,0:T(8,128)(2,1)S(1)}, u32[]{:S(2)}, u32[]{:S(2)}) collective-permute-start(bf16[80,256]{1,0:T(8,128)(2,1)S(1)} %get-tuple-element.36), channel_id=1, source_target_pairs={{0,16},{8,24},{16,0},{24,8},{1,17},{9,25},{17,1},{25,9},{2,18},{10... | collective-permute-start | bytes 122888 | tf_op jit(solution)/shard_map/ppermute | solution.py:22
  26.4 7.2 %collective-permute-start.21 = (bf16[128,256]{1,0:T(8,128)(2,1)S(1)}, bf16[128,256]{1,0:T(8,128)(2,1)S(1)}, u32[]{:S(2)}, u32[]{:S(2)}) collective-permute-start(bf16[128,256]{1,0:T(8,128)(2,1)S(1)} %get-tuple-element.37.refs_0_), channel_id=1, source_target_pairs={{0,6},{1,7},{2,4},{3,5},{4,2},{5,3},{6,0},{7,1},{8,14},{9,15},{10,... | collective-permute-start | bytes 196616 | tf_op jit(solution)/shard_map/ppermute | solution.py:22
  28.6 6.5 %collective-permute-start.18 = (bf16[128,256]{1,0:T(8,128)(2,1)S(1)}, bf16[128,256]{1,0:T(8,128)(2,1)S(1)}, u32[]{:S(2)}, u32[]{:S(2)}) collective-permute-start(bf16[128,256]{1,0:T(8,128)(2,1)S(1)} %get-tuple-element.37.refs_0_), channel_id=1, source_target_pairs={{0,2},{1,3},{2,0},{3,1},{4,6},{5,7},{6,4},{7,5},{8,10},{9,11},{10,... | collective-permute-start | bytes 196616 | tf_op jit(solution)/shard_map/ppermute | solution.py:22
  28.6 7.9 %collective-permute-start.16 = (bf16[128,256]{1,0:T(8,128)(2,1)S(1)}, bf16[128,256]{1,0:T(8,128)(2,1)S(1)}, u32[]{:S(2)}, u32[]{:S(2)}) collective-permute-start(bf16[128,256]{1,0:T(8,128)(2,1)S(1)} %get-tuple-element.37.refs_0_), channel_id=1, source_target_pairs={{0,1},{1,0},{2,3},{3,2},{4,5},{5,4},{6,7},{7,6},{8,9},{9,8},{10,11... | collective-permute-start | bytes 196616 | tf_op jit(solution)/shard_map/ppermute | solution.py:22
  30.7 6.5 %collective-permute-start.15 = (bf16[80,256]{1,0:T(8,128)(2,1)S(1)}, bf16[80,256]{1,0:T(8,128)(2,1)S(1)}, u32[]{:S(2)}, u32[]{:S(2)}) collective-permute-start(bf16[80,256]{1,0:T(8,128)(2,1)S(1)} %sum_shares.2.refs_0_), channel_id=1, source_target_pairs={{0,6},{1,7},{2,4},{3,5},{4,2},{5,3},{6,0},{7,1},{8,14},{9,15},{10,... | collective-permute-start | bytes 122888 | tf_op jit(solution)/shard_map/ppermute | solution.py:22
  32.8 5.8 %collective-permute-start.14 = (bf16[80,256]{1,0:T(8,128)(2,1)S(1)}, bf16[80,256]{1,0:T(8,128)(2,1)S(1)}, u32[]{:S(2)}, u32[]{:S(2)}) collective-permute-start(bf16[80,256]{1,0:T(8,128)(2,1)S(1)} %sum_shares.2.refs_0_), channel_id=1, source_target_pairs={{0,4},{1,5},{2,6},{3,7},{4,0},{5,1},{6,2},{7,3},{8,12},{9,13},{10,... | collective-permute-start | bytes 122888 | tf_op jit(solution)/shard_map/ppermute | solution.py:22
  33.6 5.0 %collective-permute-start.13 = (bf16[80,256]{1,0:T(8,128)(2,1)S(1)}, bf16[80,256]{1,0:T(8,128)(2,1)S(1)}, u32[]{:S(2)}, u32[]{:S(2)}) collective-permute-start(bf16[80,256]{1,0:T(8,128)(2,1)S(1)} %sum_shares.2.refs_0_), channel_id=1, source_target_pairs={{0,2},{1,3},{2,0},{3,1},{4,6},{5,7},{6,4},{7,5},{8,10},{9,11},{10,... | collective-permute-start | bytes 122888 | tf_op jit(solution)/shard_map/ppermute | solution.py:22
  35.2 5.3 %collective-permute-start.22 = (bf16[128,256]{1,0:T(8,128)(2,1)S(1)}, bf16[128,256]{1,0:T(8,128)(2,1)S(1)}, u32[]{:S(2)}, u32[]{:S(2)}) collective-permute-start(bf16[128,256]{1,0:T(8,128)(2,1)S(1)} %collective-permute-done.21.refs_6_), channel_id=1, source_target_pairs={{0,1},{1,0},{2,3},{3,2},{4,5},{5,4},{6,7},{7,6},{8,9},{9,8},{10,11... | collective-permute-start | bytes 196616 | tf_op jit(solution)/shard_map/ppermute | solution.py:22
  36.5 4.5 %collective-permute-start.19 = (bf16[128,256]{1,0:T(8,128)(2,1)S(1)}, bf16[128,256]{1,0:T(8,128)(2,1)S(1)}, u32[]{:S(2)}, u32[]{:S(2)}) collective-permute-start(bf16[128,256]{1,0:T(8,128)(2,1)S(1)} %collective-permute-done.18.refs_2_), channel_id=1, source_target_pairs={{0,1},{1,0},{2,3},{3,2},{4,5},{5,4},{6,7},{7,6},{8,9},{9,8},{10,11... | collective-permute-start | bytes 196616 | tf_op jit(solution)/shard_map/ppermute | solution.py:22
  37.2 4.6 %collective-permute-start.20 = (bf16[128,256]{1,0:T(8,128)(2,1)S(1)}, bf16[128,256]{1,0:T(8,128)(2,1)S(1)}, u32[]{:S(2)}, u32[]{:S(2)}) collective-permute-start(bf16[128,256]{1,0:T(8,128)(2,1)S(1)} %collective-permute-done.12.refs_2_.refs_4_), channel_id=1, source_target_pairs={{0,1},{1,0},{2,3},{3,2},{4,5},{5,4},{6,7},{7,6},{8,9},{9,8},{10,11... | collective-permute-start | bytes 196616 | tf_op jit(solution)/shard_map/ppermute | solution.py:22
  38.6 4.1 %collective-permute-start.17 = (bf16[80,256]{1,0:T(8,128)(2,1)S(1)}, bf16[80,256]{1,0:T(8,128)(2,1)S(1)}, u32[]{:S(2)}, u32[]{:S(2)}) collective-permute-start(bf16[80,256]{1,0:T(8,128)(2,1)S(1)} %sum_shares.3.left_ref), channel_id=1, source_target_pairs={{0,1},{1,0},{2,3},{3,2},{4,5},{5,4},{6,7},{7,6},{8,9},{9,8},{10,11... | collective-permute-start | bytes 122888 | tf_op jit(solution)/shard_map/ppermute | solution.py:22
  43.1 1.5 %collective-permute-start.23 = (bf16[320,256]{1,0:T(8,128)(2,1)S(1)}, bf16[320,256]{1,0:T(8,128)(2,1)S(1)}, u32[]{:S(2)}, u32[]{:S(2)}) collective-permute-start(bf16[320,256]{1,0:T(8,128)(2,1)S(1)} %backward_send.1.sent_ref), channel_id=1, source_target_pairs={{0,8},{8,0},{16,24},{24,16},{1,9},{9,1},{17,25},{25,17},{2,10},{10... | collective-permute-start | bytes 491528 | tf_op jit(solution)/shard_map/ppermute | solution.py:22
  44.6 6.0 %collective-permute-start.24 = (bf16[256,256]{1,0:T(8,128)(2,1)S(1)}, bf16[256,256]{1,0:T(8,128)(2,1)S(1)}, u32[]{:S(2)}, u32[]{:S(2)}) collective-permute-start(bf16[256,256]{1,0:T(8,128)(2,1)S(1)} %get-tuple-element.40.sent_ref), channel_id=1, source_target_pairs={{0,16},{8,24},{16,0},{24,8},{1,17},{9,25},{17,1},{25,9},{2,18},{10... | collective-permute-start | bytes 393224 | tf_op jit(solution)/shard_map/ppermute | solution.py:22
  (5 other events, 57.3 us)

commit v5 on v4

--- a/solution.py
+++ b/solution.py
@@ -80,7 +80,7 @@
 
 
 def peers(count):
-    return sorted(range(2, count, 2), key=lambda d: (abs(d - count // 2 - 0.5), d)) + [0]
+    return sorted(range(2, count, 2), key=lambda d: (abs(d - count // 2 - 1.5), d)) + [0]
 
 
 def copy_kernel(block_ref, after_ref, out_ref):

time: 51.5 us -> 50.9 us (0.988)
  starting transfers between devices: 32.4 us -> 30.8 us
  waiting for transfers between devices: 11.7 us -> 12.6 us
    ppermute x25, starting transfers between devices: 32.4 us -> 30.8 us  [swapped(): return lax.ppermute(block, axis, [(i, i ^ bit) for i in range(n)])]
    ppermute x25, waiting for transfers between devices: 11.7 us -> 12.6 us  [swapped(): return lax.ppermute(block, axis, [(i, i ^ bit) for i in range(n)])]
  transfers between devices with their start and end apart: 25 -> 25, of which waited for: 11 -> 10; matrix products, arithmetic and copies ran while one was open for 0% -> 0% of each run, Pallas kernels for 7% -> 7%
where the time goes in v5:
time: 50.9 us; the launch traced here: 50.7 us
  starting transfers between devices  30.8 us (61%)
  waiting for transfers between devices  12.6 us (25%)
  Pallas kernels  5.81 us (11%)
  between operations  1.44 us (3%)
    ppermute x25, starting transfers between devices, swapped(): return lax.ppermute(block, axis, [(i, i ^ bit) for i in range(n)])  30.8 us
    ppermute x25, waiting for transfers between devices, swapped(): return lax.ppermute(block, axis, [(i, i ^ bit) for i in range(n)])  12.6 us
    pallas_call x1, Pallas kernels, build_panel(): pl.pallas_call(functools.partial(build_kernel, col_tiles), out_shape=jax....  2.21 us
  transfers between devices with their start and end apart: 25, of which 10 were waited for; matrix products, arithmetic and copies ran while one was open for 0% of the time, Pallas kernels for 7%

profile of v5, /device:TPU:0, one launch (start us, length us, event | category | flops | bytes accessed | tf_op | source)
XLA Modules:
  0.0 50.7 jit_solution(5788172899966005897)
XLA Ops:
  0.6 3.0 %collective-permute-start.1 = (bf16[128,256]{1,0:T(8,128)(2,1)}, bf16[128,256]{1,0:T(8,128)(2,1)S(1)}, u32[]{:S(2)}, u32[]{:S(2)}) collective-permute-start(bf16[128,256]{1,0:T(8,128)(2,1)} %refs_0_.3), channel_id=1, source_target_pairs={{0,16},{8,24},{16,0},{24,8},{1,17},{9,25},{17,1},{25,9},{2,18},{10... | collective-permute-start | bytes 196616 | tf_op jit(solution)/shard_map/ppermute | solution.py:22
  4.3 2.2 %build_panel.1.after_ref.panel_ref = bf16[1024,512]{1,0:T(8,128)(2,1)S(1)} custom-call(s32[1,96]{1,0:T(1,128)} %bitcast.6, s32[1,1]{1,0:T(1,128)S(6)} %copy.11.count_ref, bf16[96,128,128]{2,1,0:T(8,128)(2,1)} %bitcast.5), custom_call_target="tpu_custom_call" | custom-call | flops 1572864 | bytes 3145728 | tf_op jit(solution)/shard_map/build_panel/pallas_call | solution.py:62
  7.2 0.9 %collective-permute-done.2.refs_3_ = bf16[128,256]{1,0:T(8,128)(2,1)S(1)} collective-permute-done((bf16[128,256]{1,0:T(8,128)(2,1)S(1)}, bf16[128,256]{1,0:T(8,128)(2,1)S(1)}, u32[]{:S(2)}, u32[]{:S(2)}) %collective-permute-start.2) | collective-permute-done | bytes 65568 | tf_op jit(solution)/shard_map/ppermute | solution.py:22
  8.5 1.5 %collective-permute-start.5 = (bf16[128,256]{1,0:T(8,128)(2,1)S(1)}, bf16[128,256]{1,0:T(8,128)(2,1)S(1)}, u32[]{:S(2)}, u32[]{:S(2)}) collective-permute-start(bf16[128,256]{1,0:T(8,128)(2,1)S(1)} %get-tuple-element.27), channel_id=1, source_target_pairs={{0,1},{1,0},{2,3},{3,2},{4,5},{5,4},{6,7},{7,6},{8,9},{9,8},{10,11... | collective-permute-start | bytes 196616 | tf_op jit(solution)/shard_map/ppermute | solution.py:22
  10.6 1.5 %collective-permute-start.7 = (bf16[128,256]{1,0:T(8,128)(2,1)S(1)}, bf16[128,256]{1,0:T(8,128)(2,1)S(1)}, u32[]{:S(2)}, u32[]{:S(2)}) collective-permute-start(bf16[128,256]{1,0:T(8,128)(2,1)S(1)} %get-tuple-element.29), channel_id=1, source_target_pairs={{0,1},{1,0},{2,3},{3,2},{4,5},{5,4},{6,7},{7,6},{8,9},{9,8},{10,11... | collective-permute-start | bytes 196616 | tf_op jit(solution)/shard_map/ppermute | solution.py:22
  13.2 2.5 %collective-permute-start.6 = (bf16[128,256]{1,0:T(8,128)(2,1)S(1)}, bf16[128,256]{1,0:T(8,128)(2,1)S(1)}, u32[]{:S(2)}, u32[]{:S(2)}) collective-permute-start(bf16[128,256]{1,0:T(8,128)(2,1)S(1)} %add_convert_fusion.1), channel_id=1, source_target_pairs={{0,4},{1,5},{2,6},{3,7},{4,0},{5,1},{6,2},{7,3},{8,12},{9,13},{10,... | collective-permute-start | bytes 196616 | tf_op jit(solution)/shard_map/ppermute | solution.py:22
  15.7 2.9 %collective-permute-start.4 = (bf16[128,256]{1,0:T(8,128)(2,1)S(1)}, bf16[128,256]{1,0:T(8,128)(2,1)S(1)}, u32[]{:S(2)}, u32[]{:S(2)}) collective-permute-start(bf16[128,256]{1,0:T(8,128)(2,1)S(1)} %add_convert_fusion.2), channel_id=1, source_target_pairs={{0,6},{1,7},{2,4},{3,5},{4,2},{5,3},{6,0},{7,1},{8,14},{9,15},{10,... | collective-permute-start | bytes 196616 | tf_op jit(solution)/shard_map/ppermute | solution.py:22
  18.8 3.2 %collective-permute-done.4.refs_0_ = bf16[128,256]{1,0:T(8,128)(2,1)S(1)} collective-permute-done((bf16[128,256]{1,0:T(8,128)(2,1)S(1)}, bf16[128,256]{1,0:T(8,128)(2,1)S(1)}, u32[]{:S(2)}, u32[]{:S(2)}) %collective-permute-start.4) | collective-permute-done | bytes 65568 | tf_op jit(solution)/shard_map/ppermute | solution.py:22
  22.0 1.0 %collective-permute-done.8.refs_2_ = bf16[128,256]{1,0:T(8,128)(2,1)S(1)} collective-permute-done((bf16[128,256]{1,0:T(8,128)(2,1)S(1)}, bf16[128,256]{1,0:T(8,128)(2,1)S(1)}, u32[]{:S(2)}, u32[]{:S(2)}) %collective-permute-start.8) | collective-permute-done | bytes 65568 | tf_op jit(solution)/shard_map/ppermute | solution.py:22
  23.0 0.8 %dense_stage.1 = (bf16[128,256]{1,0:T(8,128)(2,1)}, bf16[128,256]{1,0:T(8,128)(2,1)S(1)}, bf16[144,256]{1,0:T(8,128)(2,1)S(1)}, bf16[144,256]{1,0:T(8,128)(2,1)S(1)}) custom-call(bf16[256,256]{1,0:T(8,128)(2,1)S(1)} %copy-done.1, f32[1,256]{1,0:T(1,128)S(1)} %bitcast.4, bf16[128,256]{1,0:T(8,128)(2,1)S(1)} %copy-done.2, ...), custom_call_target="tpu_custom_call" | custom-call | tf_op jit(solution)/shard_map/dense_stage/pallas_call | solution.py:180
  23.8 2.1 %collective-permute-start.12 = (bf16[128,256]{1,0:T(8,128)(2,1)S(1)}, bf16[128,256]{1,0:T(8,128)(2,1)S(1)}, u32[]{:S(2)}, u32[]{:S(2)}) collective-permute-start(bf16[128,256]{1,0:T(8,128)(2,1)S(1)} %get-tuple-element.37.refs_0_), channel_id=1, source_target_pairs={{0,6},{1,7},{2,4},{3,5},{4,2},{5,3},{6,0},{7,1},{8,14},{9,15},{10,... | collective-permute-start | bytes 196616 | tf_op jit(solution)/shard_map/ppermute | solution.py:22
  25.9 1.2 %collective-permute-start.11 = (bf16[80,256]{1,0:T(8,128)(2,1)S(1)}, bf16[80,256]{1,0:T(8,128)(2,1)S(1)}, u32[]{:S(2)}, u32[]{:S(2)}) collective-permute-start(bf16[80,256]{1,0:T(8,128)(2,1)S(1)} %get-tuple-element.36), channel_id=1, source_target_pairs={{0,16},{8,24},{16,0},{24,8},{1,17},{9,25},{17,1},{25,9},{2,18},{10... | collective-permute-start | bytes 122888 | tf_op jit(solution)/shard_map/ppermute | solution.py:22
  27.4 2.3 %collective-permute-start.18 = (bf16[128,256]{1,0:T(8,128)(2,1)S(1)}, bf16[128,256]{1,0:T(8,128)(2,1)S(1)}, u32[]{:S(2)}, u32[]{:S(2)}) collective-permute-start(bf16[128,256]{1,0:T(8,128)(2,1)S(1)} %get-tuple-element.37.refs_0_), channel_id=1, source_target_pairs={{0,2},{1,3},{2,0},{3,1},{4,6},{5,7},{6,4},{7,5},{8,10},{9,11},{10,... | collective-permute-start | bytes 196616 | tf_op jit(solution)/shard_map/ppermute | solution.py:22
  29.7 1.5 %collective-permute-start.16 = (bf16[128,256]{1,0:T(8,128)(2,1)S(1)}, bf16[128,256]{1,0:T(8,128)(2,1)S(1)}, u32[]{:S(2)}, u32[]{:S(2)}) collective-permute-start(bf16[128,256]{1,0:T(8,128)(2,1)S(1)} %get-tuple-element.37.refs_0_), channel_id=1, source_target_pairs={{0,1},{1,0},{2,3},{3,2},{4,5},{5,4},{6,7},{7,6},{8,9},{9,8},{10,11... | collective-permute-start | bytes 196616 | tf_op jit(solution)/shard_map/ppermute | solution.py:22
  31.2 2.2 %collective-permute-start.15 = (bf16[80,256]{1,0:T(8,128)(2,1)S(1)}, bf16[80,256]{1,0:T(8,128)(2,1)S(1)}, u32[]{:S(2)}, u32[]{:S(2)}) collective-permute-start(bf16[80,256]{1,0:T(8,128)(2,1)S(1)} %sum_shares.2.refs_0_), channel_id=1, source_target_pairs={{0,6},{1,7},{2,4},{3,5},{4,2},{5,3},{6,0},{7,1},{8,14},{9,15},{10,... | collective-permute-start | bytes 122888 | tf_op jit(solution)/shard_map/ppermute | solution.py:22
  33.4 2.3 %collective-permute-start.13 = (bf16[80,256]{1,0:T(8,128)(2,1)S(1)}, bf16[80,256]{1,0:T(8,128)(2,1)S(1)}, u32[]{:S(2)}, u32[]{:S(2)}) collective-permute-start(bf16[80,256]{1,0:T(8,128)(2,1)S(1)} %sum_shares.2.refs_0_), channel_id=1, source_target_pairs={{0,2},{1,3},{2,0},{3,1},{4,6},{5,7},{6,4},{7,5},{8,10},{9,11},{10,... | collective-permute-start | bytes 122888 | tf_op jit(solution)/shard_map/ppermute | solution.py:22
  36.3 1.4 %collective-permute-start.19 = (bf16[128,256]{1,0:T(8,128)(2,1)S(1)}, bf16[128,256]{1,0:T(8,128)(2,1)S(1)}, u32[]{:S(2)}, u32[]{:S(2)}) collective-permute-start(bf16[128,256]{1,0:T(8,128)(2,1)S(1)} %collective-permute-done.18.refs_2_), channel_id=1, source_target_pairs={{0,1},{1,0},{2,3},{3,2},{4,5},{5,4},{6,7},{7,6},{8,9},{9,8},{10,11... | collective-permute-start | bytes 196616 | tf_op jit(solution)/shard_map/ppermute | solution.py:22
  38.4 1.4 %collective-permute-start.17 = (bf16[80,256]{1,0:T(8,128)(2,1)S(1)}, bf16[80,256]{1,0:T(8,128)(2,1)S(1)}, u32[]{:S(2)}, u32[]{:S(2)}) collective-permute-start(bf16[80,256]{1,0:T(8,128)(2,1)S(1)} %sum_shares.3.left_ref), channel_id=1, source_target_pairs={{0,1},{1,0},{2,3},{3,2},{4,5},{5,4},{6,7},{7,6},{8,9},{9,8},{10,11... | collective-permute-start | bytes 122888 | tf_op jit(solution)/shard_map/ppermute | solution.py:22
  40.0 0.7 %collective-permute-done.19.refs_3_ = bf16[128,256]{1,0:T(8,128)(2,1)S(1)} collective-permute-done((bf16[128,256]{1,0:T(8,128)(2,1)S(1)}, bf16[128,256]{1,0:T(8,128)(2,1)S(1)}, u32[]{:S(2)}, u32[]{:S(2)}) %collective-permute-start.19) | collective-permute-done | bytes 65568 | tf_op jit(solution)/shard_map/ppermute | solution.py:22
  40.7 1.2 %collective-permute-done.22.refs_7_ = bf16[128,256]{1,0:T(8,128)(2,1)S(1)} collective-permute-done((bf16[128,256]{1,0:T(8,128)(2,1)S(1)}, bf16[128,256]{1,0:T(8,128)(2,1)S(1)}, u32[]{:S(2)}, u32[]{:S(2)}) %collective-permute-start.22) | collective-permute-done | bytes 65568 | tf_op jit(solution)/shard_map/ppermute | solution.py:22
  43.0 0.8 %backward_keep.1 = (f32[256,256]{1,0:T(8,128)S(1)}, f32[1,256]{1,0:T(1,128)}) custom-call(bf16[1024,512]{1,0:T(8,128)(2,1)S(1)} %build_panel.1.after_ref.panel_ref, bf16[80,256]{1,0:T(8,128)(2,1)S(1)} %sum_shares.3.left_ref, bf16[80,256]{1,0:T(8,128)(2,1)S(1)} %collective-permute-done.17.right_ref, bf16[128,256]{1,0:T(8,128)(2,1)S(1)} %get-tuple-element.37.refs_0_, ...), custom_call_target="tpu_custom_call" | custom-call | tf_op jit(solution)/shard_map/backward_keep/pallas_call | solution.py:344
  44.4 1.6 %collective-permute-start.24 = (bf16[256,256]{1,0:T(8,128)(2,1)S(1)}, bf16[256,256]{1,0:T(8,128)(2,1)S(1)}, u32[]{:S(2)}, u32[]{:S(2)}) collective-permute-start(bf16[256,256]{1,0:T(8,128)(2,1)S(1)} %get-tuple-element.40.sent_ref), channel_id=1, source_target_pairs={{0,16},{8,24},{16,0},{24,8},{1,17},{9,25},{17,1},{25,9},{2,18},{10... | collective-permute-start | bytes 393224 | tf_op jit(solution)/shard_map/ppermute | solution.py:22
  46.0 4.0 %collective-permute-done.24.arrived_ref = bf16[256,256]{1,0:T(8,128)(2,1)S(1)} collective-permute-done((bf16[256,256]{1,0:T(8,128)(2,1)S(1)}, bf16[256,256]{1,0:T(8,128)(2,1)S(1)}, u32[]{:S(2)}, u32[]{:S(2)}) %collective-permute-start.24) | collective-permute-done | bytes 131104 | tf_op jit(solution)/shard_map/ppermute | solution.py:22
  50.0 0.8 %final_sums.1 = (bf16[128,256]{1,0:T(8,128)(2,1)}, f32[256,256]{1,0:T(8,128)}) custom-call(f32[128,256]{1,0:T(8,128)S(1)} %get-tuple-element.39.keep_ref, bf16[256,256]{1,0:T(8,128)(2,1)S(1)} %get-tuple-element.40.sent_ref, bf16[256,256]{1,0:T(8,128)(2,1)S(1)} %collective-permute-done.24.arrived_ref), custom_call_target="tpu_custom_call" | custom-call | tf_op jit(solution)/shard_map/final_sums/pallas_call | solution.py:283
  (49 shorter events, 6.3 us)
Async XLA Ops:
  0.6 5.9 %collective-permute-start.1 = (bf16[128,256]{1,0:T(8,128)(2,1)}, bf16[128,256]{1,0:T(8,128)(2,1)S(1)}, u32[]{:S(2)}, u32[]{:S(2)}) collective-permute-start(bf16[128,256]{1,0:T(8,128)(2,1)} %refs_0_.3), channel_id=1, source_target_pairs={{0,16},{8,24},{16,0},{24,8},{1,17},{9,25},{17,1},{25,9},{2,18},{10... | collective-permute-start | bytes 196616 | tf_op jit(solution)/shard_map/ppermute | solution.py:22
  3.6 3.6 %collective-permute-start = (bf16[128,256]{1,0:T(8,128)(2,1)}, bf16[128,256]{1,0:T(8,128)(2,1)S(1)}, u32[]{:S(2)}, u32[]{:S(2)}) collective-permute-start(bf16[128,256]{1,0:T(8,128)(2,1)} %refs_0_.3), channel_id=1, source_target_pairs={{0,8},{8,0},{16,24},{24,16},{1,9},{9,1},{17,25},{25,17},{2,10},{10... | collective-permute-start | bytes 196616 | tf_op jit(solution)/shard_map/ppermute | solution.py:22
  6.6 1.5 %collective-permute-start.2 = (bf16[128,256]{1,0:T(8,128)(2,1)S(1)}, bf16[128,256]{1,0:T(8,128)(2,1)S(1)}, u32[]{:S(2)}, u32[]{:S(2)}) collective-permute-start(bf16[128,256]{1,0:T(8,128)(2,1)S(1)} %copy_block.1), channel_id=1, source_target_pairs={{0,8},{8,0},{16,24},{24,16},{1,9},{9,1},{17,25},{25,17},{2,10},{10... | collective-permute-start | bytes 196616 | tf_op jit(solution)/shard_map/ppermute | solution.py:22
  8.5 4.7 %collective-permute-start.5 = (bf16[128,256]{1,0:T(8,128)(2,1)S(1)}, bf16[128,256]{1,0:T(8,128)(2,1)S(1)}, u32[]{:S(2)}, u32[]{:S(2)}) collective-permute-start(bf16[128,256]{1,0:T(8,128)(2,1)S(1)} %get-tuple-element.27), channel_id=1, source_target_pairs={{0,1},{1,0},{2,3},{3,2},{4,5},{5,4},{6,7},{7,6},{8,9},{9,8},{10,11... | collective-permute-start | bytes 196616 | tf_op jit(solution)/shard_map/ppermute | solution.py:22
  10.0 5.7 %collective-permute-start.3 = (bf16[128,256]{1,0:T(8,128)(2,1)S(1)}, bf16[128,256]{1,0:T(8,128)(2,1)S(1)}, u32[]{:S(2)}, u32[]{:S(2)}) collective-permute-start(bf16[128,256]{1,0:T(8,128)(2,1)S(1)} %get-tuple-element.25), channel_id=1, source_target_pairs={{0,1},{1,0},{2,3},{3,2},{4,5},{5,4},{6,7},{7,6},{8,9},{9,8},{10,11... | collective-permute-start | bytes 196616 | tf_op jit(solution)/shard_map/ppermute | solution.py:22
  10.6 8.1 %collective-permute-start.7 = (bf16[128,256]{1,0:T(8,128)(2,1)S(1)}, bf16[128,256]{1,0:T(8,128)(2,1)S(1)}, u32[]{:S(2)}, u32[]{:S(2)}) collective-permute-start(bf16[128,256]{1,0:T(8,128)(2,1)S(1)} %get-tuple-element.29), channel_id=1, source_target_pairs={{0,1},{1,0},{2,3},{3,2},{4,5},{5,4},{6,7},{7,6},{8,9},{9,8},{10,11... | collective-permute-start | bytes 196616 | tf_op jit(solution)/shard_map/ppermute | solution.py:22
  12.0 6.7 %collective-permute-start.9 = (bf16[128,256]{1,0:T(8,128)(2,1)S(1)}, bf16[128,256]{1,0:T(8,128)(2,1)S(1)}, u32[]{:S(2)}, u32[]{:S(2)}) collective-permute-start(bf16[128,256]{1,0:T(8,128)(2,1)S(1)} %get-tuple-element.31), channel_id=1, source_target_pairs={{0,1},{1,0},{2,3},{3,2},{4,5},{5,4},{6,7},{7,6},{8,9},{9,8},{10,11... | collective-permute-start | bytes 196616 | tf_op jit(solution)/shard_map/ppermute | solution.py:22
  13.2 5.6 %collective-permute-start.6 = (bf16[128,256]{1,0:T(8,128)(2,1)S(1)}, bf16[128,256]{1,0:T(8,128)(2,1)S(1)}, u32[]{:S(2)}, u32[]{:S(2)}) collective-permute-start(bf16[128,256]{1,0:T(8,128)(2,1)S(1)} %add_convert_fusion.1), channel_id=1, source_target_pairs={{0,4},{1,5},{2,6},{3,7},{4,0},{5,1},{6,2},{7,3},{8,12},{9,13},{10,... | collective-permute-start | bytes 196616 | tf_op jit(solution)/shard_map/ppermute | solution.py:22
  15.7 6.2 %collective-permute-start.4 = (bf16[128,256]{1,0:T(8,128)(2,1)S(1)}, bf16[128,256]{1,0:T(8,128)(2,1)S(1)}, u32[]{:S(2)}, u32[]{:S(2)}) collective-permute-start(bf16[128,256]{1,0:T(8,128)(2,1)S(1)} %add_convert_fusion.2), channel_id=1, source_target_pairs={{0,6},{1,7},{2,4},{3,5},{4,2},{5,3},{6,0},{7,1},{8,14},{9,15},{10,... | collective-permute-start | bytes 196616 | tf_op jit(solution)/shard_map/ppermute | solution.py:22
  18.7 4.3 %collective-permute-start.8 = (bf16[128,256]{1,0:T(8,128)(2,1)S(1)}, bf16[128,256]{1,0:T(8,128)(2,1)S(1)}, u32[]{:S(2)}, u32[]{:S(2)}) collective-permute-start(bf16[128,256]{1,0:T(8,128)(2,1)S(1)} %add_convert_fusion), channel_id=1, source_target_pairs={{0,2},{1,3},{2,0},{3,1},{4,6},{5,7},{6,4},{7,5},{8,10},{9,11},{10,... | collective-permute-start | bytes 196616 | tf_op jit(solution)/shard_map/ppermute | solution.py:22
  23.8 2.1 %collective-permute-start.10 = (bf16[144,256]{1,0:T(8,128)(2,1)S(1)}, bf16[144,256]{1,0:T(8,128)(2,1)S(1)}, u32[]{:S(2)}, u32[]{:S(2)}) collective-permute-start(bf16[144,256]{1,0:T(8,128)(2,1)S(1)} %get-tuple-element.34), channel_id=1, source_target_pairs={{0,8},{8,0},{16,24},{24,16},{1,9},{9,1},{17,25},{25,17},{2,10},{10... | collective-permute-start | bytes 221192 | tf_op jit(solution)/shard_map/ppermute | solution.py:22
  23.8 7.3 %collective-permute-start.12 = (bf16[128,256]{1,0:T(8,128)(2,1)S(1)}, bf16[128,256]{1,0:T(8,128)(2,1)S(1)}, u32[]{:S(2)}, u32[]{:S(2)}) collective-permute-start(bf16[128,256]{1,0:T(8,128)(2,1)S(1)} %get-tuple-element.37.refs_0_), channel_id=1, source_target_pairs={{0,6},{1,7},{2,4},{3,5},{4,2},{5,3},{6,0},{7,1},{8,14},{9,15},{10,... | collective-permute-start | bytes 196616 | tf_op jit(solution)/shard_map/ppermute | solution.py:22
  25.9 5.2 %collective-permute-start.11 = (bf16[80,256]{1,0:T(8,128)(2,1)S(1)}, bf16[80,256]{1,0:T(8,128)(2,1)S(1)}, u32[]{:S(2)}, u32[]{:S(2)}) collective-permute-start(bf16[80,256]{1,0:T(8,128)(2,1)S(1)} %get-tuple-element.36), channel_id=1, source_target_pairs={{0,16},{8,24},{16,0},{24,8},{1,17},{9,25},{17,1},{25,9},{2,18},{10... | collective-permute-start | bytes 122888 | tf_op jit(solution)/shard_map/ppermute | solution.py:22
  27.2 6.2 %collective-permute-start.20 = (bf16[128,256]{1,0:T(8,128)(2,1)S(1)}, bf16[128,256]{1,0:T(8,128)(2,1)S(1)}, u32[]{:S(2)}, u32[]{:S(2)}) collective-permute-start(bf16[128,256]{1,0:T(8,128)(2,1)S(1)} %get-tuple-element.37.refs_0_), channel_id=1, source_target_pairs={{0,4},{1,5},{2,6},{3,7},{4,0},{5,1},{6,2},{7,3},{8,12},{9,13},{10,... | collective-permute-start | bytes 196616 | tf_op jit(solution)/shard_map/ppermute | solution.py:22
  27.4 8.3 %collective-permute-start.18 = (bf16[128,256]{1,0:T(8,128)(2,1)S(1)}, bf16[128,256]{1,0:T(8,128)(2,1)S(1)}, u32[]{:S(2)}, u32[]{:S(2)}) collective-permute-start(bf16[128,256]{1,0:T(8,128)(2,1)S(1)} %get-tuple-element.37.refs_0_), channel_id=1, source_target_pairs={{0,2},{1,3},{2,0},{3,1},{4,6},{5,7},{6,4},{7,5},{8,10},{9,11},{10,... | collective-permute-start | bytes 196616 | tf_op jit(solution)/shard_map/ppermute | solution.py:22
  29.7 6.6 %collective-permute-start.16 = (bf16[128,256]{1,0:T(8,128)(2,1)S(1)}, bf16[128,256]{1,0:T(8,128)(2,1)S(1)}, u32[]{:S(2)}, u32[]{:S(2)}) collective-permute-start(bf16[128,256]{1,0:T(8,128)(2,1)S(1)} %get-tuple-element.37.refs_0_), channel_id=1, source_target_pairs={{0,1},{1,0},{2,3},{3,2},{4,5},{5,4},{6,7},{7,6},{8,9},{9,8},{10,11... | collective-permute-start | bytes 196616 | tf_op jit(solution)/shard_map/ppermute | solution.py:22
  31.2 6.5 %collective-permute-start.15 = (bf16[80,256]{1,0:T(8,128)(2,1)S(1)}, bf16[80,256]{1,0:T(8,128)(2,1)S(1)}, u32[]{:S(2)}, u32[]{:S(2)}) collective-permute-start(bf16[80,256]{1,0:T(8,128)(2,1)S(1)} %sum_shares.2.refs_0_), channel_id=1, source_target_pairs={{0,6},{1,7},{2,4},{3,5},{4,2},{5,3},{6,0},{7,1},{8,14},{9,15},{10,... | collective-permute-start | bytes 122888 | tf_op jit(solution)/shard_map/ppermute | solution.py:22
  33.4 5.0 %collective-permute-start.14 = (bf16[80,256]{1,0:T(8,128)(2,1)S(1)}, bf16[80,256]{1,0:T(8,128)(2,1)S(1)}, u32[]{:S(2)}, u32[]{:S(2)}) collective-permute-start(bf16[80,256]{1,0:T(8,128)(2,1)S(1)} %sum_shares.2.refs_0_), channel_id=1, source_target_pairs={{0,4},{1,5},{2,6},{3,7},{4,0},{5,1},{6,2},{7,3},{8,12},{9,13},{10,... | collective-permute-start | bytes 122888 | tf_op jit(solution)/shard_map/ppermute | solution.py:22
  33.4 5.0 %collective-permute-start.13 = (bf16[80,256]{1,0:T(8,128)(2,1)S(1)}, bf16[80,256]{1,0:T(8,128)(2,1)S(1)}, u32[]{:S(2)}, u32[]{:S(2)}) collective-permute-start(bf16[80,256]{1,0:T(8,128)(2,1)S(1)} %sum_shares.2.refs_0_), channel_id=1, source_target_pairs={{0,2},{1,3},{2,0},{3,1},{4,6},{5,7},{6,4},{7,5},{8,10},{9,11},{10,... | collective-permute-start | bytes 122888 | tf_op jit(solution)/shard_map/ppermute | solution.py:22
  35.6 4.4 %collective-permute-start.21 = (bf16[128,256]{1,0:T(8,128)(2,1)S(1)}, bf16[128,256]{1,0:T(8,128)(2,1)S(1)}, u32[]{:S(2)}, u32[]{:S(2)}) collective-permute-start(bf16[128,256]{1,0:T(8,128)(2,1)S(1)} %collective-permute-done.20.refs_4_), channel_id=1, source_target_pairs={{0,1},{1,0},{2,3},{3,2},{4,5},{5,4},{6,7},{7,6},{8,9},{9,8},{10,11... | collective-permute-start | bytes 196616 | tf_op jit(solution)/shard_map/ppermute | solution.py:22
  36.3 4.4 %collective-permute-start.19 = (bf16[128,256]{1,0:T(8,128)(2,1)S(1)}, bf16[128,256]{1,0:T(8,128)(2,1)S(1)}, u32[]{:S(2)}, u32[]{:S(2)}) collective-permute-start(bf16[128,256]{1,0:T(8,128)(2,1)S(1)} %collective-permute-done.18.refs_2_), channel_id=1, source_target_pairs={{0,1},{1,0},{2,3},{3,2},{4,5},{5,4},{6,7},{7,6},{8,9},{9,8},{10,11... | collective-permute-start | bytes 196616 | tf_op jit(solution)/shard_map/ppermute | solution.py:22
  37.7 4.3 %collective-permute-start.22 = (bf16[128,256]{1,0:T(8,128)(2,1)S(1)}, bf16[128,256]{1,0:T(8,128)(2,1)S(1)}, u32[]{:S(2)}, u32[]{:S(2)}) collective-permute-start(bf16[128,256]{1,0:T(8,128)(2,1)S(1)} %collective-permute-done.12.refs_2_.refs_6_), channel_id=1, source_target_pairs={{0,1},{1,0},{2,3},{3,2},{4,5},{5,4},{6,7},{7,6},{8,9},{9,8},{10,11... | collective-permute-start | bytes 196616 | tf_op jit(solution)/shard_map/ppermute | solution.py:22
  38.4 4.1 %collective-permute-start.17 = (bf16[80,256]{1,0:T(8,128)(2,1)S(1)}, bf16[80,256]{1,0:T(8,128)(2,1)S(1)}, u32[]{:S(2)}, u32[]{:S(2)}) collective-permute-start(bf16[80,256]{1,0:T(8,128)(2,1)S(1)} %sum_shares.3.left_ref), channel_id=1, source_target_pairs={{0,1},{1,0},{2,3},{3,2},{4,5},{5,4},{6,7},{7,6},{8,9},{9,8},{10,11... | collective-permute-start | bytes 122888 | tf_op jit(solution)/shard_map/ppermute | solution.py:22
  44.4 5.6 %collective-permute-start.24 = (bf16[256,256]{1,0:T(8,128)(2,1)S(1)}, bf16[256,256]{1,0:T(8,128)(2,1)S(1)}, u32[]{:S(2)}, u32[]{:S(2)}) collective-permute-start(bf16[256,256]{1,0:T(8,128)(2,1)S(1)} %get-tuple-element.40.sent_ref), channel_id=1, source_target_pairs={{0,16},{8,24},{16,0},{24,8},{1,17},{9,25},{17,1},{25,9},{2,18},{10... | collective-permute-start | bytes 393224 | tf_op jit(solution)/shard_map/ppermute | solution.py:22
  (5 other events, 58.3 us)
